TPU v7x, 256 devices: a whole 4x4x8 slice. The times are simulated.
256 devices in a mesh: visit: 32 (over y, z), tile: 8 (over x, core).
Axes of the slice: x: 4, y: 4, z: 8, core: 2. Of those that a mesh axis runs over, the one named last changes fastest.
Arguments:
- visit_image: bfloat16 [32, 2048, 2048], P('visit', 'tile'), may hold values from -6 to 6
- good_mask: int32 [32, 2048, 2048], P('visit', 'tile'), may hold values 0 or 1
- basis_rows: float32 [27, 21], replicated, may hold values from -1.25 to 1.25
- basis_cols: float32 [27, 21], replicated, may hold values from -1.25 to 1.25
- visit_coeff: float32 [32, 27], P('visit'), may hold values from -1.25 to 1.25
- visit_weight: float32 [32], P('visit'), may hold values from 0.25 to 4
- col_offset: int32 [32], P('visit'), may hold values from -64 to 64
- patch_of: int32 [32, 1], replicated, may hold values from 0 to 7
- new_image: bfloat16 [32, 2048, 2048], P('visit', 'tile'), may hold values from -6 to 6
- new_coeff: float32 [32, 27], P('visit'), may hold values from -1.25 to 1.25
- new_patch: int32 [32, 1], replicated, may hold values from 0 to 7
Outputs:
- coadd: bfloat16 [8, 8, 256, 2048], P(None, 'tile', 'visit')
- difference: float32 [32, 2048, 2048], P('visit', 'tile')
Inputs may be any that keep to these rules, and one draw needn't show every extreme that they name: `patch_of`: every one of the 8 patches is intersected by at least one visit. `new_patch`: every one of the 8 patches lies under at least one new visit.
All inputs are finite; a program needn't handle non-finite values. No bound on the sum of `good_mask` on one device may be relied on, other than what follows from the above.
Results may differ from a plain program's by a relative error of at most 0.007.
Values may be sent and summed in bfloat16 or wider, within the bound.
No kernel may reach another device: no remote copies, remote signals or barrier semaphores. Data moves between devices by JAX's collectives and lax.ppermute only.
A program may use at most 128 MiB of HBM per device.

v0:
```python
import jax
import jax.numpy as jnp
from jax import lax
from jax.sharding import PartitionSpec as P

KS = 21
PATCHES = 8
OFF = 64


def with_halo(block, sides, width):
    for axis, dim in sides:
        count = lax.axis_size(axis)
        forward = [(i, i + 1) for i in range(count - 1)]
        backward = [(target, source) for source, target in forward]
        low = lax.ppermute(
            lax.slice_in_dim(block, block.shape[dim] - width, None, axis=dim), axis, forward
        )
        high = lax.ppermute(lax.slice_in_dim(block, 0, width, axis=dim), axis, backward)
        block = jnp.concatenate([low, block, high], axis=dim)
    return block


def build_kernel(coefficients, basis_rows, basis_cols):
    summed = jnp.sum(
        coefficients[:, None, None] * basis_rows[:, :, None] * basis_cols[:, None, :], axis=0
    )
    return summed.astype(jnp.bfloat16)


def toeplitz(kernel, block_size):
    span = block_size + KS - 1
    spread = jnp.arange(span)[:, None] - jnp.arange(block_size)[None, :]
    onehot = (spread[None, :, :] == jnp.arange(KS)[:, None, None]).astype(jnp.bfloat16)
    product = jnp.dot(
        kernel, onehot.reshape(KS, span * block_size), preferred_element_type=jnp.float32
    )
    return product.reshape(KS, span, block_size).astype(jnp.bfloat16)


def convolve(extended, kernel):
    halfwidth = KS // 2
    height = extended.shape[0] - (KS - 1)
    columns = extended.shape[1]
    block_size = 128
    number = columns // block_size
    padded = jnp.pad(extended, ((0, 0), (halfwidth, block_size - halfwidth)))
    blocks = padded.reshape(extended.shape[0], number + 1, block_size)
    windows = jnp.concatenate([blocks[:, :-1], blocks[:, 1:, : KS - 1]], axis=2)
    table = toeplitz(kernel, block_size)
    running = jnp.zeros((height, number, block_size), jnp.float32)
    for shift_row in range(KS):
        running = running + jnp.einsum(
            "rgk,ko->rgo",
            windows[shift_row : shift_row + height],
            table[shift_row],
            preferred_element_type=jnp.float32,
        )
    return running.reshape(height, columns)


def per_device(
    visit_image,
    good_mask,
    basis_rows,
    basis_cols,
    visit_coeff,
    visit_weight,
    col_offset,
    patch_of,
    new_image,
    new_coeff,
    new_patch,
):
    halfwidth = KS // 2
    extended = with_halo(visit_image[0], (("tile", 0),), halfwidth)
    matched = convolve(extended, build_kernel(visit_coeff[0], basis_rows, basis_cols))
    height, columns = matched.shape
    first_col = OFF - col_offset[0]
    placed = lax.dynamic_slice_in_dim(jnp.pad(matched, ((0, 0), (OFF, OFF))), first_col, columns, 1)
    inside = lax.dynamic_slice_in_dim(
        jnp.pad(good_mask[0].astype(jnp.float32), ((0, 0), (OFF, OFF))), first_col, columns, 1
    )
    coverage = visit_weight[0] * inside
    weighted = (placed * coverage).astype(jnp.bfloat16)
    cover_rounded = coverage.astype(jnp.bfloat16)
    owners = lax.axis_size("visit")
    slice_rows = height // owners
    visit_onehot = (patch_of[:, 0][None, :] == jnp.arange(PATCHES)[:, None]).astype(jnp.bfloat16)
    outgoing = (
        weighted.reshape(owners, slice_rows, columns),
        cover_rounded.reshape(owners, slice_rows, columns),
    )
    weighted_rows = lax.all_to_all(outgoing[0], "visit", split_axis=0, concat_axis=0, tiled=True)
    cover_rows = lax.all_to_all(outgoing[1], "visit", split_axis=0, concat_axis=0, tiled=True)
    numerator = jnp.einsum(
        "pv,vsw->psw", visit_onehot, weighted_rows, preferred_element_type=jnp.float32
    )
    denominator = jnp.einsum(
        "pv,vsw->psw", visit_onehot, cover_rows, preferred_element_type=jnp.float32
    )
    coadd = (numerator / jnp.maximum(denominator, 1.0)).astype(jnp.bfloat16)
    gathered = lax.all_gather(coadd, "visit", axis=1, tiled=True)
    patch_index = lax.dynamic_index_in_dim(
        new_patch[:, 0], lax.axis_index("visit"), 0, keepdims=False
    )
    template = lax.dynamic_index_in_dim(gathered, patch_index, 0, keepdims=False)
    template_ext = with_halo(template, (("tile", 0),), halfwidth)
    difference = new_image[0].astype(jnp.float32) - convolve(
        template_ext, build_kernel(new_coeff[0], basis_rows, basis_cols)
    )
    return (coadd[:, None], difference[None])


def solution(mesh):
    return jax.shard_map(
        per_device,
        mesh=mesh,
        in_specs=(
            P("visit", "tile", None),
            P("visit", "tile", None),
            P(),
            P(),
            P("visit", None),
            P("visit"),
            P("visit"),
            P(),
            P("visit", "tile", None),
            P("visit", None),
            P(),
        ),
        out_specs=(P(None, "tile", "visit", None), P("visit", "tile", None)),
        check_vma=False,
    )
```

profile of v0, /device:TPU:1, one launch (start us, length us, event | category | flops | bytes accessed | tf_op | source)
XLA Modules:
  0.0 335.7 jit_solution(6419589440406265364)
XLA Ops:
  7.2 0.9 slice_bitcast_fusion.3
  8.1 4.5 %collective-permute-start = (bf16[10,2048]{1,0:T(8,128)(2,1)S(1)}, bf16[10,2048]{1,0:T(8,128)(2,1)S(1)}, u32[]{:S(2)}, u32[]{:S(2)}) collective-permute-start(bf16[10,2048]{1,0:T(8,128)(2,1)S(1)} %get-tuple-element.16), channel_id=1, source_target_pairs={{0,1},{1,2},{2,3},{3,4},{4,5},{5,6},{6,7},{8,9},{9,10},{10,11},{11... | collective-permute-start | bytes 122888 | tf_op jit(solution)/shard_map/ppermute | solution.py:16
  12.6 1.9 collective-permute-start.1
  15.3 0.9 multiply_reduce_fusion
  16.7 2.1 fusion.356
  18.8 1.6 convert_bitcast_fusion
  20.4 0.8 fusion.357
  22.7 1.4 copy.94
  24.8 0.8 fusion.101
  25.6 0.8 fusion.104
  27.3 2.1 fusion.110
  29.5 2.1 fusion.113
  31.6 2.1 fusion.116
  33.7 2.1 fusion.119
  35.8 2.1 fusion.122
  37.9 2.2 fusion.125
  40.0 2.0 fusion.80
  42.1 2.0 fusion.83
  44.1 2.1 fusion.86
  46.2 2.1 fusion.89
  48.3 2.1 fusion.92
  50.4 2.1 fusion.95
  52.6 2.1 fusion.98
  54.7 2.3 fusion.128
  57.0 2.1 fusion.71
  59.1 1.8 fusion.74
  60.8 2.1 fusion.77
  62.9 13.9 %add_add_fusion.1 = f32[256,16,128]{0,2,1:T(8,128)} fusion(f32[256,16,128]{0,2,1:T(8,128)} %fusion.71, f32[256,16,128]{0,2,1:T(8,128)} %fusion.128, f32[256,16,128]{0,2,1:T(8,128)} %fusion.125, f32[256,16,128]{0,2,1:T(8,128)} %fusion.122, f32[256,16,128]{0,2,1:T(8,128)} %fusion.119, f32[256,16,128]{0,2,1:T(8,128)} %fusion.116, ...), kind=kOutput, calls=%fused_computation.51 | convolution fusion | flops 168099840 | bytes 45385216 | tf_op jit(solution)/shard_map/rgk,ko->rgo/dot_general | solution.py:53
  76.9 3.1 copy.44
  79.9 4.3 %fusion.172 = (bf16[32,8,2048]{2,1,0:T(8,128)(2,1)}, bf16[32,8,2048]{2,1,0:T(8,128)(2,1)S(1)}) fusion(s32[]{:T(128)S(6)} %select_n.12, f32[256,2048]{1,0:T(8,128)S(1)} %copy-done.2, f32[]{:T(128)} %bitcast.166, f32[256,2048]{1,0:T(8,128)} %copy.44), kind=kLoop, calls=%fused_computation.184 | loop fusion | flops 2621440 | bytes 6291464 | tf_op jit(solution)/shard_map/reshape | solution.py:92
  84.2 38.8 %all_to_all.10 = bf16[32,8,2048]{2,1,0:T(8,128)(2,1)S(1)} all-to-all(bf16[32,8,2048]{2,1,0:T(8,128)(2,1)S(1)} %get-tuple-element.13), channel_id=1, replica_groups=mesh['visit'=32,'tile'=8] {'visit'}, dimensions={0} | all-to-all | bytes 2097152 | tf_op jit(solution)/shard_map/all_to_all | solution.py:94
  123.0 4.8 %all-to-all-start.1 = ((bf16[32,8,2048]{2,1,0:T(8,128)(2,1)}), bf16[32,8,2048]{2,1,0:T(8,128)(2,1)S(1)}, u32[]{:S(2)}, u32[]{:S(2)}) async-start(bf16[32,8,2048]{2,1,0:T(8,128)(2,1)} %get-tuple-element.12), calls=%async_computation.1 | async-start | bytes 2097152 | tf_op jit(solution)/shard_map/all_to_all | solution.py:95
  128.2 1.2 fusion.175
  129.4 24.5 %all-to-all-done.1 = bf16[32,8,2048]{2,1,0:T(8,128)(2,1)S(1)} async-done(((bf16[32,8,2048]{2,1,0:T(8,128)(2,1)}), bf16[32,8,2048]{2,1,0:T(8,128)(2,1)S(1)}, u32[]{:S(2)}, u32[]{:S(2)}) %all-to-all-start.1) | async-done | bytes 1048608 | tf_op jit(solution)/shard_map/all_to_all | solution.py:95
  153.8 1.9 fusion.1
  158.8 2.2 fusion.354
  161.0 93.0 %all-gather.2.cloned.1.call-done = bf16[8,256,2048]{2,0,1:T(8,128)(2,1)} async-done(((bf16[8,8,2048]{2,0,1:T(8,128)(2,1)}), bf16[8,256,2048]{2,0,1:T(8,128)(2,1)}) %all-gather.2.cloned.1.call-update) | async-done | bytes 8388624 | tf_op jit(solution)/shard_map/all_gather | solution.py:103
  253.9 5.7 %constant_dynamic-slice_fusion = bf16[1,256,2048]{2,0,1:T(2,128)(2,1)S(1)} fusion(bf16[8,256,2048]{2,0,1:T(8,128)(2,1)} %all-gather.2.cloned.1.call-done, s32[]{:T(128)S(6)} %select_n.14), kind=kLoop, calls=%fused_computation.332 | loop fusion | bytes 2097156 | tf_op jit(solution)/shard_map/jit(dynamic_index_in_dim)/dynamic_slice | solution.py:107
  260.3 4.1 %collective-permute-start.2 = (bf16[10,2048]{1,0:T(8,128)(2,1)S(1)}, bf16[10,2048]{1,0:T(8,128)(2,1)S(1)}, u32[]{:S(2)}, u32[]{:S(2)}) collective-permute-start(bf16[10,2048]{1,0:T(8,128)(2,1)S(1)} %get-tuple-element.14), channel_id=1, source_target_pairs={{0,1},{1,2},{2,3},{3,4},{4,5},{5,6},{6,7},{8,9},{9,10},{10,11},{11... | collective-permute-start | bytes 122888 | tf_op jit(solution)/shard_map/ppermute | solution.py:16
  264.3 1.9 collective-permute-start.3
  266.4 0.9 copy.50
  267.8 2.1 collective-permute-done.3
  270.2 1.1 copy.95
  272.0 0.8 fusion.17
  274.5 2.1 fusion.23
  276.6 2.1 fusion.26
  278.7 2.1 fusion.29
  280.8 2.1 fusion.32
  283.0 2.1 fusion.35
  285.1 2.2 fusion.38
  287.2 2.0 fusion.41
  289.3 2.0 fusion.44
  291.3 2.1 fusion.47
  293.4 2.1 fusion.50
  295.5 2.1 fusion.53
  297.6 2.1 fusion.56
  299.8 2.1 fusion.59
  301.8 2.2 fusion.62
  304.0 2.3 fusion.65
  306.3 2.1 fusion.68
  308.4 2.1 fusion.11
  310.5 14.4 %add_add_fusion = f32[256,16,128]{0,2,1:T(8,128)} fusion(f32[256,16,128]{0,2,1:T(8,128)} %fusion.11, f32[256,16,128]{0,2,1:T(8,128)} %fusion.68, f32[256,16,128]{0,2,1:T(8,128)} %fusion.65, f32[256,16,128]{0,2,1:T(8,128)} %fusion.62, f32[256,16,128]{0,2,1:T(8,128)} %fusion.59, f32[256,16,128]{0,2,1:T(8,128)} %fusion.56, f32[256,16,128]{0,2,1:T(8,128)} %fusion.53, ...), kind=kOutput, calls=%fused_computation.48 | convolution fusion | flops 168099840 | bytes 45385216 | tf_op jit(solution)/shard_map/rgk,ko->rgo/dot_general | solution.py:53
  324.9 2.0 copy.49
  326.9 1.6 convert_subtract_fusion
  (113 shorter events, 8.7 us)
Async XLA Ops:
  7.2 148.6 %copy-start = (s32[32,1]{0,1:T(1,128)S(1)}, s32[32,1]{0,1:T(1,128)}, u32[]{:S(2)}) copy-start(s32[32,1]{0,1:T(1,128)} %param.21) | copy-start | bytes 388
  8.1 14.4 %collective-permute-start = (bf16[10,2048]{1,0:T(8,128)(2,1)S(1)}, bf16[10,2048]{1,0:T(8,128)(2,1)S(1)}, u32[]{:S(2)}, u32[]{:S(2)}) collective-permute-start(bf16[10,2048]{1,0:T(8,128)(2,1)S(1)} %get-tuple-element.16), channel_id=1, source_target_pairs={{0,1},{1,2},{2,3},{3,4},{4,5},{5,6},{6,7},{8,9},{9,10},{10,11},{11... | collective-permute-start | bytes 122888 | tf_op jit(solution)/shard_map/ppermute | solution.py:16
  12.6 9.9 %collective-permute-start.1 = (bf16[10,2048]{1,0:T(8,128)(2,1)S(1)}, bf16[10,2048]{1,0:T(8,128)(2,1)S(1)}, u32[]{:S(2)}, u32[]{:S(2)}) collective-permute-start(bf16[10,2048]{1,0:T(8,128)(2,1)S(1)} %get-tuple-element.17), channel_id=1, source_target_pairs={{1,0},{2,1},{3,2},{4,3},{5,4},{6,5},{7,6},{9,8},{10,9},{11,10},{12... | collective-permute-start | bytes 122888 | tf_op jit(solution)/shard_map/ppermute | solution.py:19
  16.2 2.6 copy-start.3
  18.8 3.7 %copy-start.4 = (bf16[1,256,2048]{2,1,0:T(8,128)(2,1)S(1)}, bf16[1,256,2048]{2,1,0:T(8,128)(2,1)}, u32[]{:S(2)}) copy-start(bf16[1,256,2048]{2,1,0:T(8,128)(2,1)} %param.11) | copy-start | bytes 3145732
  25.6 0.9 copy-start.42
  26.5 0.9 copy-start.41
  27.3 2.1 copy-start.40
  29.5 2.1 copy-start.39
  31.6 2.1 copy-start.38
  33.7 2.1 copy-start.37
  35.8 2.1 copy-start.36
  37.9 2.2 copy-start.35
  40.0 2.0 copy-start.34
  42.1 2.1 copy-start.33
  44.1 2.1 copy-start.32
  46.2 2.1 copy-start.31
  48.3 2.1 copy-start.30
  50.4 2.1 copy-start.29
  52.6 2.1 copy-start.28
  54.7 2.3 copy-start.27
  57.0 2.1 copy-start.8
  59.1 1.8 copy-start.7
  76.8 3.1 copy-start.2
  84.2 43.9 %copy-start.43 = (s32[32,1]{0,1:T(1,128)S(1)}, s32[32,1]{0,1:T(1,128)}, u32[]{:S(2)}) copy-start(s32[32,1]{0,1:T(1,128)} %param.18) | copy-start | bytes 388
  123.0 30.8 %all-to-all-start.1 = ((bf16[32,8,2048]{2,1,0:T(8,128)(2,1)}), bf16[32,8,2048]{2,1,0:T(8,128)(2,1)S(1)}, u32[]{:S(2)}, u32[]{:S(2)}) async-start(bf16[32,8,2048]{2,1,0:T(8,128)(2,1)} %get-tuple-element.12), calls=%async_computation.1 | async-start | bytes 2097152 | tf_op jit(solution)/shard_map/all_to_all | solution.py:95
  127.9 126.0 %all-gather.2.cloned.1.call-start = ((), (), s32[]{:S(2)}) async-start(), calls=%async_computation.2 | async-start | bytes 8650752 | tf_op jit(solution)/shard_map/all_gather | solution.py:103
  259.6 6.8 %copy-start.6 = (bf16[8,8,2048]{2,0,1:T(8,128)(2,1)S(1)}, bf16[8,8,2048]{2,0,1:T(8,128)(2,1)}, u32[]{:S(2)}) copy-start(bf16[8,8,2048]{2,0,1:T(8,128)(2,1)} %fusion.1) | copy-start | bytes 786436
  260.3 7.6 %collective-permute-start.2 = (bf16[10,2048]{1,0:T(8,128)(2,1)S(1)}, bf16[10,2048]{1,0:T(8,128)(2,1)S(1)}, u32[]{:S(2)}, u32[]{:S(2)}) collective-permute-start(bf16[10,2048]{1,0:T(8,128)(2,1)S(1)} %get-tuple-element.14), channel_id=1, source_target_pairs={{0,1},{1,2},{2,3},{3,4},{4,5},{5,6},{6,7},{8,9},{9,10},{10,11},{11... | collective-permute-start | bytes 122888 | tf_op jit(solution)/shard_map/ppermute | solution.py:16
  264.3 5.6 %collective-permute-start.3 = (bf16[10,2048]{1,0:T(8,128)(2,1)S(1)}, bf16[10,2048]{1,0:T(8,128)(2,1)S(1)}, u32[]{:S(2)}, u32[]{:S(2)}) collective-permute-start(bf16[10,2048]{1,0:T(8,128)(2,1)S(1)} %get-tuple-element.15), channel_id=1, source_target_pairs={{1,0},{2,1},{3,2},{4,3},{5,4},{6,5},{7,6},{9,8},{10,9},{11,10},{12... | collective-permute-start | bytes 122888 | tf_op jit(solution)/shard_map/ppermute | solution.py:19
  272.8 0.9 copy-start.26
  273.6 0.9 copy-start.25
  274.5 2.1 copy-start.24
  276.6 2.1 copy-start.23
  278.7 2.1 copy-start.22
  280.8 2.1 copy-start.21
  283.0 2.1 copy-start.20
  285.0 2.2 copy-start.19
  287.2 2.0 copy-start.18
  289.3 2.1 copy-start.17
  291.3 2.1 copy-start.16
  293.4 2.1 copy-start.15
  295.5 2.1 copy-start.14
  297.6 2.1 copy-start.13
  299.8 2.1 copy-start.12
  301.8 2.2 copy-start.11
  304.0 2.3 copy-start.10
  306.3 2.1 copy-start.9
  324.9 2.0 copy-start.5
  324.9 3.6 %copy-start.1 = (s32[32,1]{0,1:T(1,128)S(1)}, s32[32,1]{0,1:T(1,128)}, u32[]{:S(2)}) copy-start(s32[32,1]{0,1:T(1,128)} %param.21) | copy-start | bytes 388
Sparse Core Ops, SparseCore 0:
  155.9 97.9 all-gather.1
where the time goes:
time: 339 us; the launch traced here: 336 us
  waiting for transfers between devices  120 us (35%)
  matrix products  108 us (32%)
  blocking collectives  38.8 us (11%)
  local copies, waits for them, and re-layouts  24.2 us (7%)
  between operations  18 us (5%)
  starting transfers between devices  17.5 us (5%)
  other arithmetic  9.66 us (3%)
    dot_general x42, matrix products, convolve(): jnp.einsum('rgk,ko->rgo', windows[shift_row:shift_row + height], table[sh...  104 us
    all_gather x1, waiting for transfers between devices, per_device(): gathered = lax.all_gather(coadd, 'visit', axis=1, tiled=True)  93 us
    all_to_all x1, blocking collectives, per_device(): lax.all_to_all(outgoing[0], 'visit', split_axis=0, concat_axis=0, tiled=T...  38.8 us
    all_to_all x1, waiting for transfers between devices, per_device(): lax.all_to_all(outgoing[1], 'visit', split_axis=0, concat_axis=0, tiled=T...  24.5 us
    ppermute x2, starting transfers between devices, with_halo(): lax.ppermute(lax.slice_in_dim(block, block.shape[dim] - width, None, axis...  8.58 us
  transfers between devices with their start and end apart: 6, of which 3 were waited for; matrix products, arithmetic and copies ran while one was open for 4% of the time, Pallas kernels for 0%

commit v1 on v0

v1 whole, which is shorter than its diff:
```python
import functools

import jax
import jax.numpy as jnp
from jax import lax
from jax.experimental import pallas as pl
from jax.experimental.pallas import tpu as pltpu
from jax.sharding import PartitionSpec as P

KS = 21
HALF = KS // 2
PATCHES = 8
LANES = 128
HALO = 16
QUAD = 4
SPLIT = LANES // 2
SHIFTS = QUAD + KS - 1
STRIDE = 16
PLANES = STRIDE - QUAD + SHIFTS
VMEM_LIMIT = 56 * 2**20


def neighbours(block, axis):
    count = lax.axis_size(axis)
    forward = [(i, i + 1) for i in range(count - 1)]
    backward = [(target, source) for source, target in forward]
    low = lax.ppermute(block[-HALO:], axis, forward)
    high = lax.ppermute(block[:HALO], axis, backward)
    return low, high


def table_kernel(rows_ref, cols_ref, first_ref, second_ref, *table_refs):
    tap = lax.broadcasted_iota(jnp.int32, (KS, QUAD * SPLIT), 0)
    place = lax.broadcasted_iota(jnp.int32, (KS, QUAD * SPLIT), 1)
    shift = lax.broadcasted_iota(jnp.int32, (SHIFTS, KS), 0)
    row_tap = lax.broadcasted_iota(jnp.int32, (SHIFTS, KS), 1)
    lane = lax.broadcasted_iota(jnp.int32, (LANES, QUAD * SPLIT), 0)
    column = lax.broadcasted_iota(jnp.int32, (LANES, QUAD * SPLIT), 1) % SPLIT
    inside = (lane >= column) & (lane - column < KS)
    for coeff_ref, table_ref in zip((first_ref, second_ref), table_refs):
        kernel = lax.dot_general(
            rows_ref[...] * coeff_ref[...],
            cols_ref[...],
            (((0,), (0,)), ((), ())),
            precision=lax.Precision.HIGHEST,
            preferred_element_type=jnp.float32,
        ).astype(jnp.bfloat16)
        profile = jnp.zeros((SHIFTS, QUAD * SPLIT), jnp.float32)
        for e in range(QUAD):
            at = (SPLIT * e - tap) % (QUAD * SPLIT)
            spread = jnp.dot(
                kernel, (place == at).astype(jnp.bfloat16), preferred_element_type=jnp.float32
            )
            lowered = (shift - e == row_tap).astype(jnp.bfloat16)
            profile = profile + jnp.dot(
                lowered, spread.astype(jnp.bfloat16), preferred_element_type=jnp.float32
            )
        for s in range(SHIFTS):
            wide = jnp.broadcast_to(profile[s : s + 1], (LANES, QUAD * SPLIT))
            rolled = pltpu.roll(wide, 0, 1, stride=1, stride_axis=0)
            table_ref[s * LANES : (s + 1) * LANES, :] = jnp.where(inside, rolled, 0.0).astype(
                jnp.bfloat16
            )


def build_tables(basis_rows, basis_cols, visit_coeff, new_coeff):
    table = jax.ShapeDtypeStruct((SHIFTS * LANES, QUAD * SPLIT), jnp.bfloat16)
    return pl.pallas_call(
        table_kernel,
        out_shape=(table, table),
        compiler_params=pltpu.CompilerParams(vmem_limit_bytes=VMEM_LIMIT),
        cost_estimate=pl.CostEstimate(flops=10**9, bytes_accessed=4 * 10**6, transcendentals=0),
        name="tables",
    )(basis_rows, basis_cols, visit_coeff.reshape(-1, 1), new_coeff.reshape(-1, 1))


def shifted_block(load, blocks, h, shift, lane):
    turn = lax.rem(shift + 2 * LANES, LANES)
    back = (turn - shift) // LANES

    def rolled(j):
        clamped = jnp.clip(j, 0, blocks - 1)
        block = pltpu.roll(load(clamped), turn, 1)
        return jnp.where(clamped == j, block, jnp.zeros_like(block))

    return jnp.where(lane >= turn, rolled(h + back), rolled(h + back - 1))


def convolve(low_ref, mid_ref, high_ref, table_ref, shift, moved_ref, planes_ref, matched_ref):
    height, columns = mid_ref.shape
    blocks = columns // LANES
    chunk = 64
    for align in range(2):
        for source, first, count in (
            (low_ref, 0, HALO),
            *((mid_ref.at[pl.ds(r, chunk)], HALO + r, chunk) for r in range(0, height, chunk)),
            (high_ref, HALO + height, HALO),
        ):
            lane = lax.broadcasted_iota(jnp.int32, (count, LANES), 1)

            def load(j, source=source):
                return source[:, pl.ds(pl.multiple_of(j * LANES, LANES), LANES)].astype(jnp.float32)

            for h in range(blocks):
                moved_ref[2 * h + align, first : first + count, :] = shifted_block(
                    load, blocks, h, shift + HALF - align * SPLIT, lane
                )
    per = height // STRIDE
    for g in range(2 * blocks):
        for s in range(PLANES):
            planes_ref[s, g * per : (g + 1) * per, :] = moved_ref[
                g, pl.ds(HALO - HALF + s, per, stride=STRIDE), :
            ].astype(jnp.bfloat16)
    lane = lax.broadcasted_iota(jnp.int32, (per, LANES), 1)
    for i in range(STRIDE // QUAD):
        left = jnp.concatenate([planes_ref[QUAD * i + s] for s in range(SHIFTS)], axis=1)
        product = jnp.dot(left, table_ref[...], preferred_element_type=jnp.float32)
        for h in range(blocks):
            for pair in range(QUAD // 2):
                lanes = slice(pair * LANES, (pair + 1) * LANES)
                a = product[2 * h * per : (2 * h + 1) * per, lanes]
                b = product[(2 * h + 1) * per : (2 * h + 2) * per, lanes]
                row = QUAD * i + 2 * pair
                matched_ref[h, pl.ds(row, per, stride=STRIDE), :] = jnp.where(
                    lane < SPLIT, a, pltpu.roll(b, SPLIT, 1)
                )
                matched_ref[h, pl.ds(row + 1, per, stride=STRIDE), :] = jnp.where(
                    lane < SPLIT, pltpu.roll(a, SPLIT, 1), b
                )


def visit_kernel(
    offset_ref, weight_ref, low_ref, mid_ref, high_ref, mask_ref, table_ref, out_ref, moved, planes, matched
):
    offset = offset_ref[0]
    weight = weight_ref[0]
    convolve(low_ref, mid_ref, high_ref, table_ref, offset, moved, planes, matched)
    height, columns = mid_ref.shape
    blocks = columns // LANES
    owners, double, _ = out_ref.shape
    rows = double // 2
    lane = lax.broadcasted_iota(jnp.int32, (rows, LANES), 1)
    for d in range(owners):

        def load(j, d=d):
            return mask_ref[
                d * rows : (d + 1) * rows, pl.ds(pl.multiple_of(j * LANES, LANES), LANES)
            ]

        for h in range(blocks):
            good = shifted_block(load, blocks, h, offset, lane)
            coverage = weight * good.astype(jnp.float32)
            weighted = coverage * matched[h, d * rows : (d + 1) * rows, :]
            out_ref[d, :, h * LANES : (h + 1) * LANES] = jnp.concatenate(
                [weighted, coverage], axis=0
            ).astype(jnp.bfloat16)


def new_kernel(low_ref, mid_ref, high_ref, new_ref, table_ref, out_ref, moved, planes, matched):
    convolve(low_ref, mid_ref, high_ref, table_ref, jnp.int32(0), moved, planes, matched)
    blocks = out_ref.shape[1] // LANES
    for h in range(blocks):
        lanes = slice(h * LANES, (h + 1) * LANES)
        out_ref[:, lanes] = new_ref[:, lanes].astype(jnp.float32) - matched[h]


def conv_scratch(height, columns):
    blocks = columns // LANES
    return [
        pltpu.VMEM((2 * blocks, height + 2 * HALO, LANES), jnp.float32),
        pltpu.VMEM((PLANES, 2 * blocks * (height // STRIDE), LANES), jnp.bfloat16),
        pltpu.VMEM((blocks, height, LANES), jnp.float32),
    ]


def conv_cost(height, columns):
    return pl.CostEstimate(
        flops=2 * height * columns * SHIFTS * LANES, bytes_accessed=8 * 10**6, transcendentals=0
    )


def match_visit(low, mid, high, mask, table, offset, weight, owners):
    height, columns = mid.shape
    smem = pl.BlockSpec(memory_space=pltpu.SMEM)
    vmem = pl.BlockSpec(memory_space=pltpu.VMEM)
    return pl.pallas_call(
        visit_kernel,
        out_shape=jax.ShapeDtypeStruct((owners, 2 * (height // owners), columns), jnp.bfloat16),
        in_specs=[smem, smem] + [vmem] * 5,
        out_specs=vmem,
        scratch_shapes=conv_scratch(height, columns),
        compiler_params=pltpu.CompilerParams(vmem_limit_bytes=VMEM_LIMIT),
        cost_estimate=conv_cost(height, columns),
        name="match_visit",
    )(offset, weight, low, mid, high, mask, table)


def subtract(low, mid, high, new, table):
    height, columns = mid.shape
    vmem = pl.BlockSpec(memory_space=pltpu.VMEM)
    return pl.pallas_call(
        new_kernel,
        out_shape=jax.ShapeDtypeStruct((height, columns), jnp.float32),
        in_specs=[vmem] * 5,
        out_specs=vmem,
        scratch_shapes=conv_scratch(height, columns),
        compiler_params=pltpu.CompilerParams(vmem_limit_bytes=VMEM_LIMIT),
        cost_estimate=conv_cost(height, columns),
        name="subtract",
    )(low, mid, high, new, table)


def coadd_kernel(patch_ref, wanted_ref, received_ref, coadd_ref, send_ref, sums):
    visits, double, columns = received_ref.shape
    rows = double // 2
    sums[...] = jnp.zeros_like(sums)

    def add(v, carry):
        p = patch_ref[v]
        sums[p] = sums[p] + received_ref[v].astype(jnp.float32)
        return carry

    lax.fori_loop(0, visits, add, 0)
    for p in range(PATCHES):
        coadd_ref[p] = (sums[p, :rows] / jnp.maximum(sums[p, rows:], 1.0)).astype(jnp.bfloat16)

    def place(n, carry):
        send_ref[n] = coadd_ref[wanted_ref[n]]
        return carry

    lax.fori_loop(0, send_ref.shape[0], place, 0)


def combine(received, patch_of, new_patch):
    visits, double, columns = received.shape
    rows = double // 2
    smem = pl.BlockSpec(memory_space=pltpu.SMEM)
    vmem = pl.BlockSpec(memory_space=pltpu.VMEM)
    return pl.pallas_call(
        coadd_kernel,
        out_shape=(
            jax.ShapeDtypeStruct((PATCHES, rows, columns), jnp.bfloat16),
            jax.ShapeDtypeStruct((new_patch.shape[0], rows, columns), jnp.bfloat16),
        ),
        in_specs=[smem, smem, vmem],
        out_specs=(vmem, vmem),
        scratch_shapes=[pltpu.VMEM((PATCHES, double, columns), jnp.float32)],
        compiler_params=pltpu.CompilerParams(vmem_limit_bytes=VMEM_LIMIT),
        name="combine",
    )(patch_of, new_patch, received)


def per_device(
    visit_image,
    good_mask,
    basis_rows,
    basis_cols,
    visit_coeff,
    visit_weight,
    col_offset,
    patch_of,
    new_image,
    new_coeff,
    new_patch,
):
    owners = lax.axis_size("visit")
    low, high = neighbours(visit_image[0], "tile")
    visit_table, new_table = build_tables(basis_rows, basis_cols, visit_coeff, new_coeff)
    outgoing = match_visit(
        low, visit_image[0], high, good_mask[0], visit_table, col_offset, visit_weight, owners
    )
    received = lax.all_to_all(outgoing, "visit", split_axis=0, concat_axis=0, tiled=True)
    coadd, wanted = combine(received, patch_of[:, 0], new_patch[:, 0])
    template = lax.all_to_all(wanted, "visit", split_axis=0, concat_axis=0, tiled=True)
    template = template.reshape(new_image.shape[1:])
    low, high = neighbours(template, "tile")
    difference = subtract(low, template, high, new_image[0], new_table)
    return (coadd[:, None], difference[None])


def solution(mesh):
    return jax.shard_map(
        per_device,
        mesh=mesh,
        in_specs=(
            P("visit", "tile", None),
            P("visit", "tile", None),
            P(),
            P(),
            P("visit", None),
            P("visit"),
            P("visit"),
            P(),
            P("visit", "tile", None),
            P("visit", None),
            P(),
        ),
        out_specs=(P(None, "tile", "visit", None), P("visit", "tile", None)),
        check_vma=False,
    )
```

time: 339 us -> 149 us (0.44)
  waiting for transfers between devices: 120 us -> 1.12 us
  matrix products: 108 us -> 0 us
  blocking collectives: 38.8 us -> 92.5 us
  Pallas kernels: 0 us -> 28.6 us
  local copies, waits for them, and re-layouts: 24.2 us -> 7.63 us
  between operations: 18 us -> 2 us
  other arithmetic: 9.66 us -> 0 us
    dot_general x46 -> x0, matrix products: 108 us -> none  [the longest x42 104 us: convolve(): jnp.einsum('rgk,ko->rgo', windows[shift_row:shift_row + height], table[sh...]
    all_gather x1 -> x0, waiting for transfers between devices: 93 us -> none  [per_device(): gathered = lax.all_gather(coadd, 'visit', axis=1, tiled=True)]
    all_to_all x1 -> x2, blocking collectives: 38.8 us -> 92.5 us  [the longest x1 60.9 us: per_device(): lax.all_to_all(outgoing, 'visit', split_axis=0, concat_axis=0, tiled=True)]
    pallas_call x0 -> x4, Pallas kernels: none -> 28.6 us  [the longest x1 10.9 us: match_visit(): pl.pallas_call(visit_kernel, out_shape=jax.ShapeDtypeStruct((owners, 2 *...]
    all_to_all x1 -> x0, waiting for transfers between devices: 24.5 us -> none  [per_device(): lax.all_to_all(outgoing[1], 'visit', split_axis=0, concat_axis=0, tiled=T...]
    dynamic_slice x2 -> x0, local copies, waits for them, and re-layouts: 6.25 us -> none  [the longest x1 5.66 us: per_device(): lax.dynamic_index_in_dim(gathered, patch_index, 0, keepdims=False)]
    slice x10 -> x2, local copies, waits for them, and re-layouts: 6.49 us -> 0.89 us  [neighbours(): high = lax.ppermute(block[:HALO], axis, backward)]
    all_to_all x1 -> x0, starting transfers between devices: 4.83 us -> none  [per_device(): lax.all_to_all(outgoing[1], 'visit', split_axis=0, concat_axis=0, tiled=T...]
  transfers between devices with their start and end apart: 6 -> 4, of which waited for: 3 -> 1; matrix products, arithmetic and copies ran while one was open for 4% -> 4% of each run, Pallas kernels for 0% -> 3%
where the time goes in v1:
time: 149 us; the launch traced here: 148 us
  blocking collectives  92.5 us (62%)
  Pallas kernels  28.6 us (19%)
  starting transfers between devices  16.5 us (11%)
  local copies, waits for them, and re-layouts  7.63 us (5%)
  between operations  2 us (1%)
    all_to_all x1, blocking collectives, per_device(): lax.all_to_all(outgoing, 'visit', split_axis=0, concat_axis=0, tiled=True)  60.9 us
    all_to_all x1, blocking collectives, per_device(): lax.all_to_all(wanted, 'visit', split_axis=0, concat_axis=0, tiled=True)  31.5 us
    ppermute x2, starting transfers between devices, neighbours(): high = lax.ppermute(block[:HALO], axis, backward)  11.4 us
    pallas_call x1, Pallas kernels, match_visit(): pl.pallas_call(visit_kernel, out_shape=jax.ShapeDtypeStruct((owners, 2 *...  10.9 us
    pallas_call x1, Pallas kernels, subtract(): pl.pallas_call(new_kernel, out_shape=jax.ShapeDtypeStruct((height, column...  10.5 us
    ppermute x2, starting transfers between devices, neighbours(): low = lax.ppermute(block[-HALO:], axis, forward)  5.11 us
    unnamed x12, local copies, waits for them, and re-layouts  4.06 us
    pallas_call x1, Pallas kernels, build_tables(): pl.pallas_call(table_kernel, out_shape=(table, table), compiler_params=pl...  3.77 us
  transfers between devices with their start and end apart: 4, of which 1 were waited for; matrix products, arithmetic and copies ran while one was open for 4% of the time, Pallas kernels for 3%

profile of v1, /device:TPU:1, one launch (start us, length us, event | category | flops | bytes accessed | tf_op | source)
XLA Modules:
  0.0 148.3 jit_solution(15816439951007185442)
XLA Ops:
  0.6 0.9 slice_bitcast_fusion.2
  1.5 5.1 %collective-permute-start.1 = (bf16[16,2048]{1,0:T(8,128)(2,1)S(1)}, bf16[16,2048]{1,0:T(8,128)(2,1)S(1)}, u32[]{:S(2)}, u32[]{:S(2)}) collective-permute-start(bf16[16,2048]{1,0:T(8,128)(2,1)S(1)} %get-tuple-element.14), channel_id=1, source_target_pairs={{1,0},{2,1},{3,2},{4,3},{5,4},{6,5},{7,6},{9,8},{10,9},{11,10},{12... | collective-permute-start | bytes 196616 | tf_op jit(solution)/shard_map/ppermute | solution.py:28
  6.7 1.9 %collective-permute-start = (bf16[16,2048]{1,0:T(8,128)(2,1)S(1)}, bf16[16,2048]{1,0:T(8,128)(2,1)S(1)}, u32[]{:S(2)}, u32[]{:S(2)}) collective-permute-start(bf16[16,2048]{1,0:T(8,128)(2,1)S(1)} %get-tuple-element.15), channel_id=1, source_target_pairs={{0,1},{1,2},{2,3},{3,4},{4,5},{5,6},{6,7},{8,9},{9,10},{10,11},{11... | collective-permute-start | bytes 196616 | tf_op jit(solution)/shard_map/ppermute | solution.py:27
  9.9 1.4 copy.13.rows_ref
  11.3 1.4 copy.14.cols_ref
  12.7 1.3 copy.15.first_ref
  14.0 1.3 copy.16.second_ref
  15.4 3.8 %tables.1 = (bf16[3072,256]{1,0:T(8,128)(2,1)}, bf16[3072,256]{1,0:T(8,128)(2,1)}) custom-call(f32[27,21]{1,0:T(8,128)} %copy.13.rows_ref, f32[27,21]{1,0:T(8,128)} %copy.14.cols_ref, f32[27,1]{1,0:T(8,128)} %copy.15.first_ref, f32[27,1]{1,0:T(8,128)} %copy.16.second_ref), custom_call_target="tpu_custom_call" | custom-call | flops 1000000000 | bytes 4000000 | tf_op jit(solution)/shard_map/tables/pallas_call | solution.py:68
  19.1 0.0 collective-permute-done.1.high_ref
  19.1 0.0 copy-start.1
  19.1 0.0 collective-permute-done.low_ref
  19.2 0.0 copy-start.2
  19.2 0.6 copy-done.1
  19.8 0.0 copy-done.2
  19.8 10.9 %match_visit.1 = bf16[32,16,2048]{2,1,0:T(8,128)(2,1)} custom-call(s32[1]{0:T(128)S(6)} %copy.19.offset_ref, f32[1]{0:T(128)S(6)} %copy.18.weight_ref, bf16[16,2048]{1,0:T(8,128)(2,1)} %copy-done.2, bf16[256,2048]{1,0:T(8,128)(2,1)} %bitcast.21, bf16[16,2048]{1,0:T(8,128)(2,1)} %copy-done.1, s32[256,2048]{1,0:T(8,128)} %bitcast.26, ...), custom_call_target="tpu_custom_call" | custom-call | flops 3221225472 | bytes 8000000 | tf_op jit(solution)/shard_map/match_visit/pallas_call | solution.py:186
  30.7 60.9 %all_to_all.10.received_ref = bf16[32,16,2048]{2,1,0:T(8,128)(2,1)} all-to-all(bf16[32,16,2048]{2,1,0:T(8,128)(2,1)} %match_visit.1), channel_id=1, replica_groups=mesh['visit'=32,'tile'=8] {'visit'}, dimensions={0} | all-to-all | bytes 4194304 | tf_op jit(solution)/shard_map/all_to_all | solution.py:272
  91.6 3.5 %combine.1 = (bf16[8,8,2048]{2,1,0:T(8,128)(2,1)}, bf16[32,8,2048]{2,1,0:T(8,128)(2,1)}) custom-call(s32[32]{0:T(128)} %bitcast.24, s32[32]{0:T(128)} %bitcast.25, bf16[32,16,2048]{2,1,0:T(8,128)(2,1)} %all_to_all.10.received_ref), custom_call_target="tpu_custom_call" | custom-call | tf_op jit(solution)/shard_map/combine/pallas_call | solution.py:239
  95.1 31.5 %all_to_all.11 = bf16[32,8,2048]{2,1,0:T(8,128)(2,1)S(1)} all-to-all(bf16[32,8,2048]{2,1,0:T(8,128)(2,1)} %get-tuple-element.8), channel_id=1, replica_groups=mesh['visit'=32,'tile'=8] {'visit'}, dimensions={0} | all-to-all | bytes 2097152 | tf_op jit(solution)/shard_map/all_to_all | solution.py:274
  126.6 0.0 copy-start
  126.6 6.2 %collective-permute-start.3 = (bf16[16,2048]{1,0:T(8,128)(2,1)S(1)}, bf16[16,2048]{1,0:T(8,128)(2,1)S(1)}, u32[]{:S(2)}, u32[]{:S(2)}) collective-permute-start(bf16[16,2048]{1,0:T(8,128)(2,1)S(1)} %get-tuple-element.12), channel_id=1, source_target_pairs={{1,0},{2,1},{3,2},{4,3},{5,4},{6,5},{7,6},{9,8},{10,9},{11,10},{12... | collective-permute-start | bytes 196616 | tf_op jit(solution)/shard_map/ppermute | solution.py:28
  132.9 3.2 %collective-permute-start.2 = (bf16[16,2048]{1,0:T(8,128)(2,1)S(1)}, bf16[16,2048]{1,0:T(8,128)(2,1)S(1)}, u32[]{:S(2)}, u32[]{:S(2)}) collective-permute-start(bf16[16,2048]{1,0:T(8,128)(2,1)S(1)} %get-tuple-element.13), channel_id=1, source_target_pairs={{0,1},{1,2},{2,3},{3,4},{4,5},{5,6},{6,7},{8,9},{9,10},{10,11},{11... | collective-permute-start | bytes 196616 | tf_op jit(solution)/shard_map/ppermute | solution.py:27
  136.1 0.0 collective-permute-done.3.high_ref
  136.1 0.0 copy-start.3
  136.1 1.1 collective-permute-done.2.low_ref
  137.2 0.0 copy-start.4
  137.2 0.0 copy-done
  137.2 0.0 copy-done.3
  137.2 0.6 copy-done.4
  137.8 10.5 %subtract.1 = f32[256,2048]{1,0:T(8,128)} custom-call(bf16[16,2048]{1,0:T(8,128)(2,1)} %copy-done.4, bf16[256,2048]{1,0:T(8,128)(2,1)} %bitcast.20, bf16[16,2048]{1,0:T(8,128)(2,1)} %copy-done.3, bf16[256,2048]{1,0:T(8,128)(2,1)} %bitcast.27, bf16[3072,256]{1,0:T(8,128)(2,1)} %get-tuple-element.9.table_ref), custom_call_target="tpu_custom_call" | custom-call | flops 3221225472 | bytes 8000000 | tf_op jit(solution)/shard_map/subtract/pallas_call | solution.py:201
  (1 shorter events, 0.0 us)
Async XLA Ops:
  1.5 17.6 %collective-permute-start.1 = (bf16[16,2048]{1,0:T(8,128)(2,1)S(1)}, bf16[16,2048]{1,0:T(8,128)(2,1)S(1)}, u32[]{:S(2)}, u32[]{:S(2)}) collective-permute-start(bf16[16,2048]{1,0:T(8,128)(2,1)S(1)} %get-tuple-element.14), channel_id=1, source_target_pairs={{1,0},{2,1},{3,2},{4,3},{5,4},{6,5},{7,6},{9,8},{10,9},{11,10},{12... | collective-permute-start | bytes 196616 | tf_op jit(solution)/shard_map/ppermute | solution.py:28
  6.7 12.5 %collective-permute-start = (bf16[16,2048]{1,0:T(8,128)(2,1)S(1)}, bf16[16,2048]{1,0:T(8,128)(2,1)S(1)}, u32[]{:S(2)}, u32[]{:S(2)}) collective-permute-start(bf16[16,2048]{1,0:T(8,128)(2,1)S(1)} %get-tuple-element.15), channel_id=1, source_target_pairs={{0,1},{1,2},{2,3},{3,4},{4,5},{5,6},{6,7},{8,9},{9,10},{10,11},{11... | collective-permute-start | bytes 196616 | tf_op jit(solution)/shard_map/ppermute | solution.py:27
  19.1 0.6 copy-start.1
  19.2 0.6 copy-start.2
  126.6 10.6 %copy-start = (bf16[32,8,2048]{2,1,0:T(8,128)(2,1)}, bf16[32,8,2048]{2,1,0:T(8,128)(2,1)S(1)}, u32[]{:S(2)}) copy-start(bf16[32,8,2048]{2,1,0:T(8,128)(2,1)S(1)} %all_to_all.11) | copy-start | bytes 3145732
  126.6 9.5 %collective-permute-start.3 = (bf16[16,2048]{1,0:T(8,128)(2,1)S(1)}, bf16[16,2048]{1,0:T(8,128)(2,1)S(1)}, u32[]{:S(2)}, u32[]{:S(2)}) collective-permute-start(bf16[16,2048]{1,0:T(8,128)(2,1)S(1)} %get-tuple-element.12), channel_id=1, source_target_pairs={{1,0},{2,1},{3,2},{4,3},{5,4},{6,5},{7,6},{9,8},{10,9},{11,10},{12... | collective-permute-start | bytes 196616 | tf_op jit(solution)/shard_map/ppermute | solution.py:28
  132.9 4.3 %collective-permute-start.2 = (bf16[16,2048]{1,0:T(8,128)(2,1)S(1)}, bf16[16,2048]{1,0:T(8,128)(2,1)S(1)}, u32[]{:S(2)}, u32[]{:S(2)}) collective-permute-start(bf16[16,2048]{1,0:T(8,128)(2,1)S(1)} %get-tuple-element.13), channel_id=1, source_target_pairs={{0,1},{1,2},{2,3},{3,4},{4,5},{5,6},{6,7},{8,9},{9,10},{10,11},{11... | collective-permute-start | bytes 196616 | tf_op jit(solution)/shard_map/ppermute | solution.py:27
  136.1 1.1 copy-start.3
  137.2 0.6 copy-start.4

commit v2 on v1

v2 whole, which is shorter than its diff:
```python
import jax
import jax.numpy as jnp
from jax import lax
from jax.experimental import pallas as pl
from jax.experimental.pallas import tpu as pltpu
from jax.sharding import PartitionSpec as P

KS = 21
HALF = KS // 2
PATCHES = 8
LANES = 128
HALO = 16
QUAD = 4
SPLIT = LANES // 2
SHIFTS = QUAD + KS - 1
CHUNK = 64
VMEM_LIMIT = 24 * 2**20


def params():
    return pltpu.CompilerParams(vmem_limit_bytes=VMEM_LIMIT)


def neighbours(block, axis):
    count = lax.axis_size(axis)
    forward = [(i, i + 1) for i in range(count - 1)]
    backward = [(target, source) for source, target in forward]
    low = lax.ppermute(block[-HALO:], axis, forward)
    high = lax.ppermute(block[:HALO], axis, backward)
    return low, high


def table_kernel(rows_ref, cols_ref, first_ref, second_ref, *table_refs):
    wide = QUAD * SPLIT
    tap = lax.broadcasted_iota(jnp.int32, (KS, wide), 0)
    place = lax.broadcasted_iota(jnp.int32, (KS, wide), 1)
    shift = lax.broadcasted_iota(jnp.int32, (SHIFTS, KS), 0)
    row_tap = lax.broadcasted_iota(jnp.int32, (SHIFTS, KS), 1)
    lane = lax.broadcasted_iota(jnp.int32, (LANES, wide), 0)
    column = lax.broadcasted_iota(jnp.int32, (LANES, wide), 1) % SPLIT
    inside = (lane >= column) & (lane - column < KS)
    for coeff_ref, table_ref in zip((first_ref, second_ref), table_refs):
        kernel = lax.dot_general(
            rows_ref[...] * coeff_ref[...],
            cols_ref[...],
            (((1,), (1,)), ((), ())),
            precision=lax.Precision.HIGHEST,
            preferred_element_type=jnp.float32,
        ).astype(jnp.bfloat16)
        profile = jnp.zeros((SHIFTS, wide), jnp.float32)
        for e in range(QUAD):
            at = (SPLIT * e - tap) % wide
            spread = jnp.dot(
                kernel, (place == at).astype(jnp.bfloat16), preferred_element_type=jnp.float32
            )
            lowered = (shift - e == row_tap).astype(jnp.bfloat16)
            profile = profile + jnp.dot(
                lowered, spread.astype(jnp.bfloat16), preferred_element_type=jnp.float32
            )
        for s in range(SHIFTS):
            line = jnp.broadcast_to(profile[s : s + 1], (LANES, wide))
            rolled = pltpu.roll(line, 0, 1, stride=1, stride_axis=0)
            table_ref[s * LANES : (s + 1) * LANES, :] = jnp.where(inside, rolled, 0.0).astype(
                jnp.bfloat16
            )


def build_tables(basis_rows, basis_cols, visit_coeff, new_coeff):
    table = jax.ShapeDtypeStruct((SHIFTS * LANES, QUAD * SPLIT), jnp.bfloat16)
    return pl.pallas_call(
        table_kernel,
        out_shape=(table, table),
        compiler_params=params(),
        cost_estimate=pl.CostEstimate(flops=10**9, bytes_accessed=4 * 10**6, transcendentals=0),
        name="tables",
    )(basis_rows.T, basis_cols.T, visit_coeff, new_coeff)


def split_shift(shift):
    turn = lax.rem(shift + 2 * LANES, LANES)
    return turn, (turn - shift) // LANES


def moved_block(load, blocks, h, shift, lane):
    turn, back = split_shift(shift)

    def block(j):
        clamped = jnp.clip(j, 0, blocks - 1)
        return jnp.where(clamped == j, load(clamped), 0)

    joined = jnp.where(lane < LANES - turn, block(h + back), block(h + back - 1))
    return pltpu.roll(joined, turn, 1)


def cover_kernel(offset_ref, weight_ref, mask_ref, out_ref, lines):
    height, columns = mask_ref.shape
    blocks = columns // LANES
    offset = offset_ref[0]
    weight = weight_ref[0]
    count = 32
    lane = lax.broadcasted_iota(jnp.int32, (count, LANES), 1)

    def body(c, carry):
        first = pl.multiple_of(c * count, count)

        def load(j):
            return mask_ref[pl.ds(first, count), pl.ds(pl.multiple_of(j * LANES, LANES), LANES)]

        for h in range(blocks):
            good = moved_block(load, blocks, h, offset, lane)
            lines[pl.ds(h, count, stride=blocks), :] = weight * good.astype(jnp.float32)
        out_ref[pl.ds(first, count)] = (
            lines[...].reshape(count, blocks, LANES).astype(jnp.bfloat16)
        )
        return carry

    lax.fori_loop(0, height // count, body, 0)


def cover_rows(offset, weight, mask):
    height, columns = mask.shape
    blocks = columns // LANES
    smem = pl.BlockSpec(memory_space=pltpu.SMEM)
    vmem = pl.BlockSpec(memory_space=pltpu.VMEM)
    return pl.pallas_call(
        cover_kernel,
        out_shape=jax.ShapeDtypeStruct((height, blocks, LANES), jnp.bfloat16),
        in_specs=[smem, smem, vmem],
        out_specs=vmem,
        scratch_shapes=[pltpu.VMEM((32 * blocks, LANES), jnp.float32)],
        compiler_params=params(),
        name="cover_rows",
    )(offset, weight, mask)


def multiply(windows, table_ref, first, write):
    quads = CHUNK // QUAD
    parts = []
    for s in range(SHIFTS):
        start = s + HALO - HALF
        part = windows[pl.ds(first // QUAD + start // QUAD, quads), start % QUAD]
        parts.append(part.reshape(-1, LANES))
    product = jnp.dot(
        jnp.concatenate(parts, axis=1), table_ref[...], preferred_element_type=jnp.float32
    )
    blocks = windows.shape[2] // 2
    lane = lax.broadcasted_iota(jnp.int32, (blocks, LANES), 1)
    for q in range(quads):
        for pair in range(QUAD // 2):
            lanes = slice(pair * LANES, (pair + 1) * LANES)
            a = product[(2 * q) * blocks : (2 * q + 1) * blocks, lanes]
            b = product[(2 * q + 1) * blocks : (2 * q + 2) * blocks, lanes]
            crossed = pltpu.roll(jnp.where(lane < SPLIT, b, a), SPLIT, 1)
            row = q * QUAD + 2 * pair
            write(row, jnp.where(lane < SPLIT, a, crossed))
            write(row + 1, jnp.where(lane < SPLIT, crossed, b))


def visit_kernel(
    offset_ref, weight_ref, low_ref, mid_ref, high_ref, cover_ref, table_ref, out_ref, lines, windows
):
    weight = weight_ref[0]
    height, columns = mid_ref.shape
    blocks = columns // LANES
    shift = offset_ref[0] + HALF
    lane = lax.broadcasted_iota(jnp.int32, (HALO, LANES), 1)

    def fill(source, first, row):
        def load(j):
            return source[
                pl.ds(first, HALO), pl.ds(pl.multiple_of(j * LANES, LANES), LANES)
            ].astype(jnp.float32)

        for align in range(2):
            for h in range(blocks):
                lines[pl.ds(align * blocks + h, HALO, stride=2 * blocks), :] = moved_block(
                    load, blocks, h, shift - align * SPLIT, lane
                )
        windows[pl.ds(row // QUAD, HALO // QUAD)] = (
            lines[...].reshape(HALO // QUAD, QUAD, 2 * blocks, LANES).astype(jnp.bfloat16)
        )

    fill(low_ref, 0, 0)

    def body(c, carry):
        first = pl.multiple_of(c * HALO, HALO)
        fill(mid_ref, first, first + HALO)
        return carry

    lax.fori_loop(0, height // HALO, body, 0)
    fill(high_ref, 0, HALO + height)

    def chunk(c, carry):
        first = pl.multiple_of(c * CHUNK, CHUNK)

        def write(row, line):
            good = cover_ref[first + row].astype(jnp.float32) > 0
            out_ref[first + row] = (line * jnp.where(good, weight, 0.0)).astype(jnp.bfloat16)

        multiply(windows, table_ref, first, write)
        return carry

    lax.fori_loop(0, height // CHUNK, chunk, 0)


def window_scratch(height, blocks):
    return pltpu.VMEM(((height + 2 * HALO) // QUAD, QUAD, 2 * blocks, LANES), jnp.bfloat16)


def conv_cost(height, columns):
    return pl.CostEstimate(
        flops=2 * height * columns * SHIFTS * LANES, bytes_accessed=8 * 10**6, transcendentals=0
    )


def match_visit(low, mid, high, cover, table, offset, weight):
    height, columns = mid.shape
    blocks = columns // LANES
    smem = pl.BlockSpec(memory_space=pltpu.SMEM)
    vmem = pl.BlockSpec(memory_space=pltpu.VMEM)
    return pl.pallas_call(
        visit_kernel,
        out_shape=jax.ShapeDtypeStruct(cover.shape, jnp.bfloat16),
        in_specs=[smem, smem] + [vmem] * 5,
        out_specs=vmem,
        scratch_shapes=[
            pltpu.VMEM((HALO * 2 * blocks, LANES), jnp.float32),
            window_scratch(height, blocks),
        ],
        compiler_params=params(),
        cost_estimate=conv_cost(height, columns),
        name="match_visit",
    )(offset, weight, low, mid, high, cover, table)


def new_kernel(low_ref, mid_ref, high_ref, new_ref, table_ref, out_ref, padded, windows, lines):
    height, blocks, _ = mid_ref.shape
    edge = jnp.zeros((HALO, 8, LANES), jnp.float32)
    padded[:, :8] = edge
    padded[:, 8 + blocks :] = edge
    lane = lax.broadcasted_iota(jnp.int32, (HALO, blocks, LANES), 2)
    turn = SPLIT + HALF

    def fill(source, first, row):
        here = source[pl.ds(first, HALO)].astype(jnp.float32)
        padded[:, 8 : 8 + blocks] = here
        before = padded[:, 7 : 7 + blocks]
        after = padded[:, 9 : 9 + blocks]
        left = pltpu.roll(jnp.where(lane < LANES - HALF, here, before), HALF, 2)
        right = pltpu.roll(jnp.where(lane < LANES - turn, after, here), turn, 2)
        both = jnp.concatenate([left, right], axis=1).astype(jnp.bfloat16)
        windows[pl.ds(row // QUAD, HALO // QUAD)] = both.reshape(
            HALO // QUAD, QUAD, 2 * blocks, LANES
        )

    fill(low_ref, 0, 0)

    def body(c, carry):
        first = pl.multiple_of(c * HALO, HALO)
        fill(mid_ref, first, first + HALO)
        return carry

    lax.fori_loop(0, height // HALO, body, 0)
    fill(high_ref, 0, HALO + height)

    def chunk(c, carry):
        first = pl.multiple_of(c * CHUNK, CHUNK)

        def write(row, line):
            lines[row * blocks : (row + 1) * blocks, :] = line

        multiply(windows, table_ref, first, write)
        for h in range(blocks):
            lanes = slice(h * LANES, (h + 1) * LANES)
            out_ref[pl.ds(first, CHUNK), lanes] = (
                new_ref[pl.ds(first, CHUNK), lanes].astype(jnp.float32)
                - lines[pl.ds(h, CHUNK, stride=blocks), :]
            )
        return carry

    lax.fori_loop(0, height // CHUNK, chunk, 0)


def subtract(low, mid, high, new, table):
    height, blocks, _ = mid.shape
    vmem = pl.BlockSpec(memory_space=pltpu.VMEM)
    return pl.pallas_call(
        new_kernel,
        out_shape=jax.ShapeDtypeStruct(new.shape, jnp.float32),
        in_specs=[vmem] * 5,
        out_specs=vmem,
        scratch_shapes=[
            pltpu.VMEM((HALO, blocks + 16, LANES), jnp.float32),
            window_scratch(height, blocks),
            pltpu.VMEM((CHUNK * blocks, LANES), jnp.float32),
        ],
        compiler_params=params(),
        cost_estimate=conv_cost(*new.shape),
        name="subtract",
    )(low, mid, high, new, table)


def sum_kernel(patch_ref, received_ref, sums):
    sums[...] = jnp.zeros_like(sums)

    def add(v, carry):
        p = patch_ref[v]
        sums[p] = sums[p] + received_ref[v].astype(jnp.float32)
        return carry

    lax.fori_loop(0, received_ref.shape[0], add, 0)


def sum_cover(received, patch_of):
    smem = pl.BlockSpec(memory_space=pltpu.SMEM)
    vmem = pl.BlockSpec(memory_space=pltpu.VMEM)
    return pl.pallas_call(
        sum_kernel,
        out_shape=jax.ShapeDtypeStruct((PATCHES,) + received.shape[1:], jnp.float32),
        in_specs=[smem, vmem],
        out_specs=vmem,
        compiler_params=params(),
        name="sum_cover",
    )(patch_of, received)


def combine_kernel(patch_ref, wanted_ref, received_ref, cover_ref, coadd_ref, send_ref, sums, packed, lines):
    sum_kernel(patch_ref, received_ref, sums)
    _, rows, blocks, _ = sums.shape
    for p in range(PATCHES):
        ratio = sums[p] / jnp.maximum(cover_ref[p], 1.0)
        packed[p] = ratio.astype(jnp.bfloat16)
        lines[...] = ratio.reshape(rows * blocks, LANES)
        for h in range(blocks):
            coadd_ref[p, :, h * LANES : (h + 1) * LANES] = lines[
                pl.ds(h, rows, stride=blocks), :
            ].astype(jnp.bfloat16)

    def place(n, carry):
        send_ref[n] = packed[wanted_ref[n]]
        return carry

    lax.fori_loop(0, send_ref.shape[0], place, 0)


def combine(received, cover, patch_of, new_patch):
    visits, rows, blocks, _ = received.shape
    smem = pl.BlockSpec(memory_space=pltpu.SMEM)
    vmem = pl.BlockSpec(memory_space=pltpu.VMEM)
    return pl.pallas_call(
        combine_kernel,
        out_shape=(
            jax.ShapeDtypeStruct((PATCHES, rows, blocks * LANES), jnp.bfloat16),
            jax.ShapeDtypeStruct((new_patch.shape[0],) + received.shape[1:], jnp.bfloat16),
        ),
        in_specs=[smem, smem, vmem, vmem],
        out_specs=(vmem, vmem),
        scratch_shapes=[
            pltpu.VMEM((PATCHES, rows, blocks, LANES), jnp.float32),
            pltpu.VMEM((PATCHES, rows, blocks, LANES), jnp.bfloat16),
            pltpu.VMEM((rows * blocks, LANES), jnp.float32),
        ],
        compiler_params=params(),
        name="combine",
    )(patch_of, new_patch, received, cover)


def to_owners(lines):
    height, blocks, _ = lines.shape
    owners = lax.axis_size("visit")
    return lax.all_to_all(
        lines.reshape(owners, height // owners, blocks, LANES),
        "visit",
        split_axis=0,
        concat_axis=0,
        tiled=True,
    )


def per_device(
    visit_image,
    good_mask,
    basis_rows,
    basis_cols,
    visit_coeff,
    visit_weight,
    col_offset,
    patch_of,
    new_image,
    new_coeff,
    new_patch,
):
    cover = cover_rows(col_offset, visit_weight, good_mask[0])
    received_cover = to_owners(cover)
    low, high = neighbours(visit_image[0], "tile")
    visit_table, new_table = build_tables(basis_rows, basis_cols, visit_coeff, new_coeff)
    weighted = match_visit(
        low, visit_image[0], high, cover, visit_table, col_offset, visit_weight
    )
    received = to_owners(weighted)
    cover_sums = sum_cover(received_cover, patch_of[:, 0])
    coadd, wanted = combine(received, cover_sums, patch_of[:, 0], new_patch[:, 0])
    template = lax.all_to_all(wanted, "visit", split_axis=0, concat_axis=0, tiled=True)
    template = template.reshape((-1,) + template.shape[2:])
    low, high = neighbours(template, "tile")
    difference = subtract(low, template, high, new_image[0], new_table)
    return (coadd[:, None], difference[None])


def solution(mesh):
    return jax.shard_map(
        per_device,
        mesh=mesh,
        in_specs=(
            P("visit", "tile", None),
            P("visit", "tile", None),
            P(),
            P(),
            P("visit", None),
            P("visit"),
            P("visit"),
            P(),
            P("visit", "tile", None),
            P("visit", None),
            P(),
        ),
        out_specs=(P(None, "tile", "visit", None), P("visit", "tile", None)),
        check_vma=False,
    )
```

time: 149 us -> 133 us (0.89)
  blocking collectives: 92.5 us -> 33 us
  waiting for transfers between devices: 1.12 us -> 31.8 us
  starting transfers between devices: 16.5 us -> 36.4 us
  local copies, waits for them, and re-layouts: 7.63 us -> 2.78 us
  Pallas kernels: 28.6 us -> 26.8 us
    all_to_all x1 -> x0, blocking collectives: 60.9 us -> none  [per_device(): lax.all_to_all(outgoing, 'visit', split_axis=0, concat_axis=0, tiled=True)]
    all_to_all x0 -> x2, waiting for transfers between devices: none -> 26.7 us  [to_owners(): lax.all_to_all(lines.reshape(owners, height // owners, blocks, LANES), 'v...]
    all_to_all x0 -> x2, starting transfers between devices: none -> 20.6 us  [to_owners(): lax.all_to_all(lines.reshape(owners, height // owners, blocks, LANES), 'v...]
    ppermute x2, starting transfers between devices: 11.4 us -> 3.84 us  [neighbours(): high = lax.ppermute(block[:HALO], axis, backward)]
    ppermute x2, starting transfers between devices: 5.11 us -> 12 us  [neighbours(): low = lax.ppermute(block[-HALO:], axis, forward)]
    ppermute x2, waiting for transfers between devices: 0.01 us -> 5.12 us  [neighbours(): high = lax.ppermute(block[:HALO], axis, backward)]
    reshape x2 -> x0, local copies, waits for them, and re-layouts: 2.68 us -> none  [the longest x1 1.34 us: build_tables(): new_coeff.reshape(-1, 1)]
    pallas_call x4 -> x6, Pallas kernels: 28.6 us -> 26.8 us  [the longest x1 11.9 us: match_visit(): pl.pallas_call(visit_kernel, out_shape=jax.ShapeDtypeStruct(cover.shape,...]
  transfers between devices with their start and end apart: 4 -> 6, of which waited for: 1 -> 4; matrix products, arithmetic and copies ran while one was open for 4% -> 0% of each run, Pallas kernels for 3% -> 11%
where the time goes in v2:
time: 133 us
  starting transfers between devices  36.4 us (27%)
  blocking collectives  33 us (25%)
  waiting for transfers between devices  31.8 us (24%)
  Pallas kernels  26.8 us (20%)
  local copies, waits for them, and re-layouts  2.78 us (2%)
  between operations  2.1 us (2%)
    all_to_all x1, blocking collectives, per_device(): lax.all_to_all(wanted, 'visit', split_axis=0, concat_axis=0, tiled=True)  33 us
    all_to_all x2, waiting for transfers between devices, to_owners(): lax.all_to_all(lines.reshape(owners, height // owners, blocks, LANES), 'v...  26.7 us
    all_to_all x2, starting transfers between devices, to_owners(): lax.all_to_all(lines.reshape(owners, height // owners, blocks, LANES), 'v...  20.6 us
    ppermute x2, starting transfers between devices, neighbours(): low = lax.ppermute(block[-HALO:], axis, forward)  12 us
    pallas_call x1, Pallas kernels, match_visit(): pl.pallas_call(visit_kernel, out_shape=jax.ShapeDtypeStruct(cover.shape,...  11.9 us
    pallas_call x1, Pallas kernels, subtract(): pl.pallas_call(new_kernel, out_shape=jax.ShapeDtypeStruct(new.shape, jnp....  7.89 us
    ppermute x2, waiting for transfers between devices, neighbours(): high = lax.ppermute(block[:HALO], axis, backward)  5.12 us
    ppermute x2, starting transfers between devices, neighbours(): high = lax.ppermute(block[:HALO], axis, backward)  3.84 us
  transfers between devices with their start and end apart: 6, of which 4 were waited for; matrix products, arithmetic and copies ran while one was open for 0% of the time, Pallas kernels for 11%

profile of v2, /device:TPU:1, one launch (start us, length us, event | category | flops | bytes accessed | tf_op | source)
XLA Modules:
  0.0 132.9 jit_solution(5566685690247839277)
XLA Ops:
  1.9 0.0 copy-start
  1.9 1.6 %copy-done = s32[1,256,2048]{2,1,0:T(8,128)S(1)} copy-done((s32[1,256,2048]{2,1,0:T(8,128)S(1)}, s32[1,256,2048]{2,1,0:T(8,128)}, u32[]{:S(2)}) %copy-start) | copy-done | bytes 2097176
  3.5 0.0 copy-start.1
  3.5 0.0 copy-start.5
  3.5 0.0 copy-start.6
  3.5 0.0 copy-start.7
  3.5 0.0 copy-start.8
  3.5 2.8 %cover_rows.1.cover_ref = bf16[256,16,128]{2,1,0:T(8,128)(2,1)} custom-call(s32[1]{0:T(128)S(6)} %copy.15.offset_ref, f32[1]{0:T(128)S(6)} %copy.14.weight_ref, s32[256,2048]{1,0:T(8,128)S(1)} %bitcast.20), custom_call_target="tpu_custom_call" | custom-call | tf_op jit(solution)/shard_map/cover_rows/pallas_call | solution.py:125
  6.3 12.0 %all-to-all-start.1 = ((bf16[32,8,16,128]{3,2,1,0:T(8,128)(2,1)}), bf16[32,8,16,128]{3,2,1,0:T(8,128)(2,1)S(1)}, u32[]{:S(2)}, u32[]{:S(2)}) async-start(bf16[32,8,16,128]{3,2,1,0:T(8,128)(2,1)} %bitcast.9), calls=%async_computation.1 | async-start | bytes 2097152 | tf_op jit(solution)/shard_map/all_to_all | solution.py:371
  18.4 0.0 copy-done.1
  18.4 4.0 %collective-permute-start = (bf16[16,2048]{1,0:T(8,128)(2,1)S(1)}, bf16[16,2048]{1,0:T(8,128)(2,1)S(1)}, u32[]{:S(2)}, u32[]{:S(2)}) collective-permute-start(bf16[16,2048]{1,0:T(8,128)(2,1)S(1)} %get-tuple-element.15), channel_id=1, source_target_pairs={{0,1},{1,2},{2,3},{3,4},{4,5},{5,6},{6,7},{8,9},{9,10},{10,11},{11... | collective-permute-start | bytes 196616 | tf_op jit(solution)/shard_map/ppermute | solution.py:28
  22.4 1.9 %collective-permute-start.1 = (bf16[16,2048]{1,0:T(8,128)(2,1)S(1)}, bf16[16,2048]{1,0:T(8,128)(2,1)S(1)}, u32[]{:S(2)}, u32[]{:S(2)}) collective-permute-start(bf16[16,2048]{1,0:T(8,128)(2,1)S(1)} %get-tuple-element.14), channel_id=1, source_target_pairs={{1,0},{2,1},{3,2},{4,3},{5,4},{6,5},{7,6},{9,8},{10,9},{11,10},{12... | collective-permute-start | bytes 196616 | tf_op jit(solution)/shard_map/ppermute | solution.py:29
  24.3 0.0 copy-done.5
  24.3 0.0 copy-done.6
  24.3 0.0 copy-done.7
  24.3 0.0 copy-done.8
  24.3 1.3 tables.1
  25.6 0.0 copy-start.9
  25.6 1.1 copy-done.9
  26.8 0.0 collective-permute-done.low_ref
  26.8 1.5 %collective-permute-done.1.high_ref = bf16[16,2048]{1,0:T(8,128)(2,1)S(1)} collective-permute-done((bf16[16,2048]{1,0:T(8,128)(2,1)S(1)}, bf16[16,2048]{1,0:T(8,128)(2,1)S(1)}, u32[]{:S(2)}, u32[]{:S(2)}) %collective-permute-start.1) | collective-permute-done | bytes 65568 | tf_op jit(solution)/shard_map/ppermute | solution.py:29
  28.2 11.9 %match_visit.1 = bf16[256,16,128]{2,1,0:T(8,128)(2,1)} custom-call(s32[1]{0:T(128)S(6)} %copy.15.offset_ref, f32[1]{0:T(128)S(6)} %copy.14.weight_ref, bf16[16,2048]{1,0:T(8,128)(2,1)S(1)} %collective-permute-done.low_ref, bf16[256,2048]{1,0:T(8,128)(2,1)S(1)} %bitcast.22, bf16[16,2048]{1,0:T(8,128)(2,1)S(1)} %collective-permute-done.1.high_ref, ...), custom_call_target="tpu_custom_call" | custom-call | flops 3221225472 | bytes 8000000 | tf_op jit(solution)/shard_map/match_visit/pallas_call | solution.py:221
  40.1 0.0 copy-start.2
  40.1 0.0 copy-start.3
  40.1 2.9 %all-to-all-done.1.received_ref = bf16[32,8,16,128]{3,2,1,0:T(8,128)(2,1)S(1)} async-done(((bf16[32,8,16,128]{3,2,1,0:T(8,128)(2,1)}), bf16[32,8,16,128]{3,2,1,0:T(8,128)(2,1)S(1)}, u32[]{:S(2)}, u32[]{:S(2)}) %all-to-all-start.1) | async-done | bytes 1048608 | tf_op jit(solution)/shard_map/all_to_all | solution.py:371
  43.0 8.6 %all-to-all-start = ((bf16[32,8,16,128]{3,2,1,0:T(8,128)(2,1)}), bf16[32,8,16,128]{3,2,1,0:T(8,128)(2,1)S(1)}, u32[]{:S(2)}, u32[]{:S(2)}) async-start(bf16[32,8,16,128]{3,2,1,0:T(8,128)(2,1)} %bitcast.8), calls=%async_computation | async-start | bytes 2097152 | tf_op jit(solution)/shard_map/all_to_all | solution.py:371
  51.6 0.0 copy-done.2
  51.6 0.9 sum_cover.1.cover_ref
  52.5 0.0 copy-start.4
  52.5 23.8 %all-to-all-done.received_ref = bf16[32,8,16,128]{3,2,1,0:T(8,128)(2,1)S(1)} async-done(((bf16[32,8,16,128]{3,2,1,0:T(8,128)(2,1)}), bf16[32,8,16,128]{3,2,1,0:T(8,128)(2,1)S(1)}, u32[]{:S(2)}, u32[]{:S(2)}) %all-to-all-start) | async-done | bytes 1048608 | tf_op jit(solution)/shard_map/all_to_all | solution.py:371
  76.3 0.0 copy-start.10
  76.3 0.0 copy-done.3
  76.4 2.1 %combine.1 = (bf16[8,8,2048]{2,1,0:T(8,128)(2,1)}, bf16[32,8,16,128]{3,2,1,0:T(8,128)(2,1)S(1)}) custom-call(s32[32]{0:T(128)S(1)} %bitcast.24, s32[32]{0:T(128)S(1)} %bitcast.25, bf16[32,8,16,128]{3,2,1,0:T(8,128)(2,1)S(1)} %all-to-all-done.received_ref, f32[8,8,16,128]{3,2,1,0:T(8,128)S(1)} %sum_cover.1.cover_ref), custom_call_target="tpu_custom_call" | custom-call | tf_op jit(solution)/shard_map/combine/pallas_call | solution.py:350
  78.4 33.0 %all_to_all.15 = bf16[32,8,16,128]{3,2,1,0:T(8,128)(2,1)S(1)} all-to-all(bf16[32,8,16,128]{3,2,1,0:T(8,128)(2,1)S(1)} %get-tuple-element.8), channel_id=1, replica_groups=mesh['visit'=32,'tile'=8] {'visit'}, dimensions={0} | all-to-all | bytes 2097152 | tf_op jit(solution)/shard_map/all_to_all | solution.py:403
  111.4 8.0 %collective-permute-start.2 = (bf16[16,16,128]{2,1,0:T(8,128)(2,1)S(1)}, bf16[16,16,128]{2,1,0:T(8,128)(2,1)S(1)}, u32[]{:S(2)}, u32[]{:S(2)}) collective-permute-start(bf16[16,16,128]{2,1,0:T(8,128)(2,1)S(1)} %bitcast.30), channel_id=1, source_target_pairs={{0,1},{1,2},{2,3},{3,4},{4,5},{5,6},{6,7},{8,9},{9,10},{10,11},{11... | collective-permute-start | bytes 196616 | tf_op jit(solution)/shard_map/ppermute | solution.py:28
  119.4 1.9 %collective-permute-start.3 = (bf16[16,16,128]{2,1,0:T(8,128)(2,1)S(1)}, bf16[16,16,128]{2,1,0:T(8,128)(2,1)S(1)}, u32[]{:S(2)}, u32[]{:S(2)}) collective-permute-start(bf16[16,16,128]{2,1,0:T(8,128)(2,1)S(1)} %bitcast.29), channel_id=1, source_target_pairs={{1,0},{2,1},{3,2},{4,3},{5,4},{6,5},{7,6},{9,8},{10,9},{11,10},{12... | collective-permute-start | bytes 196616 | tf_op jit(solution)/shard_map/ppermute | solution.py:29
  121.4 0.0 collective-permute-done.2.low_ref
  121.4 3.6 %collective-permute-done.3.high_ref = bf16[16,16,128]{2,1,0:T(8,128)(2,1)S(1)} collective-permute-done((bf16[16,16,128]{2,1,0:T(8,128)(2,1)S(1)}, bf16[16,16,128]{2,1,0:T(8,128)(2,1)S(1)}, u32[]{:S(2)}, u32[]{:S(2)}) %collective-permute-start.3) | collective-permute-done | bytes 65568 | tf_op jit(solution)/shard_map/ppermute | solution.py:29
  125.0 0.0 copy-done.4
  125.0 0.0 copy-done.10
  125.0 7.9 %subtract.1 = f32[256,2048]{1,0:T(8,128)} custom-call(bf16[16,16,128]{2,1,0:T(8,128)(2,1)S(1)} %collective-permute-done.2.low_ref, bf16[256,16,128]{2,1,0:T(8,128)(2,1)S(1)} %bitcast.21, bf16[16,16,128]{2,1,0:T(8,128)(2,1)S(1)} %collective-permute-done.3.high_ref, bf16[256,2048]{1,0:T(8,128)(2,1)S(1)} %bitcast.26, bf16[3072,256]{1,0:T(8,128)(2,1)S(1)} %copy-done.10), custom_call_target="tpu_custom_call" | custom-call | flops 3221225472 | bytes 8000000 | tf_op jit(solution)/shard_map/subtract/pallas_call | solution.py:287
  (2 shorter events, 0.0 us)
Async XLA Ops:
  1.9 1.6 %copy-start = (s32[1,256,2048]{2,1,0:T(8,128)S(1)}, s32[1,256,2048]{2,1,0:T(8,128)}, u32[]{:S(2)}) copy-start(s32[1,256,2048]{2,1,0:T(8,128)} %param.12) | copy-start | bytes 6291460
  3.5 14.8 %copy-start.1 = (bf16[1,256,2048]{2,1,0:T(8,128)(2,1)S(1)}, bf16[1,256,2048]{2,1,0:T(8,128)(2,1)}, u32[]{:S(2)}) copy-start(bf16[1,256,2048]{2,1,0:T(8,128)(2,1)} %param.11) | copy-start | bytes 3145732
  3.5 20.8 %copy-start.5 = (f32[27,21]{0,1:T(8,128)S(1)}, f32[27,21]{0,1:T(8,128)}, u32[]{:S(2)}) copy-start(f32[27,21]{0,1:T(8,128)} %param.13) | copy-start | bytes 6808
  3.5 20.8 %copy-start.6 = (f32[27,21]{0,1:T(8,128)S(1)}, f32[27,21]{0,1:T(8,128)}, u32[]{:S(2)}) copy-start(f32[27,21]{0,1:T(8,128)} %param.14) | copy-start | bytes 6808
  3.5 20.8 %copy-start.7 = (f32[1,27]{1,0:T(1,128)S(1)}, f32[1,27]{1,0:T(1,128)}, u32[]{:S(2)}) copy-start(f32[1,27]{1,0:T(1,128)} %first_ref.1) | copy-start | bytes 328
  3.5 20.8 %copy-start.8 = (f32[1,27]{1,0:T(1,128)S(1)}, f32[1,27]{1,0:T(1,128)}, u32[]{:S(2)}) copy-start(f32[1,27]{1,0:T(1,128)} %second_ref.1) | copy-start | bytes 328
  6.3 36.7 %all-to-all-start.1 = ((bf16[32,8,16,128]{3,2,1,0:T(8,128)(2,1)}), bf16[32,8,16,128]{3,2,1,0:T(8,128)(2,1)S(1)}, u32[]{:S(2)}, u32[]{:S(2)}) async-start(bf16[32,8,16,128]{3,2,1,0:T(8,128)(2,1)} %bitcast.9), calls=%async_computation.1 | async-start | bytes 2097152 | tf_op jit(solution)/shard_map/all_to_all | solution.py:371
  18.4 8.4 %collective-permute-start = (bf16[16,2048]{1,0:T(8,128)(2,1)S(1)}, bf16[16,2048]{1,0:T(8,128)(2,1)S(1)}, u32[]{:S(2)}, u32[]{:S(2)}) collective-permute-start(bf16[16,2048]{1,0:T(8,128)(2,1)S(1)} %get-tuple-element.15), channel_id=1, source_target_pairs={{0,1},{1,2},{2,3},{3,4},{4,5},{5,6},{6,7},{8,9},{9,10},{10,11},{11... | collective-permute-start | bytes 196616 | tf_op jit(solution)/shard_map/ppermute | solution.py:28
  22.4 5.9 %collective-permute-start.1 = (bf16[16,2048]{1,0:T(8,128)(2,1)S(1)}, bf16[16,2048]{1,0:T(8,128)(2,1)S(1)}, u32[]{:S(2)}, u32[]{:S(2)}) collective-permute-start(bf16[16,2048]{1,0:T(8,128)(2,1)S(1)} %get-tuple-element.14), channel_id=1, source_target_pairs={{1,0},{2,1},{3,2},{4,3},{5,4},{6,5},{7,6},{9,8},{10,9},{11,10},{12... | collective-permute-start | bytes 196616 | tf_op jit(solution)/shard_map/ppermute | solution.py:29
  25.6 1.1 copy-start.9
  40.1 11.5 %copy-start.2 = (s32[32,1]{0,1:T(1,128)S(1)}, s32[32,1]{0,1:T(1,128)}, u32[]{:S(2)}) copy-start(s32[32,1]{0,1:T(1,128)} %param.18) | copy-start | bytes 388
  40.1 36.2 %copy-start.3 = (s32[32,1]{0,1:T(1,128)S(1)}, s32[32,1]{0,1:T(1,128)}, u32[]{:S(2)}) copy-start(s32[32,1]{0,1:T(1,128)} %param.21) | copy-start | bytes 388
  43.0 33.4 %all-to-all-start = ((bf16[32,8,16,128]{3,2,1,0:T(8,128)(2,1)}), bf16[32,8,16,128]{3,2,1,0:T(8,128)(2,1)S(1)}, u32[]{:S(2)}, u32[]{:S(2)}) async-start(bf16[32,8,16,128]{3,2,1,0:T(8,128)(2,1)} %bitcast.8), calls=%async_computation | async-start | bytes 2097152 | tf_op jit(solution)/shard_map/all_to_all | solution.py:371
  52.5 72.5 %copy-start.4 = (bf16[1,256,2048]{2,1,0:T(8,128)(2,1)S(1)}, bf16[1,256,2048]{2,1,0:T(8,128)(2,1)}, u32[]{:S(2)}) copy-start(bf16[1,256,2048]{2,1,0:T(8,128)(2,1)} %param.19) | copy-start | bytes 3145732
  76.3 48.7 %copy-start.10 = (bf16[3072,256]{1,0:T(8,128)(2,1)S(1)}, bf16[3072,256]{1,0:T(8,128)(2,1)}, u32[]{:S(2)}) copy-start(bf16[3072,256]{1,0:T(8,128)(2,1)} %copy-done.9) | copy-start | bytes 4718596
  111.4 9.9 %collective-permute-start.2 = (bf16[16,16,128]{2,1,0:T(8,128)(2,1)S(1)}, bf16[16,16,128]{2,1,0:T(8,128)(2,1)S(1)}, u32[]{:S(2)}, u32[]{:S(2)}) collective-permute-start(bf16[16,16,128]{2,1,0:T(8,128)(2,1)S(1)} %bitcast.30), channel_id=1, source_target_pairs={{0,1},{1,2},{2,3},{3,4},{4,5},{5,6},{6,7},{8,9},{9,10},{10,11},{11... | collective-permute-start | bytes 196616 | tf_op jit(solution)/shard_map/ppermute | solution.py:28
  119.4 5.6 %collective-permute-start.3 = (bf16[16,16,128]{2,1,0:T(8,128)(2,1)S(1)}, bf16[16,16,128]{2,1,0:T(8,128)(2,1)S(1)}, u32[]{:S(2)}, u32[]{:S(2)}) collective-permute-start(bf16[16,16,128]{2,1,0:T(8,128)(2,1)S(1)} %bitcast.29), channel_id=1, source_target_pairs={{1,0},{2,1},{3,2},{4,3},{5,4},{6,5},{7,6},{9,8},{10,9},{11,10},{12... | collective-permute-start | bytes 196616 | tf_op jit(solution)/shard_map/ppermute | solution.py:29

commit v3 on v2

v3 whole, which is shorter than its diff:
```python
import jax
import jax.numpy as jnp
from jax import lax
from jax.experimental import pallas as pl
from jax.experimental.pallas import tpu as pltpu
from jax.sharding import PartitionSpec as P

KS = 21
HALF = KS // 2
PATCHES = 8
LANES = 128
HALO = 16
QUAD = 4
SPLIT = LANES // 2
SHIFTS = QUAD + KS - 1
CHUNK = 64
PARTS = 4
UNIT = 16
PAD = 8
VMEM_LIMIT = 24 * 2**20


def params():
    return pltpu.CompilerParams(vmem_limit_bytes=VMEM_LIMIT)


def neighbours(block, axis):
    count = lax.axis_size(axis)
    forward = [(i, i + 1) for i in range(count - 1)]
    backward = [(target, source) for source, target in forward]
    low = lax.ppermute(block[-HALO:], axis, forward)
    high = lax.ppermute(block[:HALO], axis, backward)
    return low, high


def table_kernel(rows_ref, cols_ref, first_ref, second_ref, *table_refs):
    wide = QUAD * SPLIT
    tap = lax.broadcasted_iota(jnp.int32, (KS, wide), 0)
    place = lax.broadcasted_iota(jnp.int32, (KS, wide), 1)
    shift = lax.broadcasted_iota(jnp.int32, (SHIFTS, KS), 0)
    row_tap = lax.broadcasted_iota(jnp.int32, (SHIFTS, KS), 1)
    lane = lax.broadcasted_iota(jnp.int32, (LANES, wide), 0)
    column = lax.broadcasted_iota(jnp.int32, (LANES, wide), 1) % SPLIT
    inside = (lane >= column) & (lane - column < KS)
    for coeff_ref, table_ref in zip((first_ref, second_ref), table_refs):
        kernel = lax.dot_general(
            rows_ref[...] * coeff_ref[...],
            cols_ref[...],
            (((1,), (1,)), ((), ())),
            precision=lax.Precision.HIGHEST,
            preferred_element_type=jnp.float32,
        ).astype(jnp.bfloat16)
        profile = jnp.zeros((SHIFTS, wide), jnp.float32)
        for e in range(QUAD):
            at = (SPLIT * e - tap) % wide
            spread = jnp.dot(
                kernel, (place == at).astype(jnp.bfloat16), preferred_element_type=jnp.float32
            )
            lowered = (shift - e == row_tap).astype(jnp.bfloat16)
            profile = profile + jnp.dot(
                lowered, spread.astype(jnp.bfloat16), preferred_element_type=jnp.float32
            )
        for s in range(SHIFTS):
            line = jnp.broadcast_to(profile[s : s + 1], (LANES, wide))
            rolled = pltpu.roll(line, 0, 1, stride=1, stride_axis=0)
            table_ref[s * LANES : (s + 1) * LANES, :] = jnp.where(inside, rolled, 0.0).astype(
                jnp.bfloat16
            )


def build_tables(basis_rows, basis_cols, visit_coeff, new_coeff):
    table = jax.ShapeDtypeStruct((SHIFTS * LANES, QUAD * SPLIT), jnp.bfloat16)
    return pl.pallas_call(
        table_kernel,
        out_shape=(table, table),
        compiler_params=params(),
        cost_estimate=pl.CostEstimate(flops=10**9, bytes_accessed=4 * 10**6, transcendentals=0),
        name="tables",
    )(basis_rows.T, basis_cols.T, visit_coeff, new_coeff)


def split_shift(shift):
    turn = lax.rem(shift + 2 * LANES, LANES)
    return turn, (turn - shift) // LANES


def lay_out(blocks_of, shift, lines, base, pitch):
    turn, back = split_shift(shift)
    count = blocks_of[0].shape[0]
    lane = lax.broadcasted_iota(jnp.int32, (count, LANES), 1)
    before = jnp.zeros((count, LANES), blocks_of[0].dtype)
    for k in range(len(blocks_of) + 1):
        here = pltpu.roll(blocks_of[k], turn, 1) if k < len(blocks_of) else jnp.zeros_like(before)
        lines[pl.ds(base + k - back, count, stride=pitch), :] = jnp.where(
            lane >= turn, here, before
        )
        before = here


def lanes_of(h):
    return slice(h * LANES, (h + 1) * LANES)


def cover_kernel(offset_ref, weight_ref, mask_ref, out_ref, *lines):
    height, columns = mask_ref.shape
    blocks = columns // LANES
    weight = weight_ref[0]
    for u in range(height // UNIT):
        spot = lines[u % len(lines)]
        rows = slice(u * UNIT, (u + 1) * UNIT)
        good = [mask_ref[rows, lanes_of(h)].astype(jnp.float32) * weight for h in range(blocks)]
        lay_out(good, offset_ref[0], spot, PAD, 2 * blocks)
        tiles = spot[...].reshape(UNIT, 2 * blocks, LANES)
        out_ref[rows] = tiles[:, PAD : PAD + blocks].astype(jnp.bfloat16)


def cover_rows(offset, weight, mask):
    height, columns = mask.shape
    blocks = columns // LANES
    smem = pl.BlockSpec(memory_space=pltpu.SMEM)
    vmem = pl.BlockSpec(memory_space=pltpu.VMEM)
    return pl.pallas_call(
        cover_kernel,
        out_shape=jax.ShapeDtypeStruct((height, blocks, LANES), jnp.bfloat16),
        in_specs=[smem, smem, vmem],
        out_specs=vmem,
        scratch_shapes=[pltpu.VMEM((UNIT * 2 * blocks, LANES), jnp.float32)] * 4,
        compiler_params=params(),
        cost_estimate=pl.CostEstimate(flops=10**6, bytes_accessed=6 * 10**6, transcendentals=0),
        name="cover_rows",
    )(offset, weight, mask)


def multiply(windows, starts, table_ref, write):
    parts = []
    for s in range(SHIFTS):
        at = s + HALO - HALF
        pieces = [
            windows[first + at // QUAD : first + at // QUAD + count, at % QUAD]
            for first, count in starts
        ]
        part = pieces[0] if len(pieces) == 1 else jnp.concatenate(pieces, axis=0)
        parts.append(part.reshape(-1, LANES))
    product = jnp.dot(
        jnp.concatenate(parts, axis=1), table_ref[...], preferred_element_type=jnp.float32
    )
    blocks = windows.shape[2] // 2
    lane = lax.broadcasted_iota(jnp.int32, (blocks, LANES), 1)
    for k in range(sum(count for _, count in starts)):
        for pair in range(QUAD // 2):
            a = product[(2 * k) * blocks : (2 * k + 1) * blocks, lanes_of(pair)]
            b = product[(2 * k + 1) * blocks : (2 * k + 2) * blocks, lanes_of(pair)]
            crossed = pltpu.roll(jnp.where(lane < SPLIT, b, a), SPLIT, 1)
            write(k, 2 * pair, jnp.where(lane < SPLIT, a, crossed))
            write(k, 2 * pair + 1, jnp.where(lane < SPLIT, crossed, b))


def visit_kernel(
    offset_ref, weight_ref, low_ref, mid_ref, high_ref, cover_ref, table_ref, out_ref, windows, *lines
):
    weight = weight_ref[0]
    height, columns = mid_ref.shape
    blocks = columns // LANES
    shift = offset_ref[0] + HALF
    rows = out_ref.shape[2]
    pitch = 4 * blocks

    def fill(u):
        spot = lines[u % len(lines)]
        if u == 0:
            source, at = low_ref, slice(0, UNIT)
        elif u == height // UNIT + 1:
            source, at = high_ref, slice(0, UNIT)
        else:
            source, at = mid_ref, slice((u - 1) * UNIT, u * UNIT)
        pixels = [source[at, lanes_of(h)].astype(jnp.float32) for h in range(blocks)]
        lay_out(pixels, shift, spot, PAD, pitch)
        lay_out(pixels, shift - SPLIT, spot, PAD + 2 * blocks, pitch)
        tiles = spot[...].reshape(UNIT, pitch, LANES)
        both = [tiles[:, PAD + 2 * blocks * k : PAD + 2 * blocks * k + blocks] for k in range(2)]
        windows[u * (UNIT // QUAD) : (u + 1) * (UNIT // QUAD)] = (
            jnp.concatenate(both, axis=1)
            .astype(jnp.bfloat16)
            .reshape(UNIT // QUAD, QUAD, 2 * blocks, LANES)
        )

    done = 0
    for first in range(0, height, CHUNK):
        needed = min((first + CHUNK + 2 * HALO) // UNIT, height // UNIT + 2)
        for u in range(done, needed):
            fill(u)
        done = needed

        def write(k, e, line, first=first):
            r = first + QUAD * k + e
            cover = cover_ref[r]
            good = cover.astype(jnp.float32) > 0
            out_ref[r // rows, 0, r % rows] = (line * jnp.where(good, weight, 0.0)).astype(
                jnp.bfloat16
            )
            out_ref[r // rows, 1, r % rows] = cover

        multiply(windows, [(first // QUAD, CHUNK // QUAD)], table_ref, write)


def window_scratch(height, blocks):
    return pltpu.VMEM((height // QUAD, QUAD, 2 * blocks, LANES), jnp.bfloat16)


def conv_cost(height, columns):
    return pl.CostEstimate(
        flops=2 * height * columns * SHIFTS * LANES, bytes_accessed=8 * 10**6, transcendentals=0
    )


def match_visit(low, mid, high, cover, table, offset, weight, owners):
    height, columns = mid.shape
    blocks = columns // LANES
    smem = pl.BlockSpec(memory_space=pltpu.SMEM)
    vmem = pl.BlockSpec(memory_space=pltpu.VMEM)
    return pl.pallas_call(
        visit_kernel,
        out_shape=jax.ShapeDtypeStruct(
            (owners, 2, height // owners, blocks, LANES), jnp.bfloat16
        ),
        in_specs=[smem, smem] + [vmem] * 5,
        out_specs=vmem,
        scratch_shapes=[window_scratch(height + 2 * HALO, blocks)]
        + [pltpu.VMEM((UNIT * 4 * blocks, LANES), jnp.float32)] * 4,
        compiler_params=params(),
        cost_estimate=conv_cost(height, columns),
        name="match_visit",
    )(offset, weight, low, mid, high, cover, table)


def fill_windows(source, first, padded, windows, unit):
    blocks = source.shape[1]
    turn = SPLIT + HALF
    lane = lax.broadcasted_iota(jnp.int32, (UNIT, blocks, LANES), 2)
    here = source[first : first + UNIT].astype(jnp.float32)
    padded[:, PAD : PAD + blocks] = here
    before = padded[:, PAD - 1 : PAD - 1 + blocks]
    after = padded[:, PAD + 1 : PAD + 1 + blocks]
    left = pltpu.roll(jnp.where(lane < LANES - HALF, here, before), HALF, 2)
    right = pltpu.roll(jnp.where(lane < LANES - turn, after, here), turn, 2)
    both = jnp.concatenate([left, right], axis=1).astype(jnp.bfloat16)
    windows[unit * (UNIT // QUAD) : (unit + 1) * (UNIT // QUAD)] = both.reshape(
        UNIT // QUAD, QUAD, 2 * blocks, LANES
    )


def zero_edges(padded, blocks):
    edge = jnp.zeros((UNIT, PAD, LANES), jnp.float32)
    for spot in padded:
        spot[:, :PAD] = edge
        spot[:, PAD + blocks :] = edge


def interior_kernel(mid_ref, new_ref, table_ref, out_ref, windows, result, lines, sems, *padded):
    height, blocks, _ = mid_ref.shape
    zero_edges(padded, blocks)
    rows = (height - 2 * HALO) // PARTS
    copies = []
    done = 0
    for part in range(PARTS):
        first = HALO + part * rows
        needed = -(-(first + rows + HALF + 1) // UNIT)
        for u in range(done, min(needed, height // UNIT)):
            fill_windows(mid_ref, u * UNIT, padded[u % len(padded)], windows, u + 1)
        done = needed
        spot = lines.at[part % 2]

        def write(k, e, line, spot=spot):
            row = QUAD * k + e
            spot[row * blocks : (row + 1) * blocks, :] = line

        multiply(windows, [(first // QUAD, rows // QUAD)], table_ref, write)
        for h in range(blocks):
            result[first - HALO : first - HALO + rows, lanes_of(h)] = (
                new_ref[first : first + rows, lanes_of(h)].astype(jnp.float32)
                - spot[pl.ds(h, rows, stride=blocks), :]
            )
        copy = pltpu.make_async_copy(
            result.at[pl.ds(first - HALO, rows)], out_ref.at[pl.ds(first, rows)], sems.at[part]
        )
        copy.start()
        copies.append(copy)
    for copy in copies:
        copy.wait()


def subtract_interior(mid, new, table):
    height, blocks, _ = mid.shape
    vmem = pl.BlockSpec(memory_space=pltpu.VMEM)
    rows = (height - 2 * HALO) // PARTS
    return pl.pallas_call(
        interior_kernel,
        out_shape=jax.ShapeDtypeStruct(new.shape, jnp.float32),
        in_specs=[vmem] * 3,
        out_specs=pl.BlockSpec(memory_space=pl.ANY),
        scratch_shapes=[
            window_scratch(height + 2 * HALO, blocks),
            pltpu.VMEM((height - 2 * HALO, blocks * LANES), jnp.float32),
            pltpu.VMEM((2, rows * blocks, LANES), jnp.float32),
            pltpu.SemaphoreType.DMA((PARTS,)),
        ]
        + [pltpu.VMEM((UNIT, blocks + 2 * PAD, LANES), jnp.float32)] * 4,
        compiler_params=params(),
        cost_estimate=conv_cost(*new.shape),
        name="subtract_interior",
    )(mid, new, table)


def edge_kernel(low_ref, mid_ref, high_ref, new_ref, table_ref, _, out_ref, windows, result, lines, sems, *padded):
    height, blocks, _ = mid_ref.shape
    zero_edges(padded, blocks)
    sources = [
        (low_ref, 0),
        (mid_ref, 0),
        (mid_ref, UNIT),
        (mid_ref, height - 2 * UNIT),
        (mid_ref, height - UNIT),
        (high_ref, 0),
    ]
    for u, (source, first) in enumerate(sources):
        fill_windows(source, first, padded[u % len(padded)], windows, u)

    def write(k, e, line):
        row = QUAD * k + e
        lines[row * blocks : (row + 1) * blocks, :] = line

    each = HALO // QUAD
    multiply(windows, [(0, each), (3 * UNIT // QUAD, each)], table_ref, write)
    copies = []
    for side, first in enumerate((0, height - HALO)):
        for h in range(blocks):
            result[side, :, lanes_of(h)] = (
                new_ref[first : first + HALO, lanes_of(h)].astype(jnp.float32)
                - lines[pl.ds(side * HALO * blocks + h, HALO, stride=blocks), :]
            )
        copy = pltpu.make_async_copy(
            result.at[side], out_ref.at[pl.ds(first, HALO)], sems.at[side]
        )
        copy.start()
        copies.append(copy)
    for copy in copies:
        copy.wait()


def subtract_edges(low, mid, high, new, table, difference):
    _, blocks, _ = mid.shape
    vmem = pl.BlockSpec(memory_space=pltpu.VMEM)
    return pl.pallas_call(
        edge_kernel,
        out_shape=jax.ShapeDtypeStruct(difference.shape, difference.dtype),
        in_specs=[vmem] * 5 + [pl.BlockSpec(memory_space=pl.ANY)],
        out_specs=pl.BlockSpec(memory_space=pl.ANY),
        input_output_aliases={5: 0},
        scratch_shapes=[
            window_scratch(6 * UNIT, blocks),
            pltpu.VMEM((2, HALO, blocks * LANES), jnp.float32),
            pltpu.VMEM((2 * HALO * blocks, LANES), jnp.float32),
            pltpu.SemaphoreType.DMA((2,)),
        ]
        + [pltpu.VMEM((UNIT, blocks + 2 * PAD, LANES), jnp.float32)] * 3,
        compiler_params=params(),
        cost_estimate=conv_cost(2 * HALO, new.shape[1]),
        name="subtract_edges",
    )(low, mid, high, new, table, difference)


def combine_kernel(patch_ref, wanted_ref, received_ref, coadd_ref, send_ref, sums, packed, lines):
    _, _, rows, blocks, _ = received_ref.shape
    sums[...] = jnp.zeros_like(sums)

    def add(v, carry):
        p = patch_ref[v]
        sums[p] = sums[p] + received_ref[v].astype(jnp.float32)
        return carry

    lax.fori_loop(0, received_ref.shape[0], add, 0)
    for p in range(PATCHES):
        ratio = sums[p, 0] / jnp.maximum(sums[p, 1], 1.0)
        packed[p] = ratio.astype(jnp.bfloat16)
        lines[p] = ratio.reshape(rows * blocks, LANES)
        for h in range(blocks):
            coadd_ref[p, :, lanes_of(h)] = lines[p, pl.ds(h, rows, stride=blocks), :].astype(
                jnp.bfloat16
            )

    def place(n, carry):
        send_ref[n] = packed[wanted_ref[n]]
        return carry

    lax.fori_loop(0, send_ref.shape[0], place, 0)


def combine(received, patch_of, new_patch):
    _, _, rows, blocks, _ = received.shape
    smem = pl.BlockSpec(memory_space=pltpu.SMEM)
    vmem = pl.BlockSpec(memory_space=pltpu.VMEM)
    return pl.pallas_call(
        combine_kernel,
        out_shape=(
            jax.ShapeDtypeStruct((PATCHES, rows, blocks * LANES), jnp.bfloat16),
            jax.ShapeDtypeStruct((new_patch.shape[0], rows, blocks, LANES), jnp.bfloat16),
        ),
        in_specs=[smem, smem, vmem],
        out_specs=(vmem, vmem),
        scratch_shapes=[
            pltpu.VMEM((PATCHES, 2, rows, blocks, LANES), jnp.float32),
            pltpu.VMEM((PATCHES, rows, blocks, LANES), jnp.bfloat16),
            pltpu.VMEM((PATCHES, rows * blocks, LANES), jnp.float32),
        ],
        compiler_params=params(),
        name="combine",
    )(patch_of, new_patch, received)


def exchange(chunks):
    return lax.all_to_all(chunks, "visit", split_axis=0, concat_axis=0, tiled=True)


def per_device(
    visit_image,
    good_mask,
    basis_rows,
    basis_cols,
    visit_coeff,
    visit_weight,
    col_offset,
    patch_of,
    new_image,
    new_coeff,
    new_patch,
):
    owners = lax.axis_size("visit")
    low, high = neighbours(visit_image[0], "tile")
    visit_table, new_table = build_tables(basis_rows, basis_cols, visit_coeff, new_coeff)
    cover = cover_rows(col_offset, visit_weight, good_mask[0])
    outgoing = match_visit(
        low, visit_image[0], high, cover, visit_table, col_offset, visit_weight, owners
    )
    received = exchange(outgoing)
    coadd, wanted = combine(received, patch_of[:, 0], new_patch[:, 0])
    template = exchange(wanted)
    template = template.reshape((-1,) + template.shape[2:])
    low, high = neighbours(template, "tile")
    difference = subtract_interior(template, new_image[0], new_table)
    difference = subtract_edges(low, template, high, new_image[0], new_table, difference)
    return (coadd[:, None], difference[None])


def solution(mesh):
    return jax.shard_map(
        per_device,
        mesh=mesh,
        in_specs=(
            P("visit", "tile", None),
            P("visit", "tile", None),
            P(),
            P(),
            P("visit", None),
            P("visit"),
            P("visit"),
            P(),
            P("visit", "tile", None),
            P("visit", None),
            P(),
        ),
        out_specs=(P(None, "tile", "visit", None), P("visit", "tile", None)),
        check_vma=False,
    )
```

time: 133 us -> 133 us (level)
  blocking collectives: 33 us -> 91.9 us
  waiting for transfers between devices: 31.8 us -> 0.01 us
  starting transfers between devices: 36.4 us -> 16.5 us
  Pallas kernels: 26.8 us -> 19.5 us
    all_to_all x1 -> x2, blocking collectives: 33 us -> 91.9 us  [exchange(): lax.all_to_all(chunks, 'visit', split_axis=0, concat_axis=0, tiled=True)]
    all_to_all x2 -> x0, waiting for transfers between devices: 26.7 us -> none  [to_owners(): lax.all_to_all(lines.reshape(owners, height // owners, blocks, LANES), 'v...]
    all_to_all x2 -> x0, starting transfers between devices: 20.6 us -> none  [to_owners(): lax.all_to_all(lines.reshape(owners, height // owners, blocks, LANES), 'v...]
    pallas_call x3, Pallas kernels: 20.7 us -> 14.1 us  [the longest x1 7.68 us: match_visit(): pl.pallas_call(visit_kernel, out_shape=jax.ShapeDtypeStruct((owners, 2, h...]
    ppermute x2, waiting for transfers between devices: 5.12 us -> 0.01 us  [neighbours(): high = lax.ppermute(block[:HALO], axis, backward)]
    ppermute x2, starting transfers between devices: 3.84 us -> 7.25 us  [neighbours(): high = lax.ppermute(block[:HALO], axis, backward)]
    ppermute x2, starting transfers between devices: 12 us -> 9.28 us  [neighbours(): low = lax.ppermute(block[-HALO:], axis, forward)]
    unnamed x22 -> x18, local copies, waits for them, and re-layouts: 2.76 us -> 1.63 us
  transfers between devices with their start and end apart: 6 -> 4, of which waited for: 4 -> 0; matrix products, arithmetic and copies ran while one was open for 0% -> 0% of each run, Pallas kernels for 11% -> 6%
where the time goes in v3:
time: 133 us
  blocking collectives  91.9 us (69%)
  Pallas kernels  19.5 us (15%)
  starting transfers between devices  16.5 us (12%)
  local copies, waits for them, and re-layouts  2.54 us (2%)
  between operations  2.3 us (2%)
    all_to_all x2, blocking collectives, exchange(): lax.all_to_all(chunks, 'visit', split_axis=0, concat_axis=0, tiled=True)  91.9 us
    ppermute x2, starting transfers between devices, neighbours(): low = lax.ppermute(block[-HALO:], axis, forward)  9.28 us
    pallas_call x1, Pallas kernels, match_visit(): pl.pallas_call(visit_kernel, out_shape=jax.ShapeDtypeStruct((owners, 2, h...  7.68 us
    ppermute x2, starting transfers between devices, neighbours(): high = lax.ppermute(block[:HALO], axis, backward)  7.25 us
    pallas_call x1, Pallas kernels, subtract_interior(): pl.pallas_call(interior_kernel, out_shape=jax.ShapeDtypeStruct(new.shape,...  4.9 us
  transfers between devices with their start and end apart: 4, of which 0 were waited for; matrix products, arithmetic and copies ran while one was open for 0% of the time, Pallas kernels for 6%

profile of v3, /device:TPU:1, one launch (start us, length us, event | category | flops | bytes accessed | tf_op | source)
XLA Modules:
  0.0 132.8 jit_solution(5269578179920740175)
XLA Ops:
  0.6 0.0 copy-start.8
  0.6 0.0 copy-start.7
  0.7 0.0 copy-start.6
  0.7 0.0 copy-start.5
  0.7 0.9 slice_bitcast_fusion
  1.6 5.1 %collective-permute-start.1 = (bf16[16,2048]{1,0:T(8,128)(2,1)S(1)}, bf16[16,2048]{1,0:T(8,128)(2,1)S(1)}, u32[]{:S(2)}, u32[]{:S(2)}) collective-permute-start(bf16[16,2048]{1,0:T(8,128)(2,1)S(1)} %get-tuple-element.14), channel_id=1, source_target_pairs={{1,0},{2,1},{3,2},{4,3},{5,4},{6,5},{7,6},{9,8},{10,9},{11,10},{12... | collective-permute-start | bytes 196616 | tf_op jit(solution)/shard_map/ppermute | solution.py:32
  6.7 1.9 %collective-permute-start = (bf16[16,2048]{1,0:T(8,128)(2,1)S(1)}, bf16[16,2048]{1,0:T(8,128)(2,1)S(1)}, u32[]{:S(2)}, u32[]{:S(2)}) collective-permute-start(bf16[16,2048]{1,0:T(8,128)(2,1)S(1)} %get-tuple-element.15), channel_id=1, source_target_pairs={{0,1},{1,2},{2,3},{3,4},{4,5},{5,6},{6,7},{8,9},{9,10},{10,11},{11... | collective-permute-start | bytes 196616 | tf_op jit(solution)/shard_map/ppermute | solution.py:31
  10.0 0.0 copy-start
  10.0 1.6 %copy-done = s32[1,256,2048]{2,1,0:T(8,128)S(1)} copy-done((s32[1,256,2048]{2,1,0:T(8,128)S(1)}, s32[1,256,2048]{2,1,0:T(8,128)}, u32[]{:S(2)}) %copy-start) | copy-done | bytes 2097176
  11.6 1.9 %cover_rows.1.cover_ref = bf16[256,16,128]{2,1,0:T(8,128)(2,1)S(1)} custom-call(s32[1]{0:T(128)S(6)} %copy.17.offset_ref, f32[1]{0:T(128)S(6)} %copy.16.weight_ref, s32[256,2048]{1,0:T(8,128)S(1)} %bitcast.20), custom_call_target="tpu_custom_call" | custom-call | flops 1000000 | bytes 6000000 | tf_op jit(solution)/shard_map/cover_rows/pallas_call | solution.py:122
  13.5 0.0 copy-start.2
  13.5 0.0 copy-done.8
  13.5 0.0 copy-done.7
  13.5 0.0 copy-done.6
  13.5 0.0 copy-done.5
  13.5 1.3 tables.1
  14.8 0.0 collective-permute-done.1.high_ref
  14.8 0.0 collective-permute-done.low_ref
  14.9 0.0 copy-done.2
  14.9 7.7 %match_visit.1 = bf16[32,2,8,16,128]{4,3,2,1,0:T(8,128)(2,1)S(1)} custom-call(s32[1]{0:T(128)S(6)} %copy.17.offset_ref, f32[1]{0:T(128)S(6)} %copy.16.weight_ref, bf16[16,2048]{1,0:T(8,128)(2,1)S(1)} %collective-permute-done.low_ref, bf16[256,2048]{1,0:T(8,128)(2,1)S(1)} %bitcast.23, bf16[16,2048]{1,0:T(8,128)(2,1)S(1)} %collective-permute-done.1.high_ref, ...), custom_call_target="tpu_custom_call" | custom-call | flops 3221225472 | bytes 8000000 | tf_op jit(solution)/shard_map/match_visit/pallas_call | solution.py:221
  22.5 0.0 copy-start.3
  22.6 0.0 copy-start.4
  22.6 60.7 %all_to_all.10.received_ref = bf16[32,2,8,16,128]{4,3,2,1,0:T(8,128)(2,1)S(1)} all-to-all(bf16[32,2,8,16,128]{4,3,2,1,0:T(8,128)(2,1)S(1)} %match_visit.1), channel_id=1, replica_groups=mesh['visit'=32,'tile'=8] {'visit'}, dimensions={0} | all-to-all | bytes 4194304 | tf_op jit(solution)/shard_map/all_to_all | solution.py:421
  83.2 0.0 copy-done.3
  83.2 0.0 copy-done.4
  83.2 0.0 copy-start.1
  83.3 2.3 %combine.1 = (bf16[8,8,2048]{2,1,0:T(8,128)(2,1)}, bf16[32,8,16,128]{3,2,1,0:T(8,128)(2,1)S(1)}) custom-call(s32[32]{0:T(128)S(1)} %bitcast.24, s32[32]{0:T(128)S(1)} %bitcast.25, bf16[32,2,8,16,128]{4,3,2,1,0:T(8,128)(2,1)S(1)} %all_to_all.10.received_ref), custom_call_target="tpu_custom_call" | custom-call | tf_op jit(solution)/shard_map/combine/pallas_call | solution.py:402
  85.5 31.2 %all_to_all.11 = bf16[32,8,16,128]{3,2,1,0:T(8,128)(2,1)S(1)} all-to-all(bf16[32,8,16,128]{3,2,1,0:T(8,128)(2,1)S(1)} %get-tuple-element.8), channel_id=1, replica_groups=mesh['visit'=32,'tile'=8] {'visit'}, dimensions={0} | all-to-all | bytes 2097152 | tf_op jit(solution)/shard_map/all_to_all | solution.py:421
  116.8 7.4 %collective-permute-start.2 = (bf16[16,16,128]{2,1,0:T(8,128)(2,1)S(1)}, bf16[16,16,128]{2,1,0:T(8,128)(2,1)S(1)}, u32[]{:S(2)}, u32[]{:S(2)}) collective-permute-start(bf16[16,16,128]{2,1,0:T(8,128)(2,1)S(1)} %bitcast.30), channel_id=1, source_target_pairs={{0,1},{1,2},{2,3},{3,4},{4,5},{5,6},{6,7},{8,9},{9,10},{10,11},{11... | collective-permute-start | bytes 196616 | tf_op jit(solution)/shard_map/ppermute | solution.py:31
  124.1 2.1 %collective-permute-start.3 = (bf16[16,16,128]{2,1,0:T(8,128)(2,1)S(1)}, bf16[16,16,128]{2,1,0:T(8,128)(2,1)S(1)}, u32[]{:S(2)}, u32[]{:S(2)}) collective-permute-start(bf16[16,16,128]{2,1,0:T(8,128)(2,1)S(1)} %bitcast.29), channel_id=1, source_target_pairs={{1,0},{2,1},{3,2},{4,3},{5,4},{6,5},{7,6},{9,8},{10,9},{11,10},{12... | collective-permute-start | bytes 196616 | tf_op jit(solution)/shard_map/ppermute | solution.py:32
  126.2 0.0 copy-done.1
  126.2 4.9 %subtract_interior.1._ = f32[256,2048]{1,0:T(8,128)} custom-call(bf16[256,16,128]{2,1,0:T(8,128)(2,1)S(1)} %bitcast.18, bf16[256,2048]{1,0:T(8,128)(2,1)S(1)} %bitcast.21, bf16[3072,256]{1,0:T(8,128)(2,1)S(1)} %get-tuple-element.9.table_ref), custom_call_target="tpu_custom_call" | custom-call | flops 3221225472 | bytes 8000000 | tf_op jit(solution)/shard_map/subtract_interior/pallas_call | solution.py:296
  131.2 0.0 collective-permute-done.2.low_ref
  131.2 0.0 collective-permute-done.3.high_ref
  131.2 1.5 %subtract_edges.1 = f32[256,2048]{1,0:T(8,128)} custom-call(bf16[16,16,128]{2,1,0:T(8,128)(2,1)S(1)} %collective-permute-done.2.low_ref, bf16[256,16,128]{2,1,0:T(8,128)(2,1)S(1)} %bitcast.19, bf16[16,16,128]{2,1,0:T(8,128)(2,1)S(1)} %collective-permute-done.3.high_ref, bf16[256,2048]{1,0:T(8,128)(2,1)S(1)} %bitcast.22, ...), custom_call_target="tpu_custom_call", output_to_operand_aliasing={{}: (5, {})} | custom-call | flops 402653184 | bytes 8000000 | tf_op jit(solution)/shard_map/subtract_edges/pallas_call | solution.py:353
  (1 shorter events, 0.0 us)
Async XLA Ops:
  0.6 12.9 %copy-start.8 = (f32[1,27]{1,0:T(1,128)S(1)}, f32[1,27]{1,0:T(1,128)}, u32[]{:S(2)}) copy-start(f32[1,27]{1,0:T(1,128)} %second_ref.1) | copy-start | bytes 328
  0.6 12.9 %copy-start.7 = (f32[1,27]{1,0:T(1,128)S(1)}, f32[1,27]{1,0:T(1,128)}, u32[]{:S(2)}) copy-start(f32[1,27]{1,0:T(1,128)} %first_ref.1) | copy-start | bytes 328
  0.7 12.9 %copy-start.6 = (f32[27,21]{0,1:T(8,128)S(1)}, f32[27,21]{0,1:T(8,128)}, u32[]{:S(2)}) copy-start(f32[27,21]{0,1:T(8,128)} %param.14) | copy-start | bytes 6808
  0.7 12.9 %copy-start.5 = (f32[27,21]{0,1:T(8,128)S(1)}, f32[27,21]{0,1:T(8,128)}, u32[]{:S(2)}) copy-start(f32[27,21]{0,1:T(8,128)} %param.13) | copy-start | bytes 6808
  1.6 13.3 %collective-permute-start.1 = (bf16[16,2048]{1,0:T(8,128)(2,1)S(1)}, bf16[16,2048]{1,0:T(8,128)(2,1)S(1)}, u32[]{:S(2)}, u32[]{:S(2)}) collective-permute-start(bf16[16,2048]{1,0:T(8,128)(2,1)S(1)} %get-tuple-element.14), channel_id=1, source_target_pairs={{1,0},{2,1},{3,2},{4,3},{5,4},{6,5},{7,6},{9,8},{10,9},{11,10},{12... | collective-permute-start | bytes 196616 | tf_op jit(solution)/shard_map/ppermute | solution.py:32
  6.7 8.1 %collective-permute-start = (bf16[16,2048]{1,0:T(8,128)(2,1)S(1)}, bf16[16,2048]{1,0:T(8,128)(2,1)S(1)}, u32[]{:S(2)}, u32[]{:S(2)}) collective-permute-start(bf16[16,2048]{1,0:T(8,128)(2,1)S(1)} %get-tuple-element.15), channel_id=1, source_target_pairs={{0,1},{1,2},{2,3},{3,4},{4,5},{5,6},{6,7},{8,9},{9,10},{10,11},{11... | collective-permute-start | bytes 196616 | tf_op jit(solution)/shard_map/ppermute | solution.py:31
  10.0 1.6 %copy-start = (s32[1,256,2048]{2,1,0:T(8,128)S(1)}, s32[1,256,2048]{2,1,0:T(8,128)}, u32[]{:S(2)}) copy-start(s32[1,256,2048]{2,1,0:T(8,128)} %param.12) | copy-start | bytes 6291460
  13.5 1.4 %copy-start.2 = (bf16[1,256,2048]{2,1,0:T(8,128)(2,1)S(1)}, bf16[1,256,2048]{2,1,0:T(8,128)(2,1)}, u32[]{:S(2)}) copy-start(bf16[1,256,2048]{2,1,0:T(8,128)(2,1)} %param.11) | copy-start | bytes 3145732
  22.5 60.7 %copy-start.3 = (s32[32,1]{0,1:T(1,128)S(1)}, s32[32,1]{0,1:T(1,128)}, u32[]{:S(2)}) copy-start(s32[32,1]{0,1:T(1,128)} %param.18) | copy-start | bytes 388
  22.6 60.7 %copy-start.4 = (s32[32,1]{0,1:T(1,128)S(1)}, s32[32,1]{0,1:T(1,128)}, u32[]{:S(2)}) copy-start(s32[32,1]{0,1:T(1,128)} %param.21) | copy-start | bytes 388
  83.2 43.0 %copy-start.1 = (bf16[1,256,2048]{2,1,0:T(8,128)(2,1)S(1)}, bf16[1,256,2048]{2,1,0:T(8,128)(2,1)}, u32[]{:S(2)}) copy-start(bf16[1,256,2048]{2,1,0:T(8,128)(2,1)} %param.19) | copy-start | bytes 3145732
  116.8 14.4 %collective-permute-start.2 = (bf16[16,16,128]{2,1,0:T(8,128)(2,1)S(1)}, bf16[16,16,128]{2,1,0:T(8,128)(2,1)S(1)}, u32[]{:S(2)}, u32[]{:S(2)}) collective-permute-start(bf16[16,16,128]{2,1,0:T(8,128)(2,1)S(1)} %bitcast.30), channel_id=1, source_target_pairs={{0,1},{1,2},{2,3},{3,4},{4,5},{5,6},{6,7},{8,9},{9,10},{10,11},{11... | collective-permute-start | bytes 196616 | tf_op jit(solution)/shard_map/ppermute | solution.py:31
  124.1 7.0 %collective-permute-start.3 = (bf16[16,16,128]{2,1,0:T(8,128)(2,1)S(1)}, bf16[16,16,128]{2,1,0:T(8,128)(2,1)S(1)}, u32[]{:S(2)}, u32[]{:S(2)}) collective-permute-start(bf16[16,16,128]{2,1,0:T(8,128)(2,1)S(1)} %bitcast.29), channel_id=1, source_target_pairs={{1,0},{2,1},{3,2},{4,3},{5,4},{6,5},{7,6},{9,8},{10,9},{11,10},{12... | collective-permute-start | bytes 196616 | tf_op jit(solution)/shard_map/ppermute | solution.py:32

commit v4 on v3

--- a/solution.py
+++ b/solution.py
@@ -13,11 +13,10 @@
 QUAD = 4
 SPLIT = LANES // 2
 SHIFTS = QUAD + KS - 1
-CHUNK = 64
 PARTS = 4
 UNIT = 16
 PAD = 8
-VMEM_LIMIT = 24 * 2**20
+VMEM_LIMIT = 16 * 2**20
 
 
 def params():
@@ -33,7 +32,7 @@
     return low, high
 
 
-def table_kernel(rows_ref, cols_ref, first_ref, second_ref, *table_refs):
+def fill_table(rows_ref, cols_ref, coeff_ref, table_ref):
     wide = QUAD * SPLIT
     tap = lax.broadcasted_iota(jnp.int32, (KS, wide), 0)
     place = lax.broadcasted_iota(jnp.int32, (KS, wide), 1)
@@ -42,41 +41,39 @@
     lane = lax.broadcasted_iota(jnp.int32, (LANES, wide), 0)
     column = lax.broadcasted_iota(jnp.int32, (LANES, wide), 1) % SPLIT
     inside = (lane >= column) & (lane - column < KS)
-    for coeff_ref, table_ref in zip((first_ref, second_ref), table_refs):
-        kernel = lax.dot_general(
-            rows_ref[...] * coeff_ref[...],
-            cols_ref[...],
-            (((1,), (1,)), ((), ())),
-            precision=lax.Precision.HIGHEST,
-            preferred_element_type=jnp.float32,
-        ).astype(jnp.bfloat16)
-        profile = jnp.zeros((SHIFTS, wide), jnp.float32)
-        for e in range(QUAD):
-            at = (SPLIT * e - tap) % wide
-            spread = jnp.dot(
-                kernel, (place == at).astype(jnp.bfloat16), preferred_element_type=jnp.float32
-            )
-            lowered = (shift - e == row_tap).astype(jnp.bfloat16)
-            profile = profile + jnp.dot(
-                lowered, spread.astype(jnp.bfloat16), preferred_element_type=jnp.float32
-            )
-        for s in range(SHIFTS):
-            line = jnp.broadcast_to(profile[s : s + 1], (LANES, wide))
-            rolled = pltpu.roll(line, 0, 1, stride=1, stride_axis=0)
-            table_ref[s * LANES : (s + 1) * LANES, :] = jnp.where(inside, rolled, 0.0).astype(
-                jnp.bfloat16
-            )
-
-
-def build_tables(basis_rows, basis_cols, visit_coeff, new_coeff):
-    table = jax.ShapeDtypeStruct((SHIFTS * LANES, QUAD * SPLIT), jnp.bfloat16)
-    return pl.pallas_call(
-        table_kernel,
-        out_shape=(table, table),
-        compiler_params=params(),
-        cost_estimate=pl.CostEstimate(flops=10**9, bytes_accessed=4 * 10**6, transcendentals=0),
-        name="tables",
-    )(basis_rows.T, basis_cols.T, visit_coeff, new_coeff)
+    kernel = lax.dot_general(
+        rows_ref[...] * coeff_ref[...],
+        cols_ref[...],
+        (((1,), (1,)), ((), ())),
+        precision=lax.Precision.HIGHEST,
+        preferred_element_type=jnp.float32,
+    ).astype(jnp.bfloat16)
+    profile = jnp.zeros((SHIFTS, wide), jnp.float32)
+    for e in range(QUAD):
+        at = (SPLIT * e - tap) % wide
+        spread = jnp.dot(
+            kernel, (place == at).astype(jnp.bfloat16), preferred_element_type=jnp.float32
+        )
+        lowered = (shift - e == row_tap).astype(jnp.bfloat16)
+        profile = profile + jnp.dot(
+            lowered, spread.astype(jnp.bfloat16), preferred_element_type=jnp.float32
+        )
+    for s in range(SHIFTS):
+        line = jnp.broadcast_to(profile[s : s + 1], (LANES, wide))
+        rolled = pltpu.roll(line, 0, 1, stride=1, stride_axis=0)
+        table_ref[s * LANES : (s + 1) * LANES, :] = jnp.where(inside, rolled, 0.0).astype(
+            jnp.bfloat16
+        )
+
+
+def build_table(basis_rows, basis_cols, coeff):
+    return pl.pallas_call(
+        fill_table,
+        out_shape=jax.ShapeDtypeStruct((SHIFTS * LANES, QUAD * SPLIT), jnp.bfloat16),
+        compiler_params=params(),
+        cost_estimate=pl.CostEstimate(flops=10**9, bytes_accessed=2 * 10**6, transcendentals=0),
+        name="table",
+    )(basis_rows.T, basis_cols.T, coeff)
 
 
 def split_shift(shift):
@@ -99,36 +96,6 @@
 
 def lanes_of(h):
     return slice(h * LANES, (h + 1) * LANES)
-
-
-def cover_kernel(offset_ref, weight_ref, mask_ref, out_ref, *lines):
-    height, columns = mask_ref.shape
-    blocks = columns // LANES
-    weight = weight_ref[0]
-    for u in range(height // UNIT):
-        spot = lines[u % len(lines)]
-        rows = slice(u * UNIT, (u + 1) * UNIT)
-        good = [mask_ref[rows, lanes_of(h)].astype(jnp.float32) * weight for h in range(blocks)]
-        lay_out(good, offset_ref[0], spot, PAD, 2 * blocks)
-        tiles = spot[...].reshape(UNIT, 2 * blocks, LANES)
-        out_ref[rows] = tiles[:, PAD : PAD + blocks].astype(jnp.bfloat16)
-
-
-def cover_rows(offset, weight, mask):
-    height, columns = mask.shape
-    blocks = columns // LANES
-    smem = pl.BlockSpec(memory_space=pltpu.SMEM)
-    vmem = pl.BlockSpec(memory_space=pltpu.VMEM)
-    return pl.pallas_call(
-        cover_kernel,
-        out_shape=jax.ShapeDtypeStruct((height, blocks, LANES), jnp.bfloat16),
-        in_specs=[smem, smem, vmem],
-        out_specs=vmem,
-        scratch_shapes=[pltpu.VMEM((UNIT * 2 * blocks, LANES), jnp.float32)] * 4,
-        compiler_params=params(),
-        cost_estimate=pl.CostEstimate(flops=10**6, bytes_accessed=6 * 10**6, transcendentals=0),
-        name="cover_rows",
-    )(offset, weight, mask)
 
 
 def multiply(windows, starts, table_ref, write):
@@ -155,52 +122,100 @@
             write(k, 2 * pair + 1, jnp.where(lane < SPLIT, crossed, b))
 
 
-def visit_kernel(
-    offset_ref, weight_ref, low_ref, mid_ref, high_ref, cover_ref, table_ref, out_ref, windows, *lines
-):
-    weight = weight_ref[0]
-    height, columns = mid_ref.shape
-    blocks = columns // LANES
-    shift = offset_ref[0] + HALF
-    rows = out_ref.shape[2]
+def lay_out_unit(source, first, shift, spot, windows, unit):
+    blocks = windows.shape[2] // 2
     pitch = 4 * blocks
-
-    def fill(u):
-        spot = lines[u % len(lines)]
-        if u == 0:
-            source, at = low_ref, slice(0, UNIT)
-        elif u == height // UNIT + 1:
-            source, at = high_ref, slice(0, UNIT)
-        else:
-            source, at = mid_ref, slice((u - 1) * UNIT, u * UNIT)
-        pixels = [source[at, lanes_of(h)].astype(jnp.float32) for h in range(blocks)]
-        lay_out(pixels, shift, spot, PAD, pitch)
-        lay_out(pixels, shift - SPLIT, spot, PAD + 2 * blocks, pitch)
-        tiles = spot[...].reshape(UNIT, pitch, LANES)
-        both = [tiles[:, PAD + 2 * blocks * k : PAD + 2 * blocks * k + blocks] for k in range(2)]
-        windows[u * (UNIT // QUAD) : (u + 1) * (UNIT // QUAD)] = (
-            jnp.concatenate(both, axis=1)
-            .astype(jnp.bfloat16)
-            .reshape(UNIT // QUAD, QUAD, 2 * blocks, LANES)
-        )
-
+    pixels = [source[first : first + UNIT, lanes_of(h)].astype(jnp.float32) for h in range(blocks)]
+    lay_out(pixels, shift, spot, PAD, pitch)
+    lay_out(pixels, shift - SPLIT, spot, PAD + 2 * blocks, pitch)
+    tiles = spot[...].reshape(UNIT, pitch, LANES)
+    both = [tiles[:, PAD + 2 * blocks * k : PAD + 2 * blocks * k + blocks] for k in range(2)]
+    windows[unit * (UNIT // QUAD) : (unit + 1) * (UNIT // QUAD)] = (
+        jnp.concatenate(both, axis=1)
+        .astype(jnp.bfloat16)
+        .reshape(UNIT // QUAD, QUAD, 2 * blocks, LANES)
+    )
+
+
+def match_interior(mid_ref, cover_ref, table_ref, shift, weight, out_ref, windows, lines):
+    height = mid_ref.shape[0]
+    rows = (height - 2 * HALO) // PARTS
     done = 0
-    for first in range(0, height, CHUNK):
-        needed = min((first + CHUNK + 2 * HALO) // UNIT, height // UNIT + 2)
+    for part in range(PARTS):
+        first = HALO + part * rows
+        needed = min(-(-(first + rows + HALF + 1) // UNIT), height // UNIT)
         for u in range(done, needed):
-            fill(u)
+            lay_out_unit(mid_ref, u * UNIT, shift, lines[u % len(lines)], windows, u + 1)
         done = needed
 
         def write(k, e, line, first=first):
             r = first + QUAD * k + e
-            cover = cover_ref[r]
-            good = cover.astype(jnp.float32) > 0
-            out_ref[r // rows, 0, r % rows] = (line * jnp.where(good, weight, 0.0)).astype(
-                jnp.bfloat16
-            )
-            out_ref[r // rows, 1, r % rows] = cover
-
-        multiply(windows, [(first // QUAD, CHUNK // QUAD)], table_ref, write)
+            good = cover_ref[r].astype(jnp.float32) > 0
+            out_ref[r] = (line * jnp.where(good, weight, 0.0)).astype(jnp.bfloat16)
+
+        multiply(windows, [(first // QUAD, rows // QUAD)], table_ref, write)
+
+
+def late_group():
+    return lax.axis_index("tile") % 2 == 1
+
+
+def first_kernel(
+    offset_ref, weight_ref, mask_ref, mid_ref, rows_ref, cols_ref, coeff_ref, cover_ref, out_ref, windows, table_ref, *lines
+):
+    height, columns = mask_ref.shape
+    blocks = columns // LANES
+    weight = weight_ref[0]
+    for u in range(height // UNIT):
+        spot = lines[u % len(lines)]
+        rows = slice(u * UNIT, (u + 1) * UNIT)
+        good = [mask_ref[rows, lanes_of(h)].astype(jnp.float32) * weight for h in range(blocks)]
+        lay_out(good, offset_ref[0], spot, PAD, 4 * blocks)
+        tiles = spot[...].reshape(UNIT, 4 * blocks, LANES)
+        cover_ref[rows] = tiles[:, PAD : PAD + blocks].astype(jnp.bfloat16)
+
+    @pl.when(late_group())
+    def _():
+        fill_table(rows_ref, cols_ref, coeff_ref, table_ref)
+        shift = offset_ref[0] + HALF
+        match_interior(mid_ref, cover_ref, table_ref, shift, weight, out_ref, windows, lines)
+
+
+def second_kernel(
+    offset_ref, weight_ref, low_ref, mid_ref, high_ref, cover_ref, rows_ref, cols_ref, coeff_ref, early_ref, out_ref, windows, table_ref, *lines
+):
+    height = mid_ref.shape[0]
+    weight = weight_ref[0]
+    shift = offset_ref[0] + HALF
+    late = late_group()
+    fill_table(rows_ref, cols_ref, coeff_ref, table_ref)
+
+    @pl.when(late)
+    def _():
+        out_ref[HALO : height - HALO] = early_ref[HALO : height - HALO]
+
+    @pl.when(jnp.logical_not(late))
+    def _():
+        match_interior(mid_ref, cover_ref, table_ref, shift, weight, out_ref, windows, lines)
+
+    sources = [
+        (low_ref, 0),
+        (mid_ref, 0),
+        (mid_ref, UNIT),
+        (mid_ref, height - 2 * UNIT),
+        (mid_ref, height - UNIT),
+        (high_ref, 0),
+    ]
+    for u, (source, first) in enumerate(sources):
+        lay_out_unit(source, first, shift, lines[u % len(lines)], windows, u)
+    each = HALO // QUAD
+
+    def write(k, e, line):
+        r = QUAD * k + e + (0 if k < each else height - 2 * HALO)
+        good = cover_ref[r].astype(jnp.float32) > 0
+        out_ref[r] = (line * jnp.where(good, weight, 0.0)).astype(jnp.bfloat16)
+
+    multiply(windows, [(0, each), (3 * UNIT // QUAD, each)], table_ref, write)
 
 
 def window_scratch(height, blocks):
@@ -213,24 +228,48 @@
     )
 
 
-def match_visit(low, mid, high, cover, table, offset, weight, owners):
+def visit_scratch(height, blocks):
+    return [
+        window_scratch(height + 2 * HALO, blocks),
+        pltpu.VMEM((SHIFTS * LANES, QUAD * SPLIT), jnp.bfloat16),
+    ] + [
+        pltpu.VMEM((UNIT * 4 * blocks, LANES), jnp.float32)
+    ] * 4
+
+
+def match_first(mid, mask, basis, offset, weight):
     height, columns = mid.shape
     blocks = columns // LANES
     smem = pl.BlockSpec(memory_space=pltpu.SMEM)
     vmem = pl.BlockSpec(memory_space=pltpu.VMEM)
-    return pl.pallas_call(
-        visit_kernel,
-        out_shape=jax.ShapeDtypeStruct(
-            (owners, 2, height // owners, blocks, LANES), jnp.bfloat16
-        ),
+    rows = jax.ShapeDtypeStruct((height, blocks, LANES), jnp.bfloat16)
+    return pl.pallas_call(
+        first_kernel,
+        out_shape=(rows, rows),
         in_specs=[smem, smem] + [vmem] * 5,
+        out_specs=(vmem, vmem),
+        scratch_shapes=visit_scratch(height, blocks),
+        compiler_params=params(),
+        cost_estimate=conv_cost(height, columns),
+        name="match_first",
+    )(offset, weight, mask, mid, *basis)
+
+
+def match_second(low, mid, high, cover, basis, offset, weight, early):
+    height, columns = mid.shape
+    blocks = columns // LANES
+    smem = pl.BlockSpec(memory_space=pltpu.SMEM)
+    vmem = pl.BlockSpec(memory_space=pltpu.VMEM)
+    return pl.pallas_call(
+        second_kernel,
+        out_shape=jax.ShapeDtypeStruct(cover.shape, jnp.bfloat16),
+        in_specs=[smem, smem] + [vmem] * 8,
         out_specs=vmem,
-        scratch_shapes=[window_scratch(height + 2 * HALO, blocks)]
-        + [pltpu.VMEM((UNIT * 4 * blocks, LANES), jnp.float32)] * 4,
+        scratch_shapes=visit_scratch(height, blocks),
         compiler_params=params(),
         cost_estimate=conv_cost(height, columns),
-        name="match_visit",
-    )(offset, weight, low, mid, high, cover, table)
+        name="match_second",
+    )(offset, weight, low, mid, high, cover, *basis, early)
 
 
 def fill_windows(source, first, padded, windows, unit):
@@ -369,8 +408,7 @@
     )(low, mid, high, new, table, difference)
 
 
-def combine_kernel(patch_ref, wanted_ref, received_ref, coadd_ref, send_ref, sums, packed, lines):
-    _, _, rows, blocks, _ = received_ref.shape
+def add_visits(patch_ref, received_ref, sums):
     sums[...] = jnp.zeros_like(sums)
 
     def add(v, carry):
@@ -379,8 +417,28 @@
         return carry
 
     lax.fori_loop(0, received_ref.shape[0], add, 0)
+
+
+def sum_cover(received, patch_of):
+    smem = pl.BlockSpec(memory_space=pltpu.SMEM)
+    vmem = pl.BlockSpec(memory_space=pltpu.VMEM)
+    return pl.pallas_call(
+        add_visits,
+        out_shape=jax.ShapeDtypeStruct((PATCHES,) + received.shape[1:], jnp.float32),
+        in_specs=[smem, vmem],
+        out_specs=vmem,
+        compiler_params=params(),
+        name="sum_cover",
+    )(patch_of, received)
+
+
+def combine_kernel(
+    patch_ref, wanted_ref, received_ref, cover_ref, coadd_ref, send_ref, sums, packed, lines
+):
+    _, rows, blocks, _ = received_ref.shape
+    add_visits(patch_ref, received_ref, sums)
     for p in range(PATCHES):
-        ratio = sums[p, 0] / jnp.maximum(sums[p, 1], 1.0)
+        ratio = sums[p] / jnp.maximum(cover_ref[p], 1.0)
         packed[p] = ratio.astype(jnp.bfloat16)
         lines[p] = ratio.reshape(rows * blocks, LANES)
         for h in range(blocks):
@@ -395,8 +453,8 @@
     lax.fori_loop(0, send_ref.shape[0], place, 0)
 
 
-def combine(received, patch_of, new_patch):
-    _, _, rows, blocks, _ = received.shape
+def combine(received, cover_sums, patch_of, new_patch):
+    _, rows, blocks, _ = received.shape
     smem = pl.BlockSpec(memory_space=pltpu.SMEM)
     vmem = pl.BlockSpec(memory_space=pltpu.VMEM)
     return pl.pallas_call(
@@ -405,19 +463,21 @@
             jax.ShapeDtypeStruct((PATCHES, rows, blocks * LANES), jnp.bfloat16),
             jax.ShapeDtypeStruct((new_patch.shape[0], rows, blocks, LANES), jnp.bfloat16),
         ),
-        in_specs=[smem, smem, vmem],
+        in_specs=[smem, smem, vmem, vmem],
         out_specs=(vmem, vmem),
         scratch_shapes=[
-            pltpu.VMEM((PATCHES, 2, rows, blocks, LANES), jnp.float32),
+            pltpu.VMEM((PATCHES, rows, blocks, LANES), jnp.float32),
             pltpu.VMEM((PATCHES, rows, blocks, LANES), jnp.bfloat16),
             pltpu.VMEM((PATCHES, rows * blocks, LANES), jnp.float32),
         ],
         compiler_params=params(),
         name="combine",
-    )(patch_of, new_patch, received)
-
-
-def exchange(chunks):
+    )(patch_of, new_patch, received, cover_sums)
+
+
+def exchange(lines):
+    owners = lax.axis_size("visit")
+    chunks = lines.reshape((owners, -1) + lines.shape[-2:])
     return lax.all_to_all(chunks, "visit", split_axis=0, concat_axis=0, tiled=True)
 
 
@@ -434,15 +494,21 @@
     new_coeff,
     new_patch,
 ):
-    owners = lax.axis_size("visit")
+    basis = (basis_rows.T, basis_cols.T, visit_coeff)
+    cover, early = match_first(
+        visit_image[0], good_mask[0], basis, col_offset, visit_weight
+    )
+    received_cover = exchange(cover)
     low, high = neighbours(visit_image[0], "tile")
-    visit_table, new_table = build_tables(basis_rows, basis_cols, visit_coeff, new_coeff)
-    cover = cover_rows(col_offset, visit_weight, good_mask[0])
-    outgoing = match_visit(
-        low, visit_image[0], high, cover, visit_table, col_offset, visit_weight, owners
-    )
-    received = exchange(outgoing)
-    coadd, wanted = combine(received, patch_of[:, 0], new_patch[:, 0])
+    weighted = match_second(
+        low, visit_image[0], high, cover, basis, col_offset, visit_weight, early
+    )
+    received = exchange(weighted)
+    cover_sums = sum_cover(received_cover, patch_of[:, 0])
+    new_coeff, cover_sums = lax.optimization_barrier((new_coeff, cover_sums))
+    new_table = build_table(basis_rows, basis_cols, new_coeff)
+    new_table, cover_sums = lax.optimization_barrier((new_table, cover_sums))
+    coadd, wanted = combine(received, cover_sums, patch_of[:, 0], new_patch[:, 0])
     template = exchange(wanted)
     template = template.reshape((-1,) + template.shape[2:])
     low, high = neighbours(template, "tile")

time: 133 us -> 134 us (level)
  blocking collectives: 91.9 us -> 32.3 us
  waiting for transfers between devices: 0.01 us -> 33.4 us
  starting transfers between devices: 16.5 us -> 30.9 us
  Pallas kernels: 19.5 us -> 25.9 us
  local copies, waits for them, and re-layouts: 2.54 us -> 8.3 us
    all_to_all x2 -> x1, blocking collectives: 91.9 us -> 32.3 us  [exchange(): lax.all_to_all(chunks, 'visit', split_axis=0, concat_axis=0, tiled=True)]
    all_to_all x0 -> x2, waiting for transfers between devices: none -> 32.1 us  [exchange(): lax.all_to_all(chunks, 'visit', split_axis=0, concat_axis=0, tiled=True)]
    all_to_all x0 -> x2, starting transfers between devices: none -> 17.1 us  [exchange(): lax.all_to_all(chunks, 'visit', split_axis=0, concat_axis=0, tiled=True)]
    unnamed x18 -> x34, local copies, waits for them, and re-layouts: 1.63 us -> 8.28 us
    pallas_call x3 -> x4, Pallas kernels: 10.9 us -> 17.4 us  [the longest x1 10.1 us: match_first(): pl.pallas_call(first_kernel, out_shape=(rows, rows), in_specs=[smem, smem...]
    ppermute x2, starting transfers between devices: 7.25 us -> 5.2 us  [neighbours(): high = lax.ppermute(block[:HALO], axis, backward)]
  transfers between devices with their start and end apart: 4 -> 6, of which waited for: 0 -> 4; matrix products, arithmetic and copies ran while one was open for 0% -> 0% of each run, Pallas kernels for 6% -> 9%
where the time goes in v4:
time: 134 us; the launch traced here: 133 us
  waiting for transfers between devices  33.4 us (25%)
  blocking collectives  32.3 us (24%)
  starting transfers between devices  30.9 us (23%)
  Pallas kernels  25.9 us (19%)
  local copies, waits for them, and re-layouts  8.3 us (6%)
  between operations  2.27 us (2%)
    all_to_all x1, blocking collectives, exchange(): lax.all_to_all(chunks, 'visit', split_axis=0, concat_axis=0, tiled=True)  32.3 us
    all_to_all x2, waiting for transfers between devices, exchange(): lax.all_to_all(chunks, 'visit', split_axis=0, concat_axis=0, tiled=True)  32.1 us
    all_to_all x2, starting transfers between devices, exchange(): lax.all_to_all(chunks, 'visit', split_axis=0, concat_axis=0, tiled=True)  17.1 us
    pallas_call x1, Pallas kernels, match_first(): pl.pallas_call(first_kernel, out_shape=(rows, rows), in_specs=[smem, smem...  10.1 us
    ppermute x2, starting transfers between devices, neighbours(): low = lax.ppermute(block[-HALO:], axis, forward)  8.6 us
    unnamed x34, local copies, waits for them, and re-layouts  8.28 us
    pallas_call x1, Pallas kernels, match_second(): pl.pallas_call(second_kernel, out_shape=jax.ShapeDtypeStruct(cover.shape,...  5.48 us
    ppermute x2, starting transfers between devices, neighbours(): high = lax.ppermute(block[:HALO], axis, backward)  5.2 us
  transfers between devices with their start and end apart: 6, of which 4 were waited for; matrix products, arithmetic and copies ran while one was open for 0% of the time, Pallas kernels for 9%

profile of v4, /device:TPU:1, one launch (start us, length us, event | category | flops | bytes accessed | tf_op | source)
XLA Modules:
  0.0 133.1 jit_solution(12914016696423252741)
XLA Ops:
  1.9 0.0 copy-start.3
  1.9 1.2 copy-done.3
  3.2 0.0 copy-start.7
  3.2 1.6 %copy-done.7 = s32[1,256,2048]{2,1,0:T(8,128)S(1)} copy-done((s32[1,256,2048]{2,1,0:T(8,128)S(1)}, s32[1,256,2048]{2,1,0:T(8,128)}, u32[]{:S(2)}) %copy-start.7) | copy-done | bytes 2097176
  4.7 0.0 copy-start.8
  4.7 0.7 copy-done.8
  5.4 0.0 copy-start.10
  5.5 0.7 copy-done.10
  6.2 0.0 copy-start.12
  6.2 0.7 copy-done.12
  6.8 10.1 %match_first.1 = (bf16[256,16,128]{2,1,0:T(8,128)(2,1)}, bf16[256,16,128]{2,1,0:T(8,128)(2,1)S(1)}) custom-call(s32[1]{0:T(128)S(6)} %copy.17.offset_ref, f32[1]{0:T(128)S(6)} %copy.16.weight_ref, s32[256,2048]{1,0:T(8,128)S(1)} %bitcast.29, bf16[256,2048]{1,0:T(8,128)(2,1)S(1)} %bitcast.24, f32[21,27]{1,0:T(8,128)S(1)} %bitcast.30, f32[21,27]{1,0:T(8,128)S(1)} %bitcast.33, ...), custom_call_target="tpu_custom_call" | custom-call | flops 3221225472 | bytes 8000000 | tf_op jit(solution)/shard_map/match_first/pallas_call | solution.py:246
  16.9 0.0 copy-start.15
  16.9 1.0 copy-done.15
  17.9 0.0 copy-start.4
  17.9 0.0 copy-start.9
  17.9 0.0 copy-start.11
  17.9 0.0 copy-start.13
  17.9 12.2 %all-to-all-start.1 = ((bf16[32,8,16,128]{3,2,1,0:T(8,128)(2,1)}), bf16[32,8,16,128]{3,2,1,0:T(8,128)(2,1)S(1)}, u32[]{:S(2)}, u32[]{:S(2)}) async-start(bf16[32,8,16,128]{3,2,1,0:T(8,128)(2,1)} %bitcast.9), calls=%async_computation.1 | async-start | bytes 2097152 | tf_op jit(solution)/shard_map/all_to_all | solution.py:481
  30.1 0.0 copy-done.4
  30.2 1.9 %collective-permute-start.1 = (bf16[16,2048]{1,0:T(8,128)(2,1)S(1)}, bf16[16,2048]{1,0:T(8,128)(2,1)S(1)}, u32[]{:S(2)}, u32[]{:S(2)}) collective-permute-start(bf16[16,2048]{1,0:T(8,128)(2,1)S(1)} %get-tuple-element.22), channel_id=1, source_target_pairs={{1,0},{2,1},{3,2},{4,3},{5,4},{6,5},{7,6},{9,8},{10,9},{11,10},{12... | collective-permute-start | bytes 196616 | tf_op jit(solution)/shard_map/ppermute | solution.py:31
  32.1 3.6 %collective-permute-start = (bf16[16,2048]{1,0:T(8,128)(2,1)S(1)}, bf16[16,2048]{1,0:T(8,128)(2,1)S(1)}, u32[]{:S(2)}, u32[]{:S(2)}) collective-permute-start(bf16[16,2048]{1,0:T(8,128)(2,1)S(1)} %get-tuple-element.23), channel_id=1, source_target_pairs={{0,1},{1,2},{2,3},{3,4},{4,5},{5,6},{6,7},{8,9},{9,10},{10,11},{11... | collective-permute-start | bytes 196616 | tf_op jit(solution)/shard_map/ppermute | solution.py:30
  35.7 0.3 collective-permute-done.1.high_ref
  36.0 1.0 collective-permute-done.low_ref
  37.0 0.0 copy-done.9
  37.0 0.0 copy-done.11
  37.0 0.0 copy-done.13
  37.0 0.0 copy-start.16
  37.1 1.2 copy-done.16
  38.3 5.5 %match_second.1 = bf16[256,16,128]{2,1,0:T(8,128)(2,1)} custom-call(s32[1]{0:T(128)S(6)} %copy.17.offset_ref, f32[1]{0:T(128)S(6)} %copy.16.weight_ref, bf16[16,2048]{1,0:T(8,128)(2,1)S(1)} %collective-permute-done.low_ref, bf16[256,2048]{1,0:T(8,128)(2,1)S(1)} %bitcast.25, bf16[16,2048]{1,0:T(8,128)(2,1)S(1)} %collective-permute-done.1.high_ref, ...), custom_call_target="tpu_custom_call" | custom-call | flops 3221225472 | bytes 8000000 | tf_op jit(solution)/shard_map/match_second/pallas_call | solution.py:263
  43.8 0.0 copy-start.5
  43.8 0.0 copy-start.14
  43.8 9.4 %all-to-all-done.1.received_ref = bf16[32,8,16,128]{3,2,1,0:T(8,128)(2,1)S(1)} async-done(((bf16[32,8,16,128]{3,2,1,0:T(8,128)(2,1)}), bf16[32,8,16,128]{3,2,1,0:T(8,128)(2,1)S(1)}, u32[]{:S(2)}, u32[]{:S(2)}) %all-to-all-start.1) | async-done | bytes 1048608 | tf_op jit(solution)/shard_map/all_to_all | solution.py:481
  53.2 4.9 %all-to-all-start = ((bf16[32,8,16,128]{3,2,1,0:T(8,128)(2,1)}), bf16[32,8,16,128]{3,2,1,0:T(8,128)(2,1)S(1)}, u32[]{:S(2)}, u32[]{:S(2)}) async-start(bf16[32,8,16,128]{3,2,1,0:T(8,128)(2,1)} %bitcast.8), calls=%async_computation | async-start | bytes 2097152 | tf_op jit(solution)/shard_map/all_to_all | solution.py:481
  58.1 0.0 copy-done.5
  58.1 0.9 sum_cover.1.cover_ref
  59.0 0.0 copy-done.14
  59.0 0.0 copy-start.6
  59.0 1.0 table.1.table_ref
  60.0 0.0 copy-start
  60.0 1.1 copy-done
  61.2 0.0 copy-start.2
  61.2 22.7 %all-to-all-done.received_ref = bf16[32,8,16,128]{3,2,1,0:T(8,128)(2,1)S(1)} async-done(((bf16[32,8,16,128]{3,2,1,0:T(8,128)(2,1)}), bf16[32,8,16,128]{3,2,1,0:T(8,128)(2,1)S(1)}, u32[]{:S(2)}, u32[]{:S(2)}) %all-to-all-start) | async-done | bytes 1048608 | tf_op jit(solution)/shard_map/all_to_all | solution.py:481
  83.9 0.0 copy-start.1
  83.9 0.0 copy-done.6
  83.9 2.1 %combine.1 = (bf16[8,8,2048]{2,1,0:T(8,128)(2,1)}, bf16[32,8,16,128]{3,2,1,0:T(8,128)(2,1)S(1)}) custom-call(s32[32]{0:T(128)S(1)} %bitcast.27, s32[32]{0:T(128)S(1)} %bitcast.28, bf16[32,8,16,128]{3,2,1,0:T(8,128)(2,1)S(1)} %all-to-all-done.received_ref, f32[8,8,16,128]{3,2,1,0:T(8,128)S(1)} %sum_cover.1.cover_ref), custom_call_target="tpu_custom_call" | custom-call | tf_op jit(solution)/shard_map/combine/pallas_call | solution.py:460
  85.9 32.3 %all_to_all.15 = bf16[32,8,16,128]{3,2,1,0:T(8,128)(2,1)S(1)} all-to-all(bf16[32,8,16,128]{3,2,1,0:T(8,128)(2,1)S(1)} %get-tuple-element.16), channel_id=1, replica_groups=mesh['visit'=32,'tile'=8] {'visit'}, dimensions={0} | all-to-all | bytes 2097152 | tf_op jit(solution)/shard_map/all_to_all | solution.py:481
  118.2 5.0 %collective-permute-start.2 = (bf16[16,16,128]{2,1,0:T(8,128)(2,1)S(1)}, bf16[16,16,128]{2,1,0:T(8,128)(2,1)S(1)}, u32[]{:S(2)}, u32[]{:S(2)}) collective-permute-start(bf16[16,16,128]{2,1,0:T(8,128)(2,1)S(1)} %bitcast.38), channel_id=1, source_target_pairs={{0,1},{1,2},{2,3},{3,4},{4,5},{5,6},{6,7},{8,9},{9,10},{10,11},{11... | collective-permute-start | bytes 196616 | tf_op jit(solution)/shard_map/ppermute | solution.py:30
  123.2 3.3 %collective-permute-start.3 = (bf16[16,16,128]{2,1,0:T(8,128)(2,1)S(1)}, bf16[16,16,128]{2,1,0:T(8,128)(2,1)S(1)}, u32[]{:S(2)}, u32[]{:S(2)}) collective-permute-start(bf16[16,16,128]{2,1,0:T(8,128)(2,1)S(1)} %bitcast.37), channel_id=1, source_target_pairs={{1,0},{2,1},{3,2},{4,3},{5,4},{6,5},{7,6},{9,8},{10,9},{11,10},{12... | collective-permute-start | bytes 196616 | tf_op jit(solution)/shard_map/ppermute | solution.py:31
  126.5 0.0 copy-done.2
  126.5 0.0 copy-done.1
  126.5 4.9 %subtract_interior.1._ = f32[256,2048]{1,0:T(8,128)} custom-call(bf16[256,16,128]{2,1,0:T(8,128)(2,1)S(1)} %bitcast.20, bf16[256,2048]{1,0:T(8,128)(2,1)S(1)} %bitcast.22, bf16[3072,256]{1,0:T(8,128)(2,1)S(1)} %copy-done.1), custom_call_target="tpu_custom_call" | custom-call | flops 3221225472 | bytes 8000000 | tf_op jit(solution)/shard_map/subtract_interior/pallas_call | solution.py:335
  131.4 0.0 collective-permute-done.2.low_ref
  131.4 0.0 collective-permute-done.3.high_ref
  131.4 1.5 %subtract_edges.1 = f32[256,2048]{1,0:T(8,128)} custom-call(bf16[16,16,128]{2,1,0:T(8,128)(2,1)S(1)} %collective-permute-done.2.low_ref, bf16[256,16,128]{2,1,0:T(8,128)(2,1)S(1)} %bitcast.21, bf16[16,16,128]{2,1,0:T(8,128)(2,1)S(1)} %collective-permute-done.3.high_ref, bf16[256,2048]{1,0:T(8,128)(2,1)S(1)} %bitcast.23, ...), custom_call_target="tpu_custom_call", output_to_operand_aliasing={{}: (5, {})} | custom-call | flops 402653184 | bytes 8000000 | tf_op jit(solution)/shard_map/subtract_edges/pallas_call | solution.py:392
  (2 shorter events, 0.0 us)
Async XLA Ops:
  1.9 1.2 copy-start.3
  3.2 1.6 %copy-start.7 = (s32[1,256,2048]{2,1,0:T(8,128)S(1)}, s32[1,256,2048]{2,1,0:T(8,128)}, u32[]{:S(2)}) copy-start(s32[1,256,2048]{2,1,0:T(8,128)} %param.12) | copy-start | bytes 6291460
  4.7 0.7 copy-start.8
  5.4 0.7 copy-start.10
  6.2 0.7 copy-start.12
  16.9 1.0 copy-start.15
  17.9 12.2 %copy-start.4 = (bf16[1,256,2048]{2,1,0:T(8,128)(2,1)S(1)}, bf16[1,256,2048]{2,1,0:T(8,128)(2,1)}, u32[]{:S(2)}) copy-start(bf16[1,256,2048]{2,1,0:T(8,128)(2,1)} %param.11) | copy-start | bytes 3145732
  17.9 19.1 %copy-start.9 = (f32[27,21]{0,1:T(8,128)S(1)}, f32[27,21]{0,1:T(8,128)}, u32[]{:S(2)}) copy-start(f32[27,21]{0,1:T(8,128)} %param.13) | copy-start | bytes 6808
  17.9 19.1 %copy-start.11 = (f32[27,21]{0,1:T(8,128)S(1)}, f32[27,21]{0,1:T(8,128)}, u32[]{:S(2)}) copy-start(f32[27,21]{0,1:T(8,128)} %param.14) | copy-start | bytes 6808
  17.9 19.1 %copy-start.13 = (f32[1,27]{1,0:T(1,128)S(1)}, f32[1,27]{1,0:T(1,128)}, u32[]{:S(2)}) copy-start(f32[1,27]{1,0:T(1,128)} %coeff_ref.3) | copy-start | bytes 328
  17.9 35.2 %all-to-all-start.1 = ((bf16[32,8,16,128]{3,2,1,0:T(8,128)(2,1)}), bf16[32,8,16,128]{3,2,1,0:T(8,128)(2,1)S(1)}, u32[]{:S(2)}, u32[]{:S(2)}) async-start(bf16[32,8,16,128]{3,2,1,0:T(8,128)(2,1)} %bitcast.9), calls=%async_computation.1 | async-start | bytes 2097152 | tf_op jit(solution)/shard_map/all_to_all | solution.py:481
  30.2 5.9 %collective-permute-start.1 = (bf16[16,2048]{1,0:T(8,128)(2,1)S(1)}, bf16[16,2048]{1,0:T(8,128)(2,1)S(1)}, u32[]{:S(2)}, u32[]{:S(2)}) collective-permute-start(bf16[16,2048]{1,0:T(8,128)(2,1)S(1)} %get-tuple-element.22), channel_id=1, source_target_pairs={{1,0},{2,1},{3,2},{4,3},{5,4},{6,5},{7,6},{9,8},{10,9},{11,10},{12... | collective-permute-start | bytes 196616 | tf_op jit(solution)/shard_map/ppermute | solution.py:31
  32.1 5.0 %collective-permute-start = (bf16[16,2048]{1,0:T(8,128)(2,1)S(1)}, bf16[16,2048]{1,0:T(8,128)(2,1)S(1)}, u32[]{:S(2)}, u32[]{:S(2)}) collective-permute-start(bf16[16,2048]{1,0:T(8,128)(2,1)S(1)} %get-tuple-element.23), channel_id=1, source_target_pairs={{0,1},{1,2},{2,3},{3,4},{4,5},{5,6},{6,7},{8,9},{9,10},{10,11},{11... | collective-permute-start | bytes 196616 | tf_op jit(solution)/shard_map/ppermute | solution.py:30
  37.0 1.2 copy-start.16
  43.8 14.4 %copy-start.5 = (s32[32,1]{0,1:T(1,128)S(1)}, s32[32,1]{0,1:T(1,128)}, u32[]{:S(2)}) copy-start(s32[32,1]{0,1:T(1,128)} %param.18) | copy-start | bytes 388
  43.8 15.3 %copy-start.14 = (f32[1,27]{1,0:T(1,128)S(1)}, f32[1,27]{1,0:T(1,128)}, u32[]{:S(2)}) copy-start(f32[1,27]{1,0:T(1,128)} %coeff_ref.4) | copy-start | bytes 328
  53.2 30.7 %all-to-all-start = ((bf16[32,8,16,128]{3,2,1,0:T(8,128)(2,1)}), bf16[32,8,16,128]{3,2,1,0:T(8,128)(2,1)S(1)}, u32[]{:S(2)}, u32[]{:S(2)}) async-start(bf16[32,8,16,128]{3,2,1,0:T(8,128)(2,1)} %bitcast.8), calls=%async_computation | async-start | bytes 2097152 | tf_op jit(solution)/shard_map/all_to_all | solution.py:481
  59.0 24.8 %copy-start.6 = (s32[32,1]{0,1:T(1,128)S(1)}, s32[32,1]{0,1:T(1,128)}, u32[]{:S(2)}) copy-start(s32[32,1]{0,1:T(1,128)} %param.21) | copy-start | bytes 388
  60.0 1.1 copy-start
  61.2 65.3 %copy-start.2 = (bf16[1,256,2048]{2,1,0:T(8,128)(2,1)S(1)}, bf16[1,256,2048]{2,1,0:T(8,128)(2,1)}, u32[]{:S(2)}) copy-start(bf16[1,256,2048]{2,1,0:T(8,128)(2,1)} %param.19) | copy-start | bytes 3145732
  83.9 42.6 %copy-start.1 = (bf16[3072,256]{1,0:T(8,128)(2,1)S(1)}, bf16[3072,256]{1,0:T(8,128)(2,1)}, u32[]{:S(2)}) copy-start(bf16[3072,256]{1,0:T(8,128)(2,1)} %copy-done) | copy-start | bytes 4718596
  118.2 13.2 %collective-permute-start.2 = (bf16[16,16,128]{2,1,0:T(8,128)(2,1)S(1)}, bf16[16,16,128]{2,1,0:T(8,128)(2,1)S(1)}, u32[]{:S(2)}, u32[]{:S(2)}) collective-permute-start(bf16[16,16,128]{2,1,0:T(8,128)(2,1)S(1)} %bitcast.38), channel_id=1, source_target_pairs={{0,1},{1,2},{2,3},{3,4},{4,5},{5,6},{6,7},{8,9},{9,10},{10,11},{11... | collective-permute-start | bytes 196616 | tf_op jit(solution)/shard_map/ppermute | solution.py:30
  123.2 8.2 %collective-permute-start.3 = (bf16[16,16,128]{2,1,0:T(8,128)(2,1)S(1)}, bf16[16,16,128]{2,1,0:T(8,128)(2,1)S(1)}, u32[]{:S(2)}, u32[]{:S(2)}) collective-permute-start(bf16[16,16,128]{2,1,0:T(8,128)(2,1)S(1)} %bitcast.37), channel_id=1, source_target_pairs={{1,0},{2,1},{3,2},{4,3},{5,4},{6,5},{7,6},{9,8},{10,9},{11,10},{12... | collective-permute-start | bytes 196616 | tf_op jit(solution)/shard_map/ppermute | solution.py:31

commit v5 on v4

--- a/solution.py
+++ b/solution.py
@@ -1,3 +1,5 @@
+import functools
+
 import jax
 import jax.numpy as jnp
 from jax import lax
@@ -13,6 +15,7 @@
 QUAD = 4
 SPLIT = LANES // 2
 SHIFTS = QUAD + KS - 1
+CHUNK = 64
 PARTS = 4
 UNIT = 16
 PAD = 8
@@ -137,32 +140,59 @@
     )
 
 
-def match_interior(mid_ref, cover_ref, table_ref, shift, weight, out_ref, windows, lines):
-    height = mid_ref.shape[0]
-    rows = (height - 2 * HALO) // PARTS
-    done = 0
-    for part in range(PARTS):
-        first = HALO + part * rows
-        needed = min(-(-(first + rows + HALF + 1) // UNIT), height // UNIT)
-        for u in range(done, needed):
-            lay_out_unit(mid_ref, u * UNIT, shift, lines[u % len(lines)], windows, u + 1)
-        done = needed
-
-        def write(k, e, line, first=first):
-            r = first + QUAD * k + e
-            good = cover_ref[r].astype(jnp.float32) > 0
-            out_ref[r] = (line * jnp.where(good, weight, 0.0)).astype(jnp.bfloat16)
-
-        multiply(windows, [(first // QUAD, rows // QUAD)], table_ref, write)
-
-
-def late_group():
-    return lax.axis_index("tile") % 2 == 1
-
-
-def first_kernel(
-    offset_ref, weight_ref, mask_ref, mid_ref, rows_ref, cols_ref, coeff_ref, cover_ref, out_ref, windows, table_ref, *lines
-):
+def match_kernel(turn, *refs):
+    offset_ref, weight_ref = refs[:2]
+    operands = refs[2:9]
+    out_ref, windows, table_ref, result, sems, *rest = refs[9 if turn == 0 else 10 :]
+    held, lines = rest[:7], rest[7:]
+
+    @pl.when(lax.axis_index("tile") % 2 == 1 - turn)
+    def _():
+        copies = [
+            pltpu.make_async_copy(source, target, sems.at[i])
+            for i, (source, target) in enumerate(zip(operands, held))
+        ]
+        for copy in copies:
+            copy.start()
+        for copy in copies:
+            copy.wait()
+        low, mid, high, cover, rows, cols, coeff = held
+        fill_table(rows, cols, coeff, table_ref)
+        height = mid.shape[0]
+        weight = weight_ref[0]
+        shift = offset_ref[0] + HALF
+        units = height // UNIT + 2
+        done = 0
+        copies = []
+        for first in range(0, height, CHUNK):
+            needed = min((first + CHUNK + 2 * HALO) // UNIT, units)
+            for u in range(done, needed):
+                if u == 0:
+                    source, at = low, 0
+                elif u == units - 1:
+                    source, at = high, 0
+                else:
+                    source, at = mid, (u - 1) * UNIT
+                lay_out_unit(source, at, shift, lines[u % len(lines)], windows, u)
+            done = needed
+
+            def write(k, e, line, first=first):
+                r = first + QUAD * k + e
+                good = cover[r].astype(jnp.float32) > 0
+                result[r] = (line * jnp.where(good, weight, 0.0)).astype(jnp.bfloat16)
+
+            multiply(windows, [(first // QUAD, CHUNK // QUAD)], table_ref, write)
+            part = pl.ds(first, CHUNK)
+            copy = pltpu.make_async_copy(
+                result.at[part], out_ref.at[part], sems.at[first // CHUNK]
+            )
+            copy.start()
+            copies.append(copy)
+        for copy in copies:
+            copy.wait()
+
+
+def cover_kernel(offset_ref, weight_ref, mask_ref, out_ref, *lines):
     height, columns = mask_ref.shape
     blocks = columns // LANES
     weight = weight_ref[0]
@@ -170,52 +200,26 @@
         spot = lines[u % len(lines)]
         rows = slice(u * UNIT, (u + 1) * UNIT)
         good = [mask_ref[rows, lanes_of(h)].astype(jnp.float32) * weight for h in range(blocks)]
-        lay_out(good, offset_ref[0], spot, PAD, 4 * blocks)
-        tiles = spot[...].reshape(UNIT, 4 * blocks, LANES)
-        cover_ref[rows] = tiles[:, PAD : PAD + blocks].astype(jnp.bfloat16)
-
-    @pl.when(late_group())
-    def _():
-        fill_table(rows_ref, cols_ref, coeff_ref, table_ref)
-        shift = offset_ref[0] + HALF
-        match_interior(mid_ref, cover_ref, table_ref, shift, weight, out_ref, windows, lines)
-
-
-def second_kernel(
-    offset_ref, weight_ref, low_ref, mid_ref, high_ref, cover_ref, rows_ref, cols_ref, coeff_ref, early_ref, out_ref, windows, table_ref, *lines
-):
-    height = mid_ref.shape[0]
-    weight = weight_ref[0]
-    shift = offset_ref[0] + HALF
-    late = late_group()
-    fill_table(rows_ref, cols_ref, coeff_ref, table_ref)
-
-    @pl.when(late)
-    def _():
-        out_ref[HALO : height - HALO] = early_ref[HALO : height - HALO]
-
-    @pl.when(jnp.logical_not(late))
-    def _():
-        match_interior(mid_ref, cover_ref, table_ref, shift, weight, out_ref, windows, lines)
-
-    sources = [
-        (low_ref, 0),
-        (mid_ref, 0),
-        (mid_ref, UNIT),
-        (mid_ref, height - 2 * UNIT),
-        (mid_ref, height - UNIT),
-        (high_ref, 0),
-    ]
-    for u, (source, first) in enumerate(sources):
-        lay_out_unit(source, first, shift, lines[u % len(lines)], windows, u)
-    each = HALO // QUAD
-
-    def write(k, e, line):
-        r = QUAD * k + e + (0 if k < each else height - 2 * HALO)
-        good = cover_ref[r].astype(jnp.float32) > 0
-        out_ref[r] = (line * jnp.where(good, weight, 0.0)).astype(jnp.bfloat16)
-
-    multiply(windows, [(0, each), (3 * UNIT // QUAD, each)], table_ref, write)
+        lay_out(good, offset_ref[0], spot, PAD, 2 * blocks)
+        tiles = spot[...].reshape(UNIT, 2 * blocks, LANES)
+        out_ref[rows] = tiles[:, PAD : PAD + blocks].astype(jnp.bfloat16)
+
+
+def cover_rows(offset, weight, mask):
+    height, columns = mask.shape
+    blocks = columns // LANES
+    smem = pl.BlockSpec(memory_space=pltpu.SMEM)
+    vmem = pl.BlockSpec(memory_space=pltpu.VMEM)
+    return pl.pallas_call(
+        cover_kernel,
+        out_shape=jax.ShapeDtypeStruct((height, blocks, LANES), jnp.bfloat16),
+        in_specs=[smem, smem, vmem],
+        out_specs=vmem,
+        scratch_shapes=[pltpu.VMEM((UNIT * 2 * blocks, LANES), jnp.float32)] * 4,
+        compiler_params=params(),
+        cost_estimate=pl.CostEstimate(flops=10**6, bytes_accessed=6 * 10**6, transcendentals=0),
+        name="cover_rows",
+    )(offset, weight, mask)
 
 
 def window_scratch(height, blocks):
@@ -228,48 +232,30 @@
     )
 
 
-def visit_scratch(height, blocks):
-    return [
-        window_scratch(height + 2 * HALO, blocks),
-        pltpu.VMEM((SHIFTS * LANES, QUAD * SPLIT), jnp.bfloat16),
-    ] + [
-        pltpu.VMEM((UNIT * 4 * blocks, LANES), jnp.float32)
-    ] * 4
-
-
-def match_first(mid, mask, basis, offset, weight):
-    height, columns = mid.shape
+def match_visit(turn, offset, weight, operands, *before):
+    height, columns = operands[1].shape
     blocks = columns // LANES
     smem = pl.BlockSpec(memory_space=pltpu.SMEM)
-    vmem = pl.BlockSpec(memory_space=pltpu.VMEM)
-    rows = jax.ShapeDtypeStruct((height, blocks, LANES), jnp.bfloat16)
-    return pl.pallas_call(
-        first_kernel,
-        out_shape=(rows, rows),
-        in_specs=[smem, smem] + [vmem] * 5,
-        out_specs=(vmem, vmem),
-        scratch_shapes=visit_scratch(height, blocks),
-        compiler_params=params(),
+    anywhere = pl.BlockSpec(memory_space=pl.ANY)
+    rows = (height, blocks, LANES)
+    return pl.pallas_call(
+        functools.partial(match_kernel, turn),
+        out_shape=jax.ShapeDtypeStruct(rows, jnp.bfloat16),
+        in_specs=[smem, smem] + [anywhere] * (len(operands) + len(before)),
+        out_specs=anywhere,
+        input_output_aliases={9: 0} if before else {},
+        scratch_shapes=[
+            window_scratch(height + 2 * HALO, blocks),
+            pltpu.VMEM((SHIFTS * LANES, QUAD * SPLIT), jnp.bfloat16),
+            pltpu.VMEM(rows, jnp.bfloat16),
+            pltpu.SemaphoreType.DMA((len(operands),)),
+        ]
+        + [pltpu.VMEM(a.shape, a.dtype) for a in operands]
+        + [pltpu.VMEM((UNIT * 4 * blocks, LANES), jnp.float32)] * 4,
+        compiler_params=pltpu.CompilerParams(vmem_limit_bytes=56 * 2**20),
         cost_estimate=conv_cost(height, columns),
-        name="match_first",
-    )(offset, weight, mask, mid, *basis)
-
-
-def match_second(low, mid, high, cover, basis, offset, weight, early):
-    height, columns = mid.shape
-    blocks = columns // LANES
-    smem = pl.BlockSpec(memory_space=pltpu.SMEM)
-    vmem = pl.BlockSpec(memory_space=pltpu.VMEM)
-    return pl.pallas_call(
-        second_kernel,
-        out_shape=jax.ShapeDtypeStruct(cover.shape, jnp.bfloat16),
-        in_specs=[smem, smem] + [vmem] * 8,
-        out_specs=vmem,
-        scratch_shapes=visit_scratch(height, blocks),
-        compiler_params=params(),
-        cost_estimate=conv_cost(height, columns),
-        name="match_second",
-    )(offset, weight, low, mid, high, cover, *basis, early)
+        name="match_visit",
+    )(offset, weight, *operands, *before)
 
 
 def fill_windows(source, first, padded, windows, unit):
@@ -494,15 +480,13 @@
     new_coeff,
     new_patch,
 ):
-    basis = (basis_rows.T, basis_cols.T, visit_coeff)
-    cover, early = match_first(
-        visit_image[0], good_mask[0], basis, col_offset, visit_weight
-    )
+    low, high = neighbours(visit_image[0], "tile")
+    cover = cover_rows(col_offset, visit_weight, good_mask[0])
+    operands = (low, visit_image[0], high, cover, basis_rows.T, basis_cols.T, visit_coeff)
+    weighted = match_visit(0, col_offset, visit_weight, operands)
+    cover, weighted = lax.optimization_barrier((cover, weighted))
     received_cover = exchange(cover)
-    low, high = neighbours(visit_image[0], "tile")
-    weighted = match_second(
-        low, visit_image[0], high, cover, basis, col_offset, visit_weight, early
-    )
+    weighted = match_visit(1, col_offset, visit_weight, operands, weighted)
     received = exchange(weighted)
     cover_sums = sum_cover(received_cover, patch_of[:, 0])
     new_coeff, cover_sums = lax.optimization_barrier((new_coeff, cover_sums))

time: 134 us -> 125 us (0.933)
  the two profiles are of different devices: /device:TPU:1 before, /device:TPU:7 now
where the time goes in v5:
time: 125 us; the launch traced here: 124 us
  waiting for transfers between devices  38.8 us (31%)
  blocking collectives  30 us (24%)
  starting transfers between devices  24.5 us (20%)
  Pallas kernels  24 us (19%)
  local copies, waits for them, and re-layouts  4.29 us (3%)
  between operations  2.31 us (2%)
    all_to_all x2, waiting for transfers between devices, exchange(): lax.all_to_all(chunks, 'visit', split_axis=0, concat_axis=0, tiled=True)  38.8 us
    all_to_all x1, blocking collectives, exchange(): lax.all_to_all(chunks, 'visit', split_axis=0, concat_axis=0, tiled=True)  30 us
    all_to_all x2, starting transfers between devices, exchange(): lax.all_to_all(chunks, 'visit', split_axis=0, concat_axis=0, tiled=True)  16.3 us
    pallas_call x2, Pallas kernels, match_visit(): pl.pallas_call(functools.partial(match_kernel, turn), out_shape=jax.Shape...  10.8 us
    ppermute x2, starting transfers between devices, neighbours(): high = lax.ppermute(block[:HALO], axis, backward)  5.62 us
    pallas_call x1, Pallas kernels, subtract_interior(): pl.pallas_call(interior_kernel, out_shape=jax.ShapeDtypeStruct(new.shape,...  4.9 us
    unnamed x22, local copies, waits for them, and re-layouts  3.4 us
    pallas_call x1, Pallas kernels, cover_rows(): pl.pallas_call(cover_kernel, out_shape=jax.ShapeDtypeStruct((height, bloc...  2.91 us
  transfers between devices with their start and end apart: 6, of which 2 were waited for; matrix products, arithmetic and copies ran while one was open for 0% of the time, Pallas kernels for 8%

profile of v5, /device:TPU:7, one launch (start us, length us, event | category | flops | bytes accessed | tf_op | source)
XLA Modules:
  0.0 124.0 jit_solution(444314511510468843)
XLA Ops:
  0.6 0.9 slice_bitcast_fusion
  1.5 2.6 %collective-permute-start.1 = (bf16[16,2048]{1,0:T(8,128)(2,1)S(1)}, bf16[16,2048]{1,0:T(8,128)(2,1)S(1)}, u32[]{:S(2)}, u32[]{:S(2)}) collective-permute-start(bf16[16,2048]{1,0:T(8,128)(2,1)S(1)} %get-tuple-element.22), channel_id=1, source_target_pairs={{1,0},{2,1},{3,2},{4,3},{5,4},{6,5},{7,6},{9,8},{10,9},{11,10},{12... | collective-permute-start | bytes 196616 | tf_op jit(solution)/shard_map/ppermute | solution.py:34
  4.1 1.3 %collective-permute-start = (bf16[16,2048]{1,0:T(8,128)(2,1)S(1)}, bf16[16,2048]{1,0:T(8,128)(2,1)S(1)}, u32[]{:S(2)}, u32[]{:S(2)}) collective-permute-start(bf16[16,2048]{1,0:T(8,128)(2,1)S(1)} %get-tuple-element.23), channel_id=1, source_target_pairs={{0,1},{1,2},{2,3},{3,4},{4,5},{5,6},{6,7},{8,9},{9,10},{10,11},{11... | collective-permute-start | bytes 196616 | tf_op jit(solution)/shard_map/ppermute | solution.py:33
  6.7 0.0 copy-start
  6.7 1.6 %copy-done = s32[1,256,2048]{2,1,0:T(8,128)S(1)} copy-done((s32[1,256,2048]{2,1,0:T(8,128)S(1)}, s32[1,256,2048]{2,1,0:T(8,128)}, u32[]{:S(2)}) %copy-start) | copy-done | bytes 2097176
  8.3 2.9 %cover_rows.1.refs_5_ = bf16[256,16,128]{2,1,0:T(8,128)(2,1)} custom-call(s32[1]{0:T(128)S(6)} %copy.19.offset_ref.refs_0_, f32[1]{0:T(128)S(6)} %copy.18.weight_ref.refs_1_, s32[256,2048]{1,0:T(8,128)S(1)} %bitcast.22), custom_call_target="tpu_custom_call" | custom-call | flops 1000000 | bytes 6000000 | tf_op jit(solution)/shard_map/cover_rows/pallas_call | solution.py:213
  11.2 0.0 collective-permute-done.1.refs_4_
  11.2 0.0 copy-start.9
  11.2 0.0 collective-permute-done.refs_2_
  11.2 0.0 copy-start.10
  11.2 0.6 copy-done.9
  11.8 0.0 copy-done.10
  11.9 10.5 %match_visit.2.refs_9_ = bf16[256,16,128]{2,1,0:T(8,128)(2,1)} custom-call(s32[1]{0:T(128)S(6)} %copy.19.offset_ref.refs_0_, f32[1]{0:T(128)S(6)} %copy.18.weight_ref.refs_1_, bf16[16,2048]{1,0:T(8,128)(2,1)} %copy-done.10, bf16[256,2048]{1,0:T(8,128)(2,1)} %bitcast.38, bf16[16,2048]{1,0:T(8,128)(2,1)} %copy-done.9, ...), custom_call_target="tpu_custom_call" | custom-call | flops 3221225472 | bytes 8000000 | tf_op jit(solution)/shard_map/match_visit/pallas_call | solution.py:241
  22.4 11.2 %all-to-all-start.1 = ((bf16[32,8,16,128]{3,2,1,0:T(8,128)(2,1)}), bf16[32,8,16,128]{3,2,1,0:T(8,128)(2,1)S(1)}, u32[]{:S(2)}, u32[]{:S(2)}) async-start(bf16[32,8,16,128]{3,2,1,0:T(8,128)(2,1)} %bitcast.9), calls=%async_computation.1 | async-start | bytes 2097152 | tf_op jit(solution)/shard_map/all_to_all | solution.py:467
  33.6 0.3 match_visit.3
  33.9 0.0 copy-start.4
  33.9 0.0 copy-start.6
  33.9 0.0 copy-start.7
  33.9 0.0 copy-start.8
  34.0 19.6 %all-to-all-done.1.received_ref = bf16[32,8,16,128]{3,2,1,0:T(8,128)(2,1)S(1)} async-done(((bf16[32,8,16,128]{3,2,1,0:T(8,128)(2,1)}), bf16[32,8,16,128]{3,2,1,0:T(8,128)(2,1)S(1)}, u32[]{:S(2)}, u32[]{:S(2)}) %all-to-all-start.1) | async-done | bytes 1048608 | tf_op jit(solution)/shard_map/all_to_all | solution.py:467
  53.6 5.1 %all-to-all-start = ((bf16[32,8,16,128]{3,2,1,0:T(8,128)(2,1)}), bf16[32,8,16,128]{3,2,1,0:T(8,128)(2,1)S(1)}, u32[]{:S(2)}, u32[]{:S(2)}) async-start(bf16[32,8,16,128]{3,2,1,0:T(8,128)(2,1)} %bitcast.35), calls=%async_computation | async-start | bytes 2097152 | tf_op jit(solution)/shard_map/all_to_all | solution.py:467
  58.7 0.0 copy-done.4
  58.7 0.9 sum_cover.1.cover_ref
  59.6 0.0 copy-done.6
  59.6 0.0 copy-done.7
  59.7 0.0 copy-done.8
  59.7 0.0 copy-start.5
  59.7 1.0 table.1.table_ref
  60.6 0.0 copy-start.1
  60.7 1.1 copy-done.1
  61.8 0.0 copy-start.3
  61.8 19.2 %all-to-all-done.received_ref = bf16[32,8,16,128]{3,2,1,0:T(8,128)(2,1)S(1)} async-done(((bf16[32,8,16,128]{3,2,1,0:T(8,128)(2,1)}), bf16[32,8,16,128]{3,2,1,0:T(8,128)(2,1)S(1)}, u32[]{:S(2)}, u32[]{:S(2)}) %all-to-all-start) | async-done | bytes 1048608 | tf_op jit(solution)/shard_map/all_to_all | solution.py:467
  81.0 0.0 copy-start.2
  81.0 0.0 copy-done.5
  81.0 2.1 %combine.1 = (bf16[8,8,2048]{2,1,0:T(8,128)(2,1)}, bf16[32,8,16,128]{3,2,1,0:T(8,128)(2,1)S(1)}) custom-call(s32[32]{0:T(128)S(1)} %bitcast.26, s32[32]{0:T(128)S(1)} %bitcast.27, bf16[32,8,16,128]{3,2,1,0:T(8,128)(2,1)S(1)} %all-to-all-done.received_ref, f32[8,8,16,128]{3,2,1,0:T(8,128)S(1)} %sum_cover.1.cover_ref), custom_call_target="tpu_custom_call" | custom-call | tf_op jit(solution)/shard_map/combine/pallas_call | solution.py:446
  83.0 30.0 %all_to_all.15 = bf16[32,8,16,128]{3,2,1,0:T(8,128)(2,1)S(1)} all-to-all(bf16[32,8,16,128]{3,2,1,0:T(8,128)(2,1)S(1)} %get-tuple-element.16), channel_id=1, replica_groups=mesh['visit'=32,'tile'=8] {'visit'}, dimensions={0} | all-to-all | bytes 2097152 | tf_op jit(solution)/shard_map/all_to_all | solution.py:467
  113.0 1.3 %collective-permute-start.2 = (bf16[16,16,128]{2,1,0:T(8,128)(2,1)S(1)}, bf16[16,16,128]{2,1,0:T(8,128)(2,1)S(1)}, u32[]{:S(2)}, u32[]{:S(2)}) collective-permute-start(bf16[16,16,128]{2,1,0:T(8,128)(2,1)S(1)} %bitcast.37), channel_id=1, source_target_pairs={{0,1},{1,2},{2,3},{3,4},{4,5},{5,6},{6,7},{8,9},{9,10},{10,11},{11... | collective-permute-start | bytes 196616 | tf_op jit(solution)/shard_map/ppermute | solution.py:33
  114.3 3.0 %collective-permute-start.3 = (bf16[16,16,128]{2,1,0:T(8,128)(2,1)S(1)}, bf16[16,16,128]{2,1,0:T(8,128)(2,1)S(1)}, u32[]{:S(2)}, u32[]{:S(2)}) collective-permute-start(bf16[16,16,128]{2,1,0:T(8,128)(2,1)S(1)} %bitcast.36), channel_id=1, source_target_pairs={{1,0},{2,1},{3,2},{4,3},{5,4},{6,5},{7,6},{9,8},{10,9},{11,10},{12... | collective-permute-start | bytes 196616 | tf_op jit(solution)/shard_map/ppermute | solution.py:34
  117.4 0.0 copy-done.3
  117.4 0.0 copy-done.2
  117.4 4.9 %subtract_interior.1._ = f32[256,2048]{1,0:T(8,128)} custom-call(bf16[256,16,128]{2,1,0:T(8,128)(2,1)S(1)} %bitcast.20, bf16[256,2048]{1,0:T(8,128)(2,1)S(1)} %bitcast.23, bf16[3072,256]{1,0:T(8,128)(2,1)S(1)} %copy-done.2), custom_call_target="tpu_custom_call" | custom-call | flops 3221225472 | bytes 8000000 | tf_op jit(solution)/shard_map/subtract_interior/pallas_call | solution.py:321
  122.3 0.0 collective-permute-done.2.low_ref
  122.3 0.0 collective-permute-done.3.high_ref
  122.3 1.5 %subtract_edges.1 = f32[256,2048]{1,0:T(8,128)} custom-call(bf16[16,16,128]{2,1,0:T(8,128)(2,1)S(1)} %collective-permute-done.2.low_ref, bf16[256,16,128]{2,1,0:T(8,128)(2,1)S(1)} %bitcast.21, bf16[16,16,128]{2,1,0:T(8,128)(2,1)S(1)} %collective-permute-done.3.high_ref, bf16[256,2048]{1,0:T(8,128)(2,1)S(1)} %bitcast.24, ...), custom_call_target="tpu_custom_call", output_to_operand_aliasing={{}: (5, {})} | custom-call | flops 402653184 | bytes 8000000 | tf_op jit(solution)/shard_map/subtract_edges/pallas_call | solution.py:378
  (1 shorter events, 0.0 us)
Async XLA Ops:
  1.5 9.7 %collective-permute-start.1 = (bf16[16,2048]{1,0:T(8,128)(2,1)S(1)}, bf16[16,2048]{1,0:T(8,128)(2,1)S(1)}, u32[]{:S(2)}, u32[]{:S(2)}) collective-permute-start(bf16[16,2048]{1,0:T(8,128)(2,1)S(1)} %get-tuple-element.22), channel_id=1, source_target_pairs={{1,0},{2,1},{3,2},{4,3},{5,4},{6,5},{7,6},{9,8},{10,9},{11,10},{12... | collective-permute-start | bytes 196616 | tf_op jit(solution)/shard_map/ppermute | solution.py:34
  4.1 7.1 %collective-permute-start = (bf16[16,2048]{1,0:T(8,128)(2,1)S(1)}, bf16[16,2048]{1,0:T(8,128)(2,1)S(1)}, u32[]{:S(2)}, u32[]{:S(2)}) collective-permute-start(bf16[16,2048]{1,0:T(8,128)(2,1)S(1)} %get-tuple-element.23), channel_id=1, source_target_pairs={{0,1},{1,2},{2,3},{3,4},{4,5},{5,6},{6,7},{8,9},{9,10},{10,11},{11... | collective-permute-start | bytes 196616 | tf_op jit(solution)/shard_map/ppermute | solution.py:33
  6.7 1.6 %copy-start = (s32[1,256,2048]{2,1,0:T(8,128)S(1)}, s32[1,256,2048]{2,1,0:T(8,128)}, u32[]{:S(2)}) copy-start(s32[1,256,2048]{2,1,0:T(8,128)} %param.12) | copy-start | bytes 6291460
  11.2 0.6 copy-start.9
  11.2 0.6 copy-start.10
  22.4 31.2 %all-to-all-start.1 = ((bf16[32,8,16,128]{3,2,1,0:T(8,128)(2,1)}), bf16[32,8,16,128]{3,2,1,0:T(8,128)(2,1)S(1)}, u32[]{:S(2)}, u32[]{:S(2)}) async-start(bf16[32,8,16,128]{3,2,1,0:T(8,128)(2,1)} %bitcast.9), calls=%async_computation.1 | async-start | bytes 2097152 | tf_op jit(solution)/shard_map/all_to_all | solution.py:467
  33.9 24.8 %copy-start.4 = (s32[32,1]{0,1:T(1,128)S(1)}, s32[32,1]{0,1:T(1,128)}, u32[]{:S(2)}) copy-start(s32[32,1]{0,1:T(1,128)} %param.18) | copy-start | bytes 388
  33.9 25.7 %copy-start.6 = (f32[27,21]{0,1:T(8,128)S(1)}, f32[27,21]{0,1:T(8,128)}, u32[]{:S(2)}) copy-start(f32[27,21]{0,1:T(8,128)} %param.13) | copy-start | bytes 6808
  33.9 25.7 %copy-start.7 = (f32[27,21]{0,1:T(8,128)S(1)}, f32[27,21]{0,1:T(8,128)}, u32[]{:S(2)}) copy-start(f32[27,21]{0,1:T(8,128)} %param.14) | copy-start | bytes 6808
  33.9 25.7 %copy-start.8 = (f32[1,27]{1,0:T(1,128)S(1)}, f32[1,27]{1,0:T(1,128)}, u32[]{:S(2)}) copy-start(f32[1,27]{1,0:T(1,128)} %coeff_ref) | copy-start | bytes 328
  53.6 27.4 %all-to-all-start = ((bf16[32,8,16,128]{3,2,1,0:T(8,128)(2,1)}), bf16[32,8,16,128]{3,2,1,0:T(8,128)(2,1)S(1)}, u32[]{:S(2)}, u32[]{:S(2)}) async-start(bf16[32,8,16,128]{3,2,1,0:T(8,128)(2,1)} %bitcast.35), calls=%async_computation | async-start | bytes 2097152 | tf_op jit(solution)/shard_map/all_to_all | solution.py:467
  59.7 21.3 %copy-start.5 = (s32[32,1]{0,1:T(1,128)S(1)}, s32[32,1]{0,1:T(1,128)}, u32[]{:S(2)}) copy-start(s32[32,1]{0,1:T(1,128)} %param.21) | copy-start | bytes 388
  60.6 1.1 copy-start.1
  61.8 55.6 %copy-start.3 = (bf16[1,256,2048]{2,1,0:T(8,128)(2,1)S(1)}, bf16[1,256,2048]{2,1,0:T(8,128)(2,1)}, u32[]{:S(2)}) copy-start(bf16[1,256,2048]{2,1,0:T(8,128)(2,1)} %param.19) | copy-start | bytes 3145732
  81.0 36.4 %copy-start.2 = (bf16[3072,256]{1,0:T(8,128)(2,1)S(1)}, bf16[3072,256]{1,0:T(8,128)(2,1)}, u32[]{:S(2)}) copy-start(bf16[3072,256]{1,0:T(8,128)(2,1)} %copy-done.1) | copy-start | bytes 4718596
  113.0 9.3 %collective-permute-start.2 = (bf16[16,16,128]{2,1,0:T(8,128)(2,1)S(1)}, bf16[16,16,128]{2,1,0:T(8,128)(2,1)S(1)}, u32[]{:S(2)}, u32[]{:S(2)}) collective-permute-start(bf16[16,16,128]{2,1,0:T(8,128)(2,1)S(1)} %bitcast.37), channel_id=1, source_target_pairs={{0,1},{1,2},{2,3},{3,4},{4,5},{5,6},{6,7},{8,9},{9,10},{10,11},{11... | collective-permute-start | bytes 196616 | tf_op jit(solution)/shard_map/ppermute | solution.py:33
  114.3 8.0 %collective-permute-start.3 = (bf16[16,16,128]{2,1,0:T(8,128)(2,1)S(1)}, bf16[16,16,128]{2,1,0:T(8,128)(2,1)S(1)}, u32[]{:S(2)}, u32[]{:S(2)}) collective-permute-start(bf16[16,16,128]{2,1,0:T(8,128)(2,1)S(1)} %bitcast.36), channel_id=1, source_target_pairs={{1,0},{2,1},{3,2},{4,3},{5,4},{6,5},{7,6},{9,8},{10,9},{11,10},{12... | collective-permute-start | bytes 196616 | tf_op jit(solution)/shard_map/ppermute | solution.py:34

commit v6 on v5

--- a/solution.py
+++ b/solution.py
@@ -26,13 +26,20 @@
     return pltpu.CompilerParams(vmem_limit_bytes=VMEM_LIMIT)
 
 
-def neighbours(block, axis):
+def roomy():
+    return pltpu.CompilerParams(vmem_limit_bytes=56 * 2**20)
+
+
+def neighbours(block, axis, *after):
     count = lax.axis_size(axis)
     forward = [(i, i + 1) for i in range(count - 1)]
     backward = [(target, source) for source, target in forward]
-    low = lax.ppermute(block[-HALO:], axis, forward)
-    high = lax.ppermute(block[:HALO], axis, backward)
-    return low, high
+    top, bottom = block[:HALO], block[-HALO:]
+    if after:
+        top, bottom, *after = lax.optimization_barrier((top, bottom, *after))
+    low = lax.ppermute(bottom, axis, forward)
+    high = lax.ppermute(top, axis, backward)
+    return low, high, *after
 
 
 def fill_table(rows_ref, cols_ref, coeff_ref, table_ref):
@@ -140,66 +147,103 @@
     )
 
 
+def start_copies(pairs, sems):
+    copies = [
+        pltpu.make_async_copy(source, target, sems.at[i])
+        for i, (source, target) in enumerate(pairs)
+    ]
+    for copy in copies:
+        copy.start()
+    return copies
+
+
+def weigh(line, cover, weight):
+    good = cover.astype(jnp.float32) > 0
+    return (line * jnp.where(good, weight, 0.0)).astype(jnp.bfloat16)
+
+
 def match_kernel(turn, *refs):
     offset_ref, weight_ref = refs[:2]
-    operands = refs[2:9]
-    out_ref, windows, table_ref, result, sems, *rest = refs[9 if turn == 0 else 10 :]
-    held, lines = rest[:7], rest[7:]
+    operands = refs[2:7]
+    out_ref, windows, table_ref, result, sems, *rest = refs[7 if turn == 0 else 8 :]
+    held, lines = rest[:5], rest[5:]
 
     @pl.when(lax.axis_index("tile") % 2 == 1 - turn)
     def _():
-        copies = [
-            pltpu.make_async_copy(source, target, sems.at[i])
-            for i, (source, target) in enumerate(zip(operands, held))
-        ]
-        for copy in copies:
-            copy.start()
-        for copy in copies:
+        for copy in start_copies(zip(operands, held), sems):
             copy.wait()
-        low, mid, high, cover, rows, cols, coeff = held
+        mid, cover, rows, cols, coeff = held
         fill_table(rows, cols, coeff, table_ref)
         height = mid.shape[0]
         weight = weight_ref[0]
         shift = offset_ref[0] + HALF
-        units = height // UNIT + 2
+        each = (height - 2 * HALO) // PARTS
         done = 0
         copies = []
-        for first in range(0, height, CHUNK):
-            needed = min((first + CHUNK + 2 * HALO) // UNIT, units)
+        for part in range(PARTS):
+            first = HALO + part * each
+            needed = min(-(-(first + each + HALF + 1) // UNIT), height // UNIT)
             for u in range(done, needed):
-                if u == 0:
-                    source, at = low, 0
-                elif u == units - 1:
-                    source, at = high, 0
-                else:
-                    source, at = mid, (u - 1) * UNIT
-                lay_out_unit(source, at, shift, lines[u % len(lines)], windows, u)
+                lay_out_unit(mid, u * UNIT, shift, lines[u % len(lines)], windows, u + 1)
             done = needed
 
             def write(k, e, line, first=first):
                 r = first + QUAD * k + e
-                good = cover[r].astype(jnp.float32) > 0
-                result[r] = (line * jnp.where(good, weight, 0.0)).astype(jnp.bfloat16)
-
-            multiply(windows, [(first // QUAD, CHUNK // QUAD)], table_ref, write)
-            part = pl.ds(first, CHUNK)
-            copy = pltpu.make_async_copy(
-                result.at[part], out_ref.at[part], sems.at[first // CHUNK]
-            )
+                result[r] = weigh(line, cover[r], weight)
+
+            multiply(windows, [(first // QUAD, each // QUAD)], table_ref, write)
+            span = pl.ds(first, each)
+            copy = pltpu.make_async_copy(result.at[span], out_ref.at[span], sems.at[part])
             copy.start()
             copies.append(copy)
         for copy in copies:
             copy.wait()
 
 
-def cover_kernel(offset_ref, weight_ref, mask_ref, out_ref, *lines):
+def match_edge_kernel(
+    offset_ref, weight_ref, low, mid, high, cover, rows, cols, coeff, _, out_ref, windows, table_ref, result, sems, *lines
+):
+    height = mid.shape[0]
+    weight = weight_ref[0]
+    shift = offset_ref[0] + HALF
+    fill_table(rows, cols, coeff, table_ref)
+    sources = [
+        (low, 0),
+        (mid, 0),
+        (mid, UNIT),
+        (mid, height - 2 * UNIT),
+        (mid, height - UNIT),
+        (high, 0),
+    ]
+    for u, (source, first) in enumerate(sources):
+        lay_out_unit(source, first, shift, lines[u % len(lines)], windows, u)
+    each = HALO // QUAD
+
+    def write(k, e, line):
+        side, row = k // each, QUAD * (k % each) + e
+        result[side, row] = weigh(line, cover[row + side * (height - HALO)], weight)
+
+    multiply(windows, [(0, each), (3 * UNIT // QUAD, each)], table_ref, write)
+    ends = [
+        (result.at[side], out_ref.at[pl.ds(first, HALO)])
+        for side, first in enumerate((0, height - HALO))
+    ]
+    for copy in start_copies(ends, sems):
+        copy.wait()
+
+
+def cover_kernel(offset_ref, weight_ref, mask_ref, out_ref, held, sems, *lines):
     height, columns = mask_ref.shape
     blocks = columns // LANES
     weight = weight_ref[0]
+    spans = [pl.ds(first, CHUNK) for first in range(0, height, CHUNK)]
+    copies = start_copies([(mask_ref.at[s], held.at[s]) for s in spans], sems)
     for u in range(height // UNIT):
+        if u % (CHUNK // UNIT) == 0:
+            copies[u // (CHUNK // UNIT)].wait()
         spot = lines[u % len(lines)]
         rows = slice(u * UNIT, (u + 1) * UNIT)
-        good = [mask_ref[rows, lanes_of(h)].astype(jnp.float32) * weight for h in range(blocks)]
+        good = [held[rows, lanes_of(h)].astype(jnp.float32) * weight for h in range(blocks)]
         lay_out(good, offset_ref[0], spot, PAD, 2 * blocks)
         tiles = spot[...].reshape(UNIT, 2 * blocks, LANES)
         out_ref[rows] = tiles[:, PAD : PAD + blocks].astype(jnp.bfloat16)
@@ -213,10 +257,14 @@
     return pl.pallas_call(
         cover_kernel,
         out_shape=jax.ShapeDtypeStruct((height, blocks, LANES), jnp.bfloat16),
-        in_specs=[smem, smem, vmem],
+        in_specs=[smem, smem, pl.BlockSpec(memory_space=pl.ANY)],
         out_specs=vmem,
-        scratch_shapes=[pltpu.VMEM((UNIT * 2 * blocks, LANES), jnp.float32)] * 4,
-        compiler_params=params(),
+        scratch_shapes=[
+            pltpu.VMEM(mask.shape, mask.dtype),
+            pltpu.SemaphoreType.DMA((height // CHUNK,)),
+        ]
+        + [pltpu.VMEM((UNIT * 2 * blocks, LANES), jnp.float32)] * 4,
+        compiler_params=roomy(),
         cost_estimate=pl.CostEstimate(flops=10**6, bytes_accessed=6 * 10**6, transcendentals=0),
         name="cover_rows",
     )(offset, weight, mask)
@@ -233,7 +281,7 @@
 
 
 def match_visit(turn, offset, weight, operands, *before):
-    height, columns = operands[1].shape
+    height, columns = operands[0].shape
     blocks = columns // LANES
     smem = pl.BlockSpec(memory_space=pltpu.SMEM)
     anywhere = pl.BlockSpec(memory_space=pl.ANY)
@@ -243,7 +291,7 @@
         out_shape=jax.ShapeDtypeStruct(rows, jnp.bfloat16),
         in_specs=[smem, smem] + [anywhere] * (len(operands) + len(before)),
         out_specs=anywhere,
-        input_output_aliases={9: 0} if before else {},
+        input_output_aliases={7: 0} if before else {},
         scratch_shapes=[
             window_scratch(height + 2 * HALO, blocks),
             pltpu.VMEM((SHIFTS * LANES, QUAD * SPLIT), jnp.bfloat16),
@@ -252,10 +300,35 @@
         ]
         + [pltpu.VMEM(a.shape, a.dtype) for a in operands]
         + [pltpu.VMEM((UNIT * 4 * blocks, LANES), jnp.float32)] * 4,
-        compiler_params=pltpu.CompilerParams(vmem_limit_bytes=56 * 2**20),
+        compiler_params=roomy(),
         cost_estimate=conv_cost(height, columns),
         name="match_visit",
     )(offset, weight, *operands, *before)
+
+
+def match_edges(low, mid, high, cover, basis, offset, weight, weighted):
+    _, columns = mid.shape
+    blocks = columns // LANES
+    smem = pl.BlockSpec(memory_space=pltpu.SMEM)
+    vmem = pl.BlockSpec(memory_space=pltpu.VMEM)
+    anywhere = pl.BlockSpec(memory_space=pl.ANY)
+    return pl.pallas_call(
+        match_edge_kernel,
+        out_shape=jax.ShapeDtypeStruct(weighted.shape, weighted.dtype),
+        in_specs=[smem, smem] + [vmem] * 7 + [anywhere],
+        out_specs=anywhere,
+        input_output_aliases={9: 0},
+        scratch_shapes=[
+            window_scratch(6 * UNIT, blocks),
+            pltpu.VMEM((SHIFTS * LANES, QUAD * SPLIT), jnp.bfloat16),
+            pltpu.VMEM((2, HALO, blocks, LANES), jnp.bfloat16),
+            pltpu.SemaphoreType.DMA((2,)),
+        ]
+        + [pltpu.VMEM((UNIT * 4 * blocks, LANES), jnp.float32)] * 3,
+        compiler_params=roomy(),
+        cost_estimate=conv_cost(2 * HALO, columns),
+        name="match_edges",
+    )(offset, weight, low, mid, high, cover, *basis, weighted)
 
 
 def fill_windows(source, first, padded, windows, unit):
@@ -480,13 +553,17 @@
     new_coeff,
     new_patch,
 ):
-    low, high = neighbours(visit_image[0], "tile")
     cover = cover_rows(col_offset, visit_weight, good_mask[0])
-    operands = (low, visit_image[0], high, cover, basis_rows.T, basis_cols.T, visit_coeff)
+    basis = (basis_rows.T, basis_cols.T, visit_coeff)
+    operands = (visit_image[0], cover, *basis)
     weighted = match_visit(0, col_offset, visit_weight, operands)
     cover, weighted = lax.optimization_barrier((cover, weighted))
     received_cover = exchange(cover)
     weighted = match_visit(1, col_offset, visit_weight, operands, weighted)
+    low, high, weighted = neighbours(visit_image[0], "tile", weighted)
+    weighted = match_edges(
+        low, visit_image[0], high, cover, basis, col_offset, visit_weight, weighted
+    )
     received = exchange(weighted)
     cover_sums = sum_cover(received_cover, patch_of[:, 0])
     new_coeff, cover_sums = lax.optimization_barrier((new_coeff, cover_sums))

time: 125 us -> 131 us (1.048)
  the two profiles are of different devices: /device:TPU:7 before, /device:TPU:1 now
where the time goes in v6:
time: 131 us; the launch traced here: 130 us
  starting transfers between devices  33.3 us (25%)
  waiting for transfers between devices  32.3 us (25%)
  blocking collectives  30.4 us (23%)
  Pallas kernels  29.1 us (22%)
  local copies, waits for them, and re-layouts  2.7 us (2%)
  between operations  2.34 us (2%)
    all_to_all x1, blocking collectives, exchange(): lax.all_to_all(chunks, 'visit', split_axis=0, concat_axis=0, tiled=True)  30.4 us
    all_to_all x2, waiting for transfers between devices, exchange(): lax.all_to_all(chunks, 'visit', split_axis=0, concat_axis=0, tiled=True)  28.6 us
    all_to_all x2, starting transfers between devices, exchange(): lax.all_to_all(chunks, 'visit', split_axis=0, concat_axis=0, tiled=True)  17.2 us
    ppermute x2, starting transfers between devices, neighbours(): low = lax.ppermute(bottom, axis, forward)  12.1 us
    pallas_call x2, Pallas kernels, match_visit(): pl.pallas_call(functools.partial(match_kernel, turn), out_shape=jax.Shape...  9.83 us
    pallas_call x1, Pallas kernels, subtract_interior(): pl.pallas_call(interior_kernel, out_shape=jax.ShapeDtypeStruct(new.shape,...  4.9 us
    pallas_call x1, Pallas kernels, match_edges(): pl.pallas_call(match_edge_kernel, out_shape=jax.ShapeDtypeStruct(weighted...  4.67 us
    pallas_call x1, Pallas kernels, cover_rows(): pl.pallas_call(cover_kernel, out_shape=jax.ShapeDtypeStruct((height, bloc...  4.25 us
  transfers between devices with their start and end apart: 6, of which 3 were waited for; matrix products, arithmetic and copies ran while one was open for 1% of the time, Pallas kernels for 9%

profile of v6, /device:TPU:1, one launch (start us, length us, event | category | flops | bytes accessed | tf_op | source)
XLA Modules:
  0.0 130.1 jit_solution(1569970438868020346)
XLA Ops:
  1.9 4.2 %cover_rows.1.refs_3_.cover = bf16[256,16,128]{2,1,0:T(8,128)(2,1)} custom-call(s32[1]{0:T(128)S(6)} %copy.21.offset_ref.refs_0_, f32[1]{0:T(128)S(6)} %copy.20.weight_ref.refs_1_, s32[256,2048]{1,0:T(8,128)} %bitcast.36), custom_call_target="tpu_custom_call" | custom-call | flops 1000000 | bytes 6000000 | tf_op jit(solution)/shard_map/cover_rows/pallas_call | solution.py:257
  6.2 9.6 %match_visit.2.refs_7_ = bf16[256,16,128]{2,1,0:T(8,128)(2,1)} custom-call(s32[1]{0:T(128)S(6)} %copy.21.offset_ref.refs_0_, f32[1]{0:T(128)S(6)} %copy.20.weight_ref.refs_1_, bf16[256,2048]{1,0:T(8,128)(2,1)} %bitcast.38, bf16[256,16,128]{2,1,0:T(8,128)(2,1)} %cover_rows.1.refs_3_.cover, f32[21,27]{1,0:T(8,128)} %bitcast.24, f32[21,27]{1,0:T(8,128)} %bitcast.28, ...), custom_call_target="tpu_custom_call" | custom-call | flops 3221225472 | bytes 8000000 | tf_op jit(solution)/shard_map/match_visit/pallas_call | solution.py:289
  15.8 12.1 %all-to-all-start.1 = ((bf16[32,8,16,128]{3,2,1,0:T(8,128)(2,1)}), bf16[32,8,16,128]{3,2,1,0:T(8,128)(2,1)S(1)}, u32[]{:S(2)}, u32[]{:S(2)}) async-start(bf16[32,8,16,128]{3,2,1,0:T(8,128)(2,1)} %bitcast.9), calls=%async_computation.1 | async-start | bytes 2097152 | tf_op jit(solution)/shard_map/all_to_all | solution.py:540
  27.9 0.2 match_visit.3._
  28.1 0.9 slice_bitcast_fusion
  29.0 3.9 %collective-permute-start = (bf16[16,2048]{1,0:T(8,128)(2,1)S(1)}, bf16[16,2048]{1,0:T(8,128)(2,1)S(1)}, u32[]{:S(2)}, u32[]{:S(2)}) collective-permute-start(bf16[16,2048]{1,0:T(8,128)(2,1)S(1)} %get-tuple-element.14), channel_id=1, source_target_pairs={{0,1},{1,2},{2,3},{3,4},{4,5},{5,6},{6,7},{8,9},{9,10},{10,11},{11... | collective-permute-start | bytes 196616 | tf_op jit(solution)/shard_map/ppermute | solution.py:40
  32.9 1.9 %collective-permute-start.1 = (bf16[16,2048]{1,0:T(8,128)(2,1)S(1)}, bf16[16,2048]{1,0:T(8,128)(2,1)S(1)}, u32[]{:S(2)}, u32[]{:S(2)}) collective-permute-start(bf16[16,2048]{1,0:T(8,128)(2,1)S(1)} %get-tuple-element.15), channel_id=1, source_target_pairs={{1,0},{2,1},{3,2},{4,3},{5,4},{6,5},{7,6},{9,8},{10,9},{11,10},{12... | collective-permute-start | bytes 196616 | tf_op jit(solution)/shard_map/ppermute | solution.py:41
  34.9 0.0 collective-permute-done.low
  34.9 0.0 copy-start.8
  34.9 3.7 %collective-permute-done.1.high = bf16[16,2048]{1,0:T(8,128)(2,1)S(1)} collective-permute-done((bf16[16,2048]{1,0:T(8,128)(2,1)S(1)}, bf16[16,2048]{1,0:T(8,128)(2,1)S(1)}, u32[]{:S(2)}, u32[]{:S(2)}) %collective-permute-start.1) | collective-permute-done | bytes 65568 | tf_op jit(solution)/shard_map/ppermute | solution.py:41
  38.6 0.0 copy-done.8
  38.6 0.0 copy-start.9
  38.6 0.6 copy-done.9
  39.2 4.7 %match_edges.1 = bf16[256,16,128]{2,1,0:T(8,128)(2,1)} custom-call(s32[1]{0:T(128)S(6)} %copy.21.offset_ref.refs_0_, f32[1]{0:T(128)S(6)} %copy.20.weight_ref.refs_1_, bf16[16,2048]{1,0:T(8,128)(2,1)} %copy-done.8, bf16[256,2048]{1,0:T(8,128)(2,1)} %bitcast.40, bf16[16,2048]{1,0:T(8,128)(2,1)} %copy-done.9, ...), custom_call_target="tpu_custom_call", output_to_operand_aliasing={{}: (9, {})} | custom-call | flops 402653184 | bytes 8000000 | tf_op jit(solution)/shard_map/match_edges/pallas_call | solution.py:315
  43.9 0.0 copy-start.5
  43.9 0.0 copy-start.3
  43.9 0.0 copy-start.4
  43.9 0.0 copy-start.7
  43.9 4.4 %all-to-all-done.1.received_ref = bf16[32,8,16,128]{3,2,1,0:T(8,128)(2,1)S(1)} async-done(((bf16[32,8,16,128]{3,2,1,0:T(8,128)(2,1)}), bf16[32,8,16,128]{3,2,1,0:T(8,128)(2,1)S(1)}, u32[]{:S(2)}, u32[]{:S(2)}) %all-to-all-start.1) | async-done | bytes 1048608 | tf_op jit(solution)/shard_map/all_to_all | solution.py:540
  48.3 5.1 %all-to-all-start = ((bf16[32,8,16,128]{3,2,1,0:T(8,128)(2,1)}), bf16[32,8,16,128]{3,2,1,0:T(8,128)(2,1)S(1)}, u32[]{:S(2)}, u32[]{:S(2)}) async-start(bf16[32,8,16,128]{3,2,1,0:T(8,128)(2,1)} %bitcast.35), calls=%async_computation | async-start | bytes 2097152 | tf_op jit(solution)/shard_map/all_to_all | solution.py:540
  53.4 0.0 copy-done.5
  53.4 0.9 sum_cover.1.cover_ref
  54.3 0.0 copy-done.3
  54.3 0.0 copy-done.4
  54.4 0.0 copy-done.7
  54.4 0.0 copy-start.6
  54.4 1.0 table.1.table_ref
  55.3 0.0 copy-start
  55.4 1.1 copy-done
  56.5 0.0 copy-start.2
  56.5 24.3 %all-to-all-done.received_ref = bf16[32,8,16,128]{3,2,1,0:T(8,128)(2,1)S(1)} async-done(((bf16[32,8,16,128]{3,2,1,0:T(8,128)(2,1)}), bf16[32,8,16,128]{3,2,1,0:T(8,128)(2,1)S(1)}, u32[]{:S(2)}, u32[]{:S(2)}) %all-to-all-start) | async-done | bytes 1048608 | tf_op jit(solution)/shard_map/all_to_all | solution.py:540
  80.8 0.0 copy-start.1
  80.8 0.0 copy-done.6
  80.8 2.1 %combine.1 = (bf16[8,8,2048]{2,1,0:T(8,128)(2,1)}, bf16[32,8,16,128]{3,2,1,0:T(8,128)(2,1)S(1)}) custom-call(s32[32]{0:T(128)S(1)} %bitcast.33, s32[32]{0:T(128)S(1)} %bitcast.34, bf16[32,8,16,128]{3,2,1,0:T(8,128)(2,1)S(1)} %all-to-all-done.received_ref, f32[8,8,16,128]{3,2,1,0:T(8,128)S(1)} %sum_cover.1.cover_ref), custom_call_target="tpu_custom_call" | custom-call | tf_op jit(solution)/shard_map/combine/pallas_call | solution.py:519
  82.8 30.4 %all_to_all.15 = bf16[32,8,16,128]{3,2,1,0:T(8,128)(2,1)S(1)} all-to-all(bf16[32,8,16,128]{3,2,1,0:T(8,128)(2,1)S(1)} %get-tuple-element.22), channel_id=1, replica_groups=mesh['visit'=32,'tile'=8] {'visit'}, dimensions={0} | all-to-all | bytes 2097152 | tf_op jit(solution)/shard_map/all_to_all | solution.py:540
  113.2 8.1 %collective-permute-start.2 = (bf16[16,16,128]{2,1,0:T(8,128)(2,1)S(1)}, bf16[16,16,128]{2,1,0:T(8,128)(2,1)S(1)}, u32[]{:S(2)}, u32[]{:S(2)}) collective-permute-start(bf16[16,16,128]{2,1,0:T(8,128)(2,1)S(1)} %bitcast.42), channel_id=1, source_target_pairs={{0,1},{1,2},{2,3},{3,4},{4,5},{5,6},{6,7},{8,9},{9,10},{10,11},{11... | collective-permute-start | bytes 196616 | tf_op jit(solution)/shard_map/ppermute | solution.py:40
  121.4 2.1 %collective-permute-start.3 = (bf16[16,16,128]{2,1,0:T(8,128)(2,1)S(1)}, bf16[16,16,128]{2,1,0:T(8,128)(2,1)S(1)}, u32[]{:S(2)}, u32[]{:S(2)}) collective-permute-start(bf16[16,16,128]{2,1,0:T(8,128)(2,1)S(1)} %bitcast.41), channel_id=1, source_target_pairs={{1,0},{2,1},{3,2},{4,3},{5,4},{6,5},{7,6},{9,8},{10,9},{11,10},{12... | collective-permute-start | bytes 196616 | tf_op jit(solution)/shard_map/ppermute | solution.py:41
  123.5 0.0 copy-done.2
  123.5 0.0 copy-done.1
  123.5 4.9 %subtract_interior.1._ = f32[256,2048]{1,0:T(8,128)} custom-call(bf16[256,16,128]{2,1,0:T(8,128)(2,1)S(1)} %bitcast.20, bf16[256,2048]{1,0:T(8,128)(2,1)S(1)} %bitcast.22, bf16[3072,256]{1,0:T(8,128)(2,1)S(1)} %copy-done.1), custom_call_target="tpu_custom_call" | custom-call | flops 3221225472 | bytes 8000000 | tf_op jit(solution)/shard_map/subtract_interior/pallas_call | solution.py:394
  128.4 0.0 collective-permute-done.2.low_ref
  128.5 0.0 collective-permute-done.3.high_ref
  128.5 1.5 %subtract_edges.1 = f32[256,2048]{1,0:T(8,128)} custom-call(bf16[16,16,128]{2,1,0:T(8,128)(2,1)S(1)} %collective-permute-done.2.low_ref, bf16[256,16,128]{2,1,0:T(8,128)(2,1)S(1)} %bitcast.21, bf16[16,16,128]{2,1,0:T(8,128)(2,1)S(1)} %collective-permute-done.3.high_ref, bf16[256,2048]{1,0:T(8,128)(2,1)S(1)} %bitcast.23, ...), custom_call_target="tpu_custom_call", output_to_operand_aliasing={{}: (5, {})} | custom-call | flops 402653184 | bytes 8000000 | tf_op jit(solution)/shard_map/subtract_edges/pallas_call | solution.py:451
  (1 shorter events, 0.0 us)
Async XLA Ops:
  15.8 32.5 %all-to-all-start.1 = ((bf16[32,8,16,128]{3,2,1,0:T(8,128)(2,1)}), bf16[32,8,16,128]{3,2,1,0:T(8,128)(2,1)S(1)}, u32[]{:S(2)}, u32[]{:S(2)}) async-start(bf16[32,8,16,128]{3,2,1,0:T(8,128)(2,1)} %bitcast.9), calls=%async_computation.1 | async-start | bytes 2097152 | tf_op jit(solution)/shard_map/all_to_all | solution.py:540
  29.0 5.9 %collective-permute-start = (bf16[16,2048]{1,0:T(8,128)(2,1)S(1)}, bf16[16,2048]{1,0:T(8,128)(2,1)S(1)}, u32[]{:S(2)}, u32[]{:S(2)}) collective-permute-start(bf16[16,2048]{1,0:T(8,128)(2,1)S(1)} %get-tuple-element.14), channel_id=1, source_target_pairs={{0,1},{1,2},{2,3},{3,4},{4,5},{5,6},{6,7},{8,9},{9,10},{10,11},{11... | collective-permute-start | bytes 196616 | tf_op jit(solution)/shard_map/ppermute | solution.py:40
  32.9 5.6 %collective-permute-start.1 = (bf16[16,2048]{1,0:T(8,128)(2,1)S(1)}, bf16[16,2048]{1,0:T(8,128)(2,1)S(1)}, u32[]{:S(2)}, u32[]{:S(2)}) collective-permute-start(bf16[16,2048]{1,0:T(8,128)(2,1)S(1)} %get-tuple-element.15), channel_id=1, source_target_pairs={{1,0},{2,1},{3,2},{4,3},{5,4},{6,5},{7,6},{9,8},{10,9},{11,10},{12... | collective-permute-start | bytes 196616 | tf_op jit(solution)/shard_map/ppermute | solution.py:41
  34.9 3.7 %copy-start.8 = (bf16[16,2048]{1,0:T(8,128)(2,1)}, bf16[16,2048]{1,0:T(8,128)(2,1)S(1)}, u32[]{:S(2)}) copy-start(bf16[16,2048]{1,0:T(8,128)(2,1)S(1)} %collective-permute-done.low) | copy-start | bytes 196612
  38.6 0.6 copy-start.9
  43.9 9.6 %copy-start.5 = (s32[32,1]{0,1:T(1,128)S(1)}, s32[32,1]{0,1:T(1,128)}, u32[]{:S(2)}) copy-start(s32[32,1]{0,1:T(1,128)} %param.18) | copy-start | bytes 388
  43.9 10.5 %copy-start.3 = (f32[27,21]{0,1:T(8,128)S(1)}, f32[27,21]{0,1:T(8,128)}, u32[]{:S(2)}) copy-start(f32[27,21]{0,1:T(8,128)} %param.13) | copy-start | bytes 6808
  43.9 10.5 %copy-start.4 = (f32[27,21]{0,1:T(8,128)S(1)}, f32[27,21]{0,1:T(8,128)}, u32[]{:S(2)}) copy-start(f32[27,21]{0,1:T(8,128)} %param.14) | copy-start | bytes 6808
  43.9 10.5 %copy-start.7 = (f32[1,27]{1,0:T(1,128)S(1)}, f32[1,27]{1,0:T(1,128)}, u32[]{:S(2)}) copy-start(f32[1,27]{1,0:T(1,128)} %coeff_ref) | copy-start | bytes 328
  48.3 32.5 %all-to-all-start = ((bf16[32,8,16,128]{3,2,1,0:T(8,128)(2,1)}), bf16[32,8,16,128]{3,2,1,0:T(8,128)(2,1)S(1)}, u32[]{:S(2)}, u32[]{:S(2)}) async-start(bf16[32,8,16,128]{3,2,1,0:T(8,128)(2,1)} %bitcast.35), calls=%async_computation | async-start | bytes 2097152 | tf_op jit(solution)/shard_map/all_to_all | solution.py:540
  54.4 26.4 %copy-start.6 = (s32[32,1]{0,1:T(1,128)S(1)}, s32[32,1]{0,1:T(1,128)}, u32[]{:S(2)}) copy-start(s32[32,1]{0,1:T(1,128)} %param.21) | copy-start | bytes 388
  55.3 1.1 copy-start
  56.5 67.0 %copy-start.2 = (bf16[1,256,2048]{2,1,0:T(8,128)(2,1)S(1)}, bf16[1,256,2048]{2,1,0:T(8,128)(2,1)}, u32[]{:S(2)}) copy-start(bf16[1,256,2048]{2,1,0:T(8,128)(2,1)} %param.19) | copy-start | bytes 3145732
  80.8 42.8 %copy-start.1 = (bf16[3072,256]{1,0:T(8,128)(2,1)S(1)}, bf16[3072,256]{1,0:T(8,128)(2,1)}, u32[]{:S(2)}) copy-start(bf16[3072,256]{1,0:T(8,128)(2,1)} %copy-done) | copy-start | bytes 4718596
  113.2 15.2 %collective-permute-start.2 = (bf16[16,16,128]{2,1,0:T(8,128)(2,1)S(1)}, bf16[16,16,128]{2,1,0:T(8,128)(2,1)S(1)}, u32[]{:S(2)}, u32[]{:S(2)}) collective-permute-start(bf16[16,16,128]{2,1,0:T(8,128)(2,1)S(1)} %bitcast.42), channel_id=1, source_target_pairs={{0,1},{1,2},{2,3},{3,4},{4,5},{5,6},{6,7},{8,9},{9,10},{10,11},{11... | collective-permute-start | bytes 196616 | tf_op jit(solution)/shard_map/ppermute | solution.py:40
  121.4 7.1 %collective-permute-start.3 = (bf16[16,16,128]{2,1,0:T(8,128)(2,1)S(1)}, bf16[16,16,128]{2,1,0:T(8,128)(2,1)S(1)}, u32[]{:S(2)}, u32[]{:S(2)}) collective-permute-start(bf16[16,16,128]{2,1,0:T(8,128)(2,1)S(1)} %bitcast.41), channel_id=1, source_target_pairs={{1,0},{2,1},{3,2},{4,3},{5,4},{6,5},{7,6},{9,8},{10,9},{11,10},{12... | collective-permute-start | bytes 196616 | tf_op jit(solution)/shard_map/ppermute | solution.py:41

commit v7 on v5

--- a/solution.py
+++ b/solution.py
@@ -24,6 +24,10 @@
 
 def params():
     return pltpu.CompilerParams(vmem_limit_bytes=VMEM_LIMIT)
+
+
+def roomy():
+    return pltpu.CompilerParams(vmem_limit_bytes=56 * 2**20)
 
 
 def neighbours(block, axis):
@@ -192,14 +196,28 @@
             copy.wait()
 
 
-def cover_kernel(offset_ref, weight_ref, mask_ref, out_ref, *lines):
+def start_copies(pairs, sems):
+    copies = [
+        pltpu.make_async_copy(source, target, sems.at[i])
+        for i, (source, target) in enumerate(pairs)
+    ]
+    for copy in copies:
+        copy.start()
+    return copies
+
+
+def cover_kernel(offset_ref, weight_ref, mask_ref, out_ref, held, sems, *lines):
     height, columns = mask_ref.shape
     blocks = columns // LANES
     weight = weight_ref[0]
+    spans = [pl.ds(first, CHUNK) for first in range(0, height, CHUNK)]
+    copies = start_copies([(mask_ref.at[s], held.at[s]) for s in spans], sems)
     for u in range(height // UNIT):
+        if u % (CHUNK // UNIT) == 0:
+            copies[u // (CHUNK // UNIT)].wait()
         spot = lines[u % len(lines)]
         rows = slice(u * UNIT, (u + 1) * UNIT)
-        good = [mask_ref[rows, lanes_of(h)].astype(jnp.float32) * weight for h in range(blocks)]
+        good = [held[rows, lanes_of(h)].astype(jnp.float32) * weight for h in range(blocks)]
         lay_out(good, offset_ref[0], spot, PAD, 2 * blocks)
         tiles = spot[...].reshape(UNIT, 2 * blocks, LANES)
         out_ref[rows] = tiles[:, PAD : PAD + blocks].astype(jnp.bfloat16)
@@ -213,10 +231,14 @@
     return pl.pallas_call(
         cover_kernel,
         out_shape=jax.ShapeDtypeStruct((height, blocks, LANES), jnp.bfloat16),
-        in_specs=[smem, smem, vmem],
+        in_specs=[smem, smem, pl.BlockSpec(memory_space=pl.ANY)],
         out_specs=vmem,
-        scratch_shapes=[pltpu.VMEM((UNIT * 2 * blocks, LANES), jnp.float32)] * 4,
-        compiler_params=params(),
+        scratch_shapes=[
+            pltpu.VMEM(mask.shape, mask.dtype),
+            pltpu.SemaphoreType.DMA((height // CHUNK,)),
+        ]
+        + [pltpu.VMEM((UNIT * 2 * blocks, LANES), jnp.float32)] * 4,
+        compiler_params=roomy(),
         cost_estimate=pl.CostEstimate(flops=10**6, bytes_accessed=6 * 10**6, transcendentals=0),
         name="cover_rows",
     )(offset, weight, mask)
@@ -402,7 +424,7 @@
         sums[p] = sums[p] + received_ref[v].astype(jnp.float32)
         return carry
 
-    lax.fori_loop(0, received_ref.shape[0], add, 0)
+    lax.fori_loop(0, received_ref.shape[0], add, 0, unroll=4)
 
 
 def sum_cover(received, patch_of):
@@ -436,7 +458,7 @@
         send_ref[n] = packed[wanted_ref[n]]
         return carry
 
-    lax.fori_loop(0, send_ref.shape[0], place, 0)
+    lax.fori_loop(0, send_ref.shape[0], place, 0, unroll=4)
 
 
 def combine(received, cover_sums, patch_of, new_patch):

time: 125 us -> 124 us (level)
  local copies, waits for them, and re-layouts: 4.29 us -> 2.69 us
    unnamed x22 -> x20, local copies, waits for them, and re-layouts: 3.4 us -> 1.8 us
    pallas_call x1, Pallas kernels: 2.91 us -> 4.25 us  [cover_rows(): pl.pallas_call(cover_kernel, out_shape=jax.ShapeDtypeStruct((height, bloc...]
  transfers between devices with their start and end apart: 6 -> 6, of which waited for: 2 -> 2; matrix products, arithmetic and copies ran while one was open for 0% -> 0% of each run, Pallas kernels for 8% -> 9%
where the time goes in v7:
time: 124 us
  waiting for transfers between devices  38.9 us (31%)
  blocking collectives  30 us (24%)
  Pallas kernels  25.1 us (20%)
  starting transfers between devices  24.5 us (20%)
  local copies, waits for them, and re-layouts  2.69 us (2%)
  between operations  2.33 us (2%)
    all_to_all x2, waiting for transfers between devices, exchange(): lax.all_to_all(chunks, 'visit', split_axis=0, concat_axis=0, tiled=True)  38.9 us
    all_to_all x1, blocking collectives, exchange(): lax.all_to_all(chunks, 'visit', split_axis=0, concat_axis=0, tiled=True)  30 us
    all_to_all x2, starting transfers between devices, exchange(): lax.all_to_all(chunks, 'visit', split_axis=0, concat_axis=0, tiled=True)  16.3 us
    pallas_call x2, Pallas kernels, match_visit(): pl.pallas_call(functools.partial(match_kernel, turn), out_shape=jax.Shape...  10.8 us
    ppermute x2, starting transfers between devices, neighbours(): high = lax.ppermute(block[:HALO], axis, backward)  5.62 us
    pallas_call x1, Pallas kernels, subtract_interior(): pl.pallas_call(interior_kernel, out_shape=jax.ShapeDtypeStruct(new.shape,...  4.89 us
    pallas_call x1, Pallas kernels, cover_rows(): pl.pallas_call(cover_kernel, out_shape=jax.ShapeDtypeStruct((height, bloc...  4.25 us
    ppermute x2, starting transfers between devices, neighbours(): low = lax.ppermute(block[-HALO:], axis, forward)  2.58 us
  transfers between devices with their start and end apart: 6, of which 2 were waited for; matrix products, arithmetic and copies ran while one was open for 0% of the time, Pallas kernels for 9%

profile of v7, /device:TPU:7, one launch (start us, length us, event | category | flops | bytes accessed | tf_op | source)
XLA Modules:
  0.0 123.5 jit_solution(12166207996597848495)
XLA Ops:
  0.6 0.9 slice_bitcast_fusion
  1.5 2.6 %collective-permute-start.1 = (bf16[16,2048]{1,0:T(8,128)(2,1)S(1)}, bf16[16,2048]{1,0:T(8,128)(2,1)S(1)}, u32[]{:S(2)}, u32[]{:S(2)}) collective-permute-start(bf16[16,2048]{1,0:T(8,128)(2,1)S(1)} %get-tuple-element.22), channel_id=1, source_target_pairs={{1,0},{2,1},{3,2},{4,3},{5,4},{6,5},{7,6},{9,8},{10,9},{11,10},{12... | collective-permute-start | bytes 196616 | tf_op jit(solution)/shard_map/ppermute | solution.py:38
  4.1 1.3 %collective-permute-start = (bf16[16,2048]{1,0:T(8,128)(2,1)S(1)}, bf16[16,2048]{1,0:T(8,128)(2,1)S(1)}, u32[]{:S(2)}, u32[]{:S(2)}) collective-permute-start(bf16[16,2048]{1,0:T(8,128)(2,1)S(1)} %get-tuple-element.23), channel_id=1, source_target_pairs={{0,1},{1,2},{2,3},{3,4},{4,5},{5,6},{6,7},{8,9},{9,10},{10,11},{11... | collective-permute-start | bytes 196616 | tf_op jit(solution)/shard_map/ppermute | solution.py:37
  6.7 4.2 %cover_rows.1.refs_5_ = bf16[256,16,128]{2,1,0:T(8,128)(2,1)} custom-call(s32[1]{0:T(128)S(6)} %copy.19.offset_ref.refs_0_, f32[1]{0:T(128)S(6)} %copy.18.weight_ref.refs_1_, s32[256,2048]{1,0:T(8,128)} %bitcast.33), custom_call_target="tpu_custom_call" | custom-call | flops 1000000 | bytes 6000000 | tf_op jit(solution)/shard_map/cover_rows/pallas_call | solution.py:231
  11.0 0.0 collective-permute-done.1.refs_4_
  11.0 0.0 copy-start.8
  11.0 0.0 collective-permute-done.refs_2_
  11.0 0.0 copy-start.9
  11.0 0.6 copy-done.8
  11.6 0.0 copy-done.9
  11.6 10.6 %match_visit.2.refs_9_ = bf16[256,16,128]{2,1,0:T(8,128)(2,1)} custom-call(s32[1]{0:T(128)S(6)} %copy.19.offset_ref.refs_0_, f32[1]{0:T(128)S(6)} %copy.18.weight_ref.refs_1_, bf16[16,2048]{1,0:T(8,128)(2,1)} %copy-done.9, bf16[256,2048]{1,0:T(8,128)(2,1)} %bitcast.38, bf16[16,2048]{1,0:T(8,128)(2,1)} %copy-done.8, bf16[256,16,128]{2,1,0:T(8,128)(2,1)} %cover_rows.1.refs_5_, ...), custom_call_target="tpu_custom_call" | custom-call | flops 3221225472 | bytes 8000000 | tf_op jit(solution)/shard_map/match_visit/pallas_call | solution.py:263
  22.2 11.2 %all-to-all-start.1 = ((bf16[32,8,16,128]{3,2,1,0:T(8,128)(2,1)}), bf16[32,8,16,128]{3,2,1,0:T(8,128)(2,1)S(1)}, u32[]{:S(2)}, u32[]{:S(2)}) async-start(bf16[32,8,16,128]{3,2,1,0:T(8,128)(2,1)} %bitcast.9), calls=%async_computation.1 | async-start | bytes 2097152 | tf_op jit(solution)/shard_map/all_to_all | solution.py:489
  33.4 0.3 match_visit.3
  33.7 0.0 copy-start.3
  33.7 0.0 copy-start.5
  33.7 0.0 copy-start.6
  33.7 0.0 copy-start.7
  33.7 19.6 %all-to-all-done.1.received_ref = bf16[32,8,16,128]{3,2,1,0:T(8,128)(2,1)S(1)} async-done(((bf16[32,8,16,128]{3,2,1,0:T(8,128)(2,1)}), bf16[32,8,16,128]{3,2,1,0:T(8,128)(2,1)S(1)}, u32[]{:S(2)}, u32[]{:S(2)}) %all-to-all-start.1) | async-done | bytes 1048608 | tf_op jit(solution)/shard_map/all_to_all | solution.py:489
  53.3 5.1 %all-to-all-start = ((bf16[32,8,16,128]{3,2,1,0:T(8,128)(2,1)}), bf16[32,8,16,128]{3,2,1,0:T(8,128)(2,1)S(1)}, u32[]{:S(2)}, u32[]{:S(2)}) async-start(bf16[32,8,16,128]{3,2,1,0:T(8,128)(2,1)} %bitcast.35), calls=%async_computation | async-start | bytes 2097152 | tf_op jit(solution)/shard_map/all_to_all | solution.py:489
  58.5 0.0 copy-done.3
  58.5 0.8 sum_cover.1.cover_ref
  59.3 0.0 copy-done.5
  59.3 0.0 copy-done.6
  59.3 0.0 copy-done.7
  59.3 0.0 copy-start.4
  59.4 1.0 table.1.table_ref
  60.3 0.0 copy-start
  60.3 1.1 copy-done
  61.5 0.0 copy-start.2
  61.5 19.2 %all-to-all-done.received_ref = bf16[32,8,16,128]{3,2,1,0:T(8,128)(2,1)S(1)} async-done(((bf16[32,8,16,128]{3,2,1,0:T(8,128)(2,1)}), bf16[32,8,16,128]{3,2,1,0:T(8,128)(2,1)S(1)}, u32[]{:S(2)}, u32[]{:S(2)}) %all-to-all-start) | async-done | bytes 1048608 | tf_op jit(solution)/shard_map/all_to_all | solution.py:489
  80.7 0.0 copy-start.1
  80.7 0.0 copy-done.4
  80.7 1.9 %combine.1 = (bf16[8,8,2048]{2,1,0:T(8,128)(2,1)}, bf16[32,8,16,128]{3,2,1,0:T(8,128)(2,1)S(1)}) custom-call(s32[32]{0:T(128)S(1)} %bitcast.25, s32[32]{0:T(128)S(1)} %bitcast.26, bf16[32,8,16,128]{3,2,1,0:T(8,128)(2,1)S(1)} %all-to-all-done.received_ref, f32[8,8,16,128]{3,2,1,0:T(8,128)S(1)} %sum_cover.1.cover_ref), custom_call_target="tpu_custom_call" | custom-call | tf_op jit(solution)/shard_map/combine/pallas_call | solution.py:468
  82.6 30.0 %all_to_all.15 = bf16[32,8,16,128]{3,2,1,0:T(8,128)(2,1)S(1)} all-to-all(bf16[32,8,16,128]{3,2,1,0:T(8,128)(2,1)S(1)} %get-tuple-element.16), channel_id=1, replica_groups=mesh['visit'=32,'tile'=8] {'visit'}, dimensions={0} | all-to-all | bytes 2097152 | tf_op jit(solution)/shard_map/all_to_all | solution.py:489
  112.6 1.3 %collective-permute-start.2 = (bf16[16,16,128]{2,1,0:T(8,128)(2,1)S(1)}, bf16[16,16,128]{2,1,0:T(8,128)(2,1)S(1)}, u32[]{:S(2)}, u32[]{:S(2)}) collective-permute-start(bf16[16,16,128]{2,1,0:T(8,128)(2,1)S(1)} %bitcast.37), channel_id=1, source_target_pairs={{0,1},{1,2},{2,3},{3,4},{4,5},{5,6},{6,7},{8,9},{9,10},{10,11},{11... | collective-permute-start | bytes 196616 | tf_op jit(solution)/shard_map/ppermute | solution.py:37
  113.9 3.0 %collective-permute-start.3 = (bf16[16,16,128]{2,1,0:T(8,128)(2,1)S(1)}, bf16[16,16,128]{2,1,0:T(8,128)(2,1)S(1)}, u32[]{:S(2)}, u32[]{:S(2)}) collective-permute-start(bf16[16,16,128]{2,1,0:T(8,128)(2,1)S(1)} %bitcast.36), channel_id=1, source_target_pairs={{1,0},{2,1},{3,2},{4,3},{5,4},{6,5},{7,6},{9,8},{10,9},{11,10},{12... | collective-permute-start | bytes 196616 | tf_op jit(solution)/shard_map/ppermute | solution.py:38
  117.0 0.0 copy-done.2
  117.0 0.0 copy-done.1
  117.0 4.9 %subtract_interior.1._ = f32[256,2048]{1,0:T(8,128)} custom-call(bf16[256,16,128]{2,1,0:T(8,128)(2,1)S(1)} %bitcast.20, bf16[256,2048]{1,0:T(8,128)(2,1)S(1)} %bitcast.22, bf16[3072,256]{1,0:T(8,128)(2,1)S(1)} %copy-done.1), custom_call_target="tpu_custom_call" | custom-call | flops 3221225472 | bytes 8000000 | tf_op jit(solution)/shard_map/subtract_interior/pallas_call | solution.py:343
  121.9 0.0 collective-permute-done.2.low_ref
  121.9 0.0 collective-permute-done.3.high_ref
  121.9 1.5 %subtract_edges.1 = f32[256,2048]{1,0:T(8,128)} custom-call(bf16[16,16,128]{2,1,0:T(8,128)(2,1)S(1)} %collective-permute-done.2.low_ref, bf16[256,16,128]{2,1,0:T(8,128)(2,1)S(1)} %bitcast.21, bf16[16,16,128]{2,1,0:T(8,128)(2,1)S(1)} %collective-permute-done.3.high_ref, bf16[256,2048]{1,0:T(8,128)(2,1)S(1)} %bitcast.23, ...), custom_call_target="tpu_custom_call", output_to_operand_aliasing={{}: (5, {})} | custom-call | flops 402653184 | bytes 8000000 | tf_op jit(solution)/shard_map/subtract_edges/pallas_call | solution.py:400
  (1 shorter events, 0.0 us)
Async XLA Ops:
  1.5 9.4 %collective-permute-start.1 = (bf16[16,2048]{1,0:T(8,128)(2,1)S(1)}, bf16[16,2048]{1,0:T(8,128)(2,1)S(1)}, u32[]{:S(2)}, u32[]{:S(2)}) collective-permute-start(bf16[16,2048]{1,0:T(8,128)(2,1)S(1)} %get-tuple-element.22), channel_id=1, source_target_pairs={{1,0},{2,1},{3,2},{4,3},{5,4},{6,5},{7,6},{9,8},{10,9},{11,10},{12... | collective-permute-start | bytes 196616 | tf_op jit(solution)/shard_map/ppermute | solution.py:38
  4.1 6.9 %collective-permute-start = (bf16[16,2048]{1,0:T(8,128)(2,1)S(1)}, bf16[16,2048]{1,0:T(8,128)(2,1)S(1)}, u32[]{:S(2)}, u32[]{:S(2)}) collective-permute-start(bf16[16,2048]{1,0:T(8,128)(2,1)S(1)} %get-tuple-element.23), channel_id=1, source_target_pairs={{0,1},{1,2},{2,3},{3,4},{4,5},{5,6},{6,7},{8,9},{9,10},{10,11},{11... | collective-permute-start | bytes 196616 | tf_op jit(solution)/shard_map/ppermute | solution.py:37
  11.0 0.6 copy-start.8
  11.0 0.6 copy-start.9
  22.2 31.2 %all-to-all-start.1 = ((bf16[32,8,16,128]{3,2,1,0:T(8,128)(2,1)}), bf16[32,8,16,128]{3,2,1,0:T(8,128)(2,1)S(1)}, u32[]{:S(2)}, u32[]{:S(2)}) async-start(bf16[32,8,16,128]{3,2,1,0:T(8,128)(2,1)} %bitcast.9), calls=%async_computation.1 | async-start | bytes 2097152 | tf_op jit(solution)/shard_map/all_to_all | solution.py:489
  33.7 24.8 %copy-start.3 = (s32[32,1]{0,1:T(1,128)S(1)}, s32[32,1]{0,1:T(1,128)}, u32[]{:S(2)}) copy-start(s32[32,1]{0,1:T(1,128)} %param.18) | copy-start | bytes 388
  33.7 25.6 %copy-start.5 = (f32[27,21]{0,1:T(8,128)S(1)}, f32[27,21]{0,1:T(8,128)}, u32[]{:S(2)}) copy-start(f32[27,21]{0,1:T(8,128)} %param.13) | copy-start | bytes 6808
  33.7 25.6 %copy-start.6 = (f32[27,21]{0,1:T(8,128)S(1)}, f32[27,21]{0,1:T(8,128)}, u32[]{:S(2)}) copy-start(f32[27,21]{0,1:T(8,128)} %param.14) | copy-start | bytes 6808
  33.7 25.6 %copy-start.7 = (f32[1,27]{1,0:T(1,128)S(1)}, f32[1,27]{1,0:T(1,128)}, u32[]{:S(2)}) copy-start(f32[1,27]{1,0:T(1,128)} %coeff_ref) | copy-start | bytes 328
  53.3 27.4 %all-to-all-start = ((bf16[32,8,16,128]{3,2,1,0:T(8,128)(2,1)}), bf16[32,8,16,128]{3,2,1,0:T(8,128)(2,1)S(1)}, u32[]{:S(2)}, u32[]{:S(2)}) async-start(bf16[32,8,16,128]{3,2,1,0:T(8,128)(2,1)} %bitcast.35), calls=%async_computation | async-start | bytes 2097152 | tf_op jit(solution)/shard_map/all_to_all | solution.py:489
  59.3 21.4 %copy-start.4 = (s32[32,1]{0,1:T(1,128)S(1)}, s32[32,1]{0,1:T(1,128)}, u32[]{:S(2)}) copy-start(s32[32,1]{0,1:T(1,128)} %param.21) | copy-start | bytes 388
  60.3 1.1 copy-start
  61.5 55.5 %copy-start.2 = (bf16[1,256,2048]{2,1,0:T(8,128)(2,1)S(1)}, bf16[1,256,2048]{2,1,0:T(8,128)(2,1)}, u32[]{:S(2)}) copy-start(bf16[1,256,2048]{2,1,0:T(8,128)(2,1)} %param.19) | copy-start | bytes 3145732
  80.7 36.2 %copy-start.1 = (bf16[3072,256]{1,0:T(8,128)(2,1)S(1)}, bf16[3072,256]{1,0:T(8,128)(2,1)}, u32[]{:S(2)}) copy-start(bf16[3072,256]{1,0:T(8,128)(2,1)} %copy-done) | copy-start | bytes 4718596
  112.6 9.3 %collective-permute-start.2 = (bf16[16,16,128]{2,1,0:T(8,128)(2,1)S(1)}, bf16[16,16,128]{2,1,0:T(8,128)(2,1)S(1)}, u32[]{:S(2)}, u32[]{:S(2)}) collective-permute-start(bf16[16,16,128]{2,1,0:T(8,128)(2,1)S(1)} %bitcast.37), channel_id=1, source_target_pairs={{0,1},{1,2},{2,3},{3,4},{4,5},{5,6},{6,7},{8,9},{9,10},{10,11},{11... | collective-permute-start | bytes 196616 | tf_op jit(solution)/shard_map/ppermute | solution.py:37
  113.9 8.0 %collective-permute-start.3 = (bf16[16,16,128]{2,1,0:T(8,128)(2,1)S(1)}, bf16[16,16,128]{2,1,0:T(8,128)(2,1)S(1)}, u32[]{:S(2)}, u32[]{:S(2)}) collective-permute-start(bf16[16,16,128]{2,1,0:T(8,128)(2,1)S(1)} %bitcast.36), channel_id=1, source_target_pairs={{1,0},{2,1},{3,2},{4,3},{5,4},{6,5},{7,6},{9,8},{10,9},{11,10},{12... | collective-permute-start | bytes 196616 | tf_op jit(solution)/shard_map/ppermute | solution.py:38

commit v8 on v6

--- a/solution.py
+++ b/solution.py
@@ -475,7 +475,7 @@
         sums[p] = sums[p] + received_ref[v].astype(jnp.float32)
         return carry
 
-    lax.fori_loop(0, received_ref.shape[0], add, 0)
+    lax.fori_loop(0, received_ref.shape[0], add, 0, unroll=4)
 
 
 def sum_cover(received, patch_of):
@@ -509,7 +509,7 @@
         send_ref[n] = packed[wanted_ref[n]]
         return carry
 
-    lax.fori_loop(0, send_ref.shape[0], place, 0)
+    lax.fori_loop(0, send_ref.shape[0], place, 0, unroll=4)
 
 
 def combine(received, cover_sums, patch_of, new_patch):
@@ -553,6 +553,7 @@
     new_coeff,
     new_patch,
 ):
+    low, high = neighbours(visit_image[0], "tile")
     cover = cover_rows(col_offset, visit_weight, good_mask[0])
     basis = (basis_rows.T, basis_cols.T, visit_coeff)
     operands = (visit_image[0], cover, *basis)
@@ -560,7 +561,6 @@
     cover, weighted = lax.optimization_barrier((cover, weighted))
     received_cover = exchange(cover)
     weighted = match_visit(1, col_offset, visit_weight, operands, weighted)
-    low, high, weighted = neighbours(visit_image[0], "tile", weighted)
     weighted = match_edges(
         low, visit_image[0], high, cover, basis, col_offset, visit_weight, weighted
     )

time: 131 us -> 125 us (0.954)
  waiting for transfers between devices: 32.3 us -> 24.7 us
  starting transfers between devices: 33.3 us -> 36.9 us
    all_to_all x2, waiting for transfers between devices: 28.6 us -> 23.6 us  [exchange(): lax.all_to_all(chunks, 'visit', split_axis=0, concat_axis=0, tiled=True)]
    ppermute x2, starting transfers between devices: 12.1 us -> 15.7 us  [neighbours(): low = lax.ppermute(bottom, axis, forward)]
    ppermute x2, waiting for transfers between devices: 3.68 us -> 0.05 us  [neighbours(): high = lax.ppermute(top, axis, backward)]
where the time goes in v8:
time: 125 us
  starting transfers between devices  36.9 us (30%)
  blocking collectives  29.2 us (23%)
  Pallas kernels  28.8 us (23%)
  waiting for transfers between devices  24.7 us (20%)
  local copies, waits for them, and re-layouts  2.7 us (2%)
  between operations  2.33 us (2%)
    all_to_all x1, blocking collectives, exchange(): lax.all_to_all(chunks, 'visit', split_axis=0, concat_axis=0, tiled=True)  29.2 us
    all_to_all x2, waiting for transfers between devices, exchange(): lax.all_to_all(chunks, 'visit', split_axis=0, concat_axis=0, tiled=True)  23.6 us
    all_to_all x2, starting transfers between devices, exchange(): lax.all_to_all(chunks, 'visit', split_axis=0, concat_axis=0, tiled=True)  17.2 us
    ppermute x2, starting transfers between devices, neighbours(): low = lax.ppermute(bottom, axis, forward)  15.7 us
    pallas_call x2, Pallas kernels, match_visit(): pl.pallas_call(functools.partial(match_kernel, turn), out_shape=jax.Shape...  9.86 us
    pallas_call x1, Pallas kernels, subtract_interior(): pl.pallas_call(interior_kernel, out_shape=jax.ShapeDtypeStruct(new.shape,...  4.89 us
    pallas_call x1, Pallas kernels, match_edges(): pl.pallas_call(match_edge_kernel, out_shape=jax.ShapeDtypeStruct(weighted...  4.66 us
    pallas_call x1, Pallas kernels, cover_rows(): pl.pallas_call(cover_kernel, out_shape=jax.ShapeDtypeStruct((height, bloc...  4.24 us
  transfers between devices with their start and end apart: 6, of which 3 were waited for; matrix products, arithmetic and copies ran while one was open for 1% of the time, Pallas kernels for 9%

profile of v8, /device:TPU:1, one launch (start us, length us, event | category | flops | bytes accessed | tf_op | source)
XLA Modules:
  0.0 124.6 jit_solution(6026575704776760835)
XLA Ops:
  1.9 4.2 %cover_rows.1.refs_3_.cover = bf16[256,16,128]{2,1,0:T(8,128)(2,1)} custom-call(s32[1]{0:T(128)S(6)} %copy.21.offset_ref.refs_0_, f32[1]{0:T(128)S(6)} %copy.20.weight_ref.refs_1_, s32[256,2048]{1,0:T(8,128)} %bitcast.36), custom_call_target="tpu_custom_call" | custom-call | flops 1000000 | bytes 6000000 | tf_op jit(solution)/shard_map/cover_rows/pallas_call | solution.py:257
  6.2 9.6 %match_visit.2.refs_7_ = bf16[256,16,128]{2,1,0:T(8,128)(2,1)} custom-call(s32[1]{0:T(128)S(6)} %copy.21.offset_ref.refs_0_, f32[1]{0:T(128)S(6)} %copy.20.weight_ref.refs_1_, bf16[256,2048]{1,0:T(8,128)(2,1)} %bitcast.38, bf16[256,16,128]{2,1,0:T(8,128)(2,1)} %cover_rows.1.refs_3_.cover, f32[21,27]{1,0:T(8,128)} %bitcast.24, f32[21,27]{1,0:T(8,128)} %bitcast.28, ...), custom_call_target="tpu_custom_call" | custom-call | flops 3221225472 | bytes 8000000 | tf_op jit(solution)/shard_map/match_visit/pallas_call | solution.py:289
  15.8 12.0 %all-to-all-start.1 = ((bf16[32,8,16,128]{3,2,1,0:T(8,128)(2,1)}), bf16[32,8,16,128]{3,2,1,0:T(8,128)(2,1)S(1)}, u32[]{:S(2)}, u32[]{:S(2)}) async-start(bf16[32,8,16,128]{3,2,1,0:T(8,128)(2,1)} %bitcast.9), calls=%async_computation.1 | async-start | bytes 2097152 | tf_op jit(solution)/shard_map/all_to_all | solution.py:540
  27.9 0.9 slice_bitcast_fusion
  28.7 1.9 %collective-permute-start.1 = (bf16[16,2048]{1,0:T(8,128)(2,1)S(1)}, bf16[16,2048]{1,0:T(8,128)(2,1)S(1)}, u32[]{:S(2)}, u32[]{:S(2)}) collective-permute-start(bf16[16,2048]{1,0:T(8,128)(2,1)S(1)} %get-tuple-element.22), channel_id=1, source_target_pairs={{1,0},{2,1},{3,2},{4,3},{5,4},{6,5},{7,6},{9,8},{10,9},{11,10},{12... | collective-permute-start | bytes 196616 | tf_op jit(solution)/shard_map/ppermute | solution.py:41
  30.7 3.6 %collective-permute-start = (bf16[16,2048]{1,0:T(8,128)(2,1)S(1)}, bf16[16,2048]{1,0:T(8,128)(2,1)S(1)}, u32[]{:S(2)}, u32[]{:S(2)}) collective-permute-start(bf16[16,2048]{1,0:T(8,128)(2,1)S(1)} %get-tuple-element.23), channel_id=1, source_target_pairs={{0,1},{1,2},{2,3},{3,4},{4,5},{5,6},{6,7},{8,9},{9,10},{10,11},{11... | collective-permute-start | bytes 196616 | tf_op jit(solution)/shard_map/ppermute | solution.py:40
  34.3 0.2 match_visit.3._
  34.6 0.0 collective-permute-done.1.high
  34.6 0.0 copy-start.8
  34.6 1.0 collective-permute-done.low
  35.6 0.0 copy-done.8
  35.6 0.0 copy-start.9
  35.6 0.6 copy-done.9
  36.3 4.7 %match_edges.1 = bf16[256,16,128]{2,1,0:T(8,128)(2,1)} custom-call(s32[1]{0:T(128)S(6)} %copy.21.offset_ref.refs_0_, f32[1]{0:T(128)S(6)} %copy.20.weight_ref.refs_1_, bf16[16,2048]{1,0:T(8,128)(2,1)} %copy-done.9, bf16[256,2048]{1,0:T(8,128)(2,1)} %bitcast.40, bf16[16,2048]{1,0:T(8,128)(2,1)} %copy-done.8, ...), custom_call_target="tpu_custom_call", output_to_operand_aliasing={{}: (9, {})} | custom-call | flops 402653184 | bytes 8000000 | tf_op jit(solution)/shard_map/match_edges/pallas_call | solution.py:315
  40.9 0.0 copy-start.5
  40.9 0.0 copy-start.3
  41.0 0.0 copy-start.4
  41.0 0.0 copy-start.7
  41.0 7.3 %all-to-all-done.1.received_ref = bf16[32,8,16,128]{3,2,1,0:T(8,128)(2,1)S(1)} async-done(((bf16[32,8,16,128]{3,2,1,0:T(8,128)(2,1)}), bf16[32,8,16,128]{3,2,1,0:T(8,128)(2,1)S(1)}, u32[]{:S(2)}, u32[]{:S(2)}) %all-to-all-start.1) | async-done | bytes 1048608 | tf_op jit(solution)/shard_map/all_to_all | solution.py:540
  48.3 5.1 %all-to-all-start = ((bf16[32,8,16,128]{3,2,1,0:T(8,128)(2,1)}), bf16[32,8,16,128]{3,2,1,0:T(8,128)(2,1)S(1)}, u32[]{:S(2)}, u32[]{:S(2)}) async-start(bf16[32,8,16,128]{3,2,1,0:T(8,128)(2,1)} %bitcast.35), calls=%async_computation | async-start | bytes 2097152 | tf_op jit(solution)/shard_map/all_to_all | solution.py:540
  53.4 0.0 copy-done.5
  53.4 0.8 sum_cover.1.cover_ref
  54.3 0.0 copy-done.3
  54.3 0.0 copy-done.4
  54.3 0.0 copy-done.7
  54.3 0.0 copy-start.6
  54.3 1.0 table.1.table_ref
  55.3 0.0 copy-start
  55.3 1.1 copy-done
  56.4 0.0 copy-start.2
  56.4 16.3 %all-to-all-done.received_ref = bf16[32,8,16,128]{3,2,1,0:T(8,128)(2,1)S(1)} async-done(((bf16[32,8,16,128]{3,2,1,0:T(8,128)(2,1)}), bf16[32,8,16,128]{3,2,1,0:T(8,128)(2,1)S(1)}, u32[]{:S(2)}, u32[]{:S(2)}) %all-to-all-start) | async-done | bytes 1048608 | tf_op jit(solution)/shard_map/all_to_all | solution.py:540
  72.7 0.0 copy-start.1
  72.7 0.0 copy-done.6
  72.7 1.9 %combine.1 = (bf16[8,8,2048]{2,1,0:T(8,128)(2,1)}, bf16[32,8,16,128]{3,2,1,0:T(8,128)(2,1)S(1)}) custom-call(s32[32]{0:T(128)S(1)} %bitcast.33, s32[32]{0:T(128)S(1)} %bitcast.34, bf16[32,8,16,128]{3,2,1,0:T(8,128)(2,1)S(1)} %all-to-all-done.received_ref, f32[8,8,16,128]{3,2,1,0:T(8,128)S(1)} %sum_cover.1.cover_ref), custom_call_target="tpu_custom_call" | custom-call | tf_op jit(solution)/shard_map/combine/pallas_call | solution.py:519
  74.6 29.2 %all_to_all.15 = bf16[32,8,16,128]{3,2,1,0:T(8,128)(2,1)S(1)} all-to-all(bf16[32,8,16,128]{3,2,1,0:T(8,128)(2,1)S(1)} %get-tuple-element.16), channel_id=1, replica_groups=mesh['visit'=32,'tile'=8] {'visit'}, dimensions={0} | all-to-all | bytes 2097152 | tf_op jit(solution)/shard_map/all_to_all | solution.py:540
  103.8 12.0 %collective-permute-start.2 = (bf16[16,16,128]{2,1,0:T(8,128)(2,1)S(1)}, bf16[16,16,128]{2,1,0:T(8,128)(2,1)S(1)}, u32[]{:S(2)}, u32[]{:S(2)}) collective-permute-start(bf16[16,16,128]{2,1,0:T(8,128)(2,1)S(1)} %bitcast.42), channel_id=1, source_target_pairs={{0,1},{1,2},{2,3},{3,4},{4,5},{5,6},{6,7},{8,9},{9,10},{10,11},{11... | collective-permute-start | bytes 196616 | tf_op jit(solution)/shard_map/ppermute | solution.py:40
  115.8 2.1 %collective-permute-start.3 = (bf16[16,16,128]{2,1,0:T(8,128)(2,1)S(1)}, bf16[16,16,128]{2,1,0:T(8,128)(2,1)S(1)}, u32[]{:S(2)}, u32[]{:S(2)}) collective-permute-start(bf16[16,16,128]{2,1,0:T(8,128)(2,1)S(1)} %bitcast.41), channel_id=1, source_target_pairs={{1,0},{2,1},{3,2},{4,3},{5,4},{6,5},{7,6},{9,8},{10,9},{11,10},{12... | collective-permute-start | bytes 196616 | tf_op jit(solution)/shard_map/ppermute | solution.py:41
  118.0 0.0 copy-done.2
  118.0 0.0 copy-done.1
  118.0 4.9 %subtract_interior.1._ = f32[256,2048]{1,0:T(8,128)} custom-call(bf16[256,16,128]{2,1,0:T(8,128)(2,1)S(1)} %bitcast.20, bf16[256,2048]{1,0:T(8,128)(2,1)S(1)} %bitcast.22, bf16[3072,256]{1,0:T(8,128)(2,1)S(1)} %copy-done.1), custom_call_target="tpu_custom_call" | custom-call | flops 3221225472 | bytes 8000000 | tf_op jit(solution)/shard_map/subtract_interior/pallas_call | solution.py:394
  122.9 0.0 collective-permute-done.2.low_ref
  122.9 0.0 collective-permute-done.3.high_ref
  122.9 1.5 %subtract_edges.1 = f32[256,2048]{1,0:T(8,128)} custom-call(bf16[16,16,128]{2,1,0:T(8,128)(2,1)S(1)} %collective-permute-done.2.low_ref, bf16[256,16,128]{2,1,0:T(8,128)(2,1)S(1)} %bitcast.21, bf16[16,16,128]{2,1,0:T(8,128)(2,1)S(1)} %collective-permute-done.3.high_ref, bf16[256,2048]{1,0:T(8,128)(2,1)S(1)} %bitcast.23, ...), custom_call_target="tpu_custom_call", output_to_operand_aliasing={{}: (5, {})} | custom-call | flops 402653184 | bytes 8000000 | tf_op jit(solution)/shard_map/subtract_edges/pallas_call | solution.py:451
  (1 shorter events, 0.0 us)
Async XLA Ops:
  15.8 32.5 %all-to-all-start.1 = ((bf16[32,8,16,128]{3,2,1,0:T(8,128)(2,1)}), bf16[32,8,16,128]{3,2,1,0:T(8,128)(2,1)S(1)}, u32[]{:S(2)}, u32[]{:S(2)}) async-start(bf16[32,8,16,128]{3,2,1,0:T(8,128)(2,1)} %bitcast.9), calls=%async_computation.1 | async-start | bytes 2097152 | tf_op jit(solution)/shard_map/all_to_all | solution.py:540
  28.7 5.9 %collective-permute-start.1 = (bf16[16,2048]{1,0:T(8,128)(2,1)S(1)}, bf16[16,2048]{1,0:T(8,128)(2,1)S(1)}, u32[]{:S(2)}, u32[]{:S(2)}) collective-permute-start(bf16[16,2048]{1,0:T(8,128)(2,1)S(1)} %get-tuple-element.22), channel_id=1, source_target_pairs={{1,0},{2,1},{3,2},{4,3},{5,4},{6,5},{7,6},{9,8},{10,9},{11,10},{12... | collective-permute-start | bytes 196616 | tf_op jit(solution)/shard_map/ppermute | solution.py:41
  30.7 5.0 %collective-permute-start = (bf16[16,2048]{1,0:T(8,128)(2,1)S(1)}, bf16[16,2048]{1,0:T(8,128)(2,1)S(1)}, u32[]{:S(2)}, u32[]{:S(2)}) collective-permute-start(bf16[16,2048]{1,0:T(8,128)(2,1)S(1)} %get-tuple-element.23), channel_id=1, source_target_pairs={{0,1},{1,2},{2,3},{3,4},{4,5},{5,6},{6,7},{8,9},{9,10},{10,11},{11... | collective-permute-start | bytes 196616 | tf_op jit(solution)/shard_map/ppermute | solution.py:40
  34.6 1.0 copy-start.8
  35.6 0.6 copy-start.9
  40.9 12.5 %copy-start.5 = (s32[32,1]{0,1:T(1,128)S(1)}, s32[32,1]{0,1:T(1,128)}, u32[]{:S(2)}) copy-start(s32[32,1]{0,1:T(1,128)} %param.18) | copy-start | bytes 388
  40.9 13.3 %copy-start.3 = (f32[27,21]{0,1:T(8,128)S(1)}, f32[27,21]{0,1:T(8,128)}, u32[]{:S(2)}) copy-start(f32[27,21]{0,1:T(8,128)} %param.13) | copy-start | bytes 6808
  41.0 13.3 %copy-start.4 = (f32[27,21]{0,1:T(8,128)S(1)}, f32[27,21]{0,1:T(8,128)}, u32[]{:S(2)}) copy-start(f32[27,21]{0,1:T(8,128)} %param.14) | copy-start | bytes 6808
  41.0 13.3 %copy-start.7 = (f32[1,27]{1,0:T(1,128)S(1)}, f32[1,27]{1,0:T(1,128)}, u32[]{:S(2)}) copy-start(f32[1,27]{1,0:T(1,128)} %coeff_ref) | copy-start | bytes 328
  48.3 24.4 %all-to-all-start = ((bf16[32,8,16,128]{3,2,1,0:T(8,128)(2,1)}), bf16[32,8,16,128]{3,2,1,0:T(8,128)(2,1)S(1)}, u32[]{:S(2)}, u32[]{:S(2)}) async-start(bf16[32,8,16,128]{3,2,1,0:T(8,128)(2,1)} %bitcast.35), calls=%async_computation | async-start | bytes 2097152 | tf_op jit(solution)/shard_map/all_to_all | solution.py:540
  54.3 18.4 %copy-start.6 = (s32[32,1]{0,1:T(1,128)S(1)}, s32[32,1]{0,1:T(1,128)}, u32[]{:S(2)}) copy-start(s32[32,1]{0,1:T(1,128)} %param.21) | copy-start | bytes 388
  55.3 1.1 copy-start
  56.4 61.6 %copy-start.2 = (bf16[1,256,2048]{2,1,0:T(8,128)(2,1)S(1)}, bf16[1,256,2048]{2,1,0:T(8,128)(2,1)}, u32[]{:S(2)}) copy-start(bf16[1,256,2048]{2,1,0:T(8,128)(2,1)} %param.19) | copy-start | bytes 3145732
  72.7 45.3 %copy-start.1 = (bf16[3072,256]{1,0:T(8,128)(2,1)S(1)}, bf16[3072,256]{1,0:T(8,128)(2,1)}, u32[]{:S(2)}) copy-start(bf16[3072,256]{1,0:T(8,128)(2,1)} %copy-done) | copy-start | bytes 4718596
  103.8 19.1 %collective-permute-start.2 = (bf16[16,16,128]{2,1,0:T(8,128)(2,1)S(1)}, bf16[16,16,128]{2,1,0:T(8,128)(2,1)S(1)}, u32[]{:S(2)}, u32[]{:S(2)}) collective-permute-start(bf16[16,16,128]{2,1,0:T(8,128)(2,1)S(1)} %bitcast.42), channel_id=1, source_target_pairs={{0,1},{1,2},{2,3},{3,4},{4,5},{5,6},{6,7},{8,9},{9,10},{10,11},{11... | collective-permute-start | bytes 196616 | tf_op jit(solution)/shard_map/ppermute | solution.py:40
  115.8 7.1 %collective-permute-start.3 = (bf16[16,16,128]{2,1,0:T(8,128)(2,1)S(1)}, bf16[16,16,128]{2,1,0:T(8,128)(2,1)S(1)}, u32[]{:S(2)}, u32[]{:S(2)}) collective-permute-start(bf16[16,16,128]{2,1,0:T(8,128)(2,1)S(1)} %bitcast.41), channel_id=1, source_target_pairs={{1,0},{2,1},{3,2},{4,3},{5,4},{6,5},{7,6},{9,8},{10,9},{11,10},{12... | collective-permute-start | bytes 196616 | tf_op jit(solution)/shard_map/ppermute | solution.py:41
